TPU v7x, 32 devices: a whole 2x2x4 slice. The times are simulated.
32 devices in a mesh: rep: 4 (over x, core), fsdp: 8 (over z, y).
Axes of the slice: x: 2, y: 2, z: 4, core: 2. Of those that a mesh axis runs over, the one named last changes fastest.
Arguments:
- tokens: bfloat16 [512, 4096], P(('rep', 'fsdp')), may hold values from -6 to 6
- readout: bfloat16 [512, 14336], P('rep', 'fsdp'), may hold values from -0.046875 to 0.046875
- resp_mask: int32 [512], P('rep'), may hold values 0 or 1
- order: int32 [4, 8], P('rep'), may hold values from 0 to 7, each once within a row
- w_gate: bfloat16 [4, 14336, 4096], P('rep', 'fsdp'), may hold values from -0.09375 to 0.09375
- w_up: bfloat16 [4, 14336, 4096], P('rep', 'fsdp'), may hold values from -0.09375 to 0.09375
- outer_gate: bfloat16 [14336, 4096], P('fsdp', 'rep'), may hold values from -0.09375 to 0.09375
- outer_up: bfloat16 [14336, 4096], P('fsdp', 'rep'), may hold values from -0.09375 to 0.09375
- moment: float32 [14336, 4096], P('fsdp', 'rep'), may hold values from -0.09375 to 0.09375
Outputs:
- loss: float32 [4], P('rep')
- grad_gate: bfloat16 [4, 14336, 4096], P('rep', 'fsdp')
- grad_up: bfloat16 [4, 14336, 4096], P('rep', 'fsdp')
- new_outer: bfloat16 [14336, 4096], P('fsdp', 'rep')
- new_moment: float32 [14336, 4096], P('fsdp', 'rep')
Inputs may be any that keep to these rules, and one draw needn't show every extreme that they name: Each row of order holds every sequence number of its group once.
All inputs are finite; a program needn't handle non-finite values. Where the computation divides by a largest or mean magnitude, that divisor is 1e-20 or more. No bound on the sum of `resp_mask` on one device may be relied on, other than what follows from the above.
Results may differ from a plain program's by a relative error of at most 0.022.
Values may be sent and summed in bfloat16 or wider, within the bound.
No kernel may reach another device: no remote copies, remote signals or barrier semaphores. Data moves between devices by JAX's collectives and lax.ppermute only.
A program may use at most 256 MiB of HBM per device.

v0:
```python
import jax
import jax.numpy as jnp
from jax import lax
from jax.sharding import PartitionSpec as P

BLOCK = 128
LEN = 16


dpo_beta = 0.1
outer_rate = 0.7
outer_mu = 0.9
tiny_eps = 1e-06


def project(rows, weight):
    return lax.dot_general(
        rows, weight, (((1,), (1,)), ((), ())), preferred_element_type=jnp.float32
    )


def local_scores(hidden, readout, mask_f, seqs):
    per_token = jnp.sum(hidden.astype(jnp.float32) * readout.astype(jnp.float32), axis=1)
    return jnp.sum((per_token * mask_f).reshape(seqs, LEN), axis=1)


def per_device(tokens, readout, resp_mask, order, w_gate, w_up, outer_gate, outer_up, moment):
    full_gate, full_up = (
        lax.all_gather(outer_gate, "rep", axis=1, tiled=True),
        lax.all_gather(outer_up, "rep", axis=1, tiled=True),
    )
    policy_gate = w_gate[0]
    policy_up = w_up[0]
    inputs = lax.all_gather(tokens, "fsdp", axis=0, tiled=True)
    gate = project(inputs, policy_gate)
    upper = project(inputs, policy_up)
    gate_ref = project(inputs, full_gate)
    upper_ref = project(inputs, full_up)
    group_tok = inputs.shape[0]
    seqs = group_tok // LEN
    mask_f = resp_mask.astype(jnp.float32)
    hidden = (jax.nn.silu(gate) * upper).astype(jnp.bfloat16)
    hidden_ref = (jax.nn.silu(gate_ref) * upper_ref).astype(jnp.bfloat16)
    score, score_ref = lax.psum(
        (
            local_scores(hidden, readout, mask_f, seqs),
            local_scores(hidden_ref, readout, mask_f, seqs),
        ),
        "fsdp",
    )
    places = jnp.arange(seqs, dtype=jnp.int32)
    pick_chosen = (order[0, 0::2][:, None] == places[None, :]).astype(jnp.float32)
    pick_rejected = (order[0, 1::2][:, None] == places[None, :]).astype(jnp.float32)
    relative = score - score_ref
    highest = lax.Precision.HIGHEST
    margin = dpo_beta * (
        jnp.dot(pick_chosen, relative, precision=highest)
        - jnp.dot(pick_rejected, relative, precision=highest)
    )
    loss = jnp.mean(jax.nn.softplus(-margin)).reshape(1)
    weight = dpo_beta * jax.nn.sigmoid(-margin) / pick_chosen.shape[0]
    coef = jnp.dot(weight, pick_rejected - pick_chosen, precision=highest)
    token_grad = jnp.broadcast_to(coef[:, None], (seqs, LEN)).reshape(-1) * mask_f
    hidden_grad = token_grad[:, None] * readout.astype(jnp.float32)
    sigma = jax.nn.sigmoid(gate)
    gate_grad = (hidden_grad * upper * sigma * (1.0 + gate * (1.0 - sigma))).astype(jnp.bfloat16)
    up_grad = (hidden_grad * jax.nn.silu(gate)).astype(jnp.bfloat16)
    contract = (((0,), (0,)), ((), ()))
    grad_gate = lax.dot_general(
        gate_grad, inputs, contract, preferred_element_type=jnp.float32
    ).astype(jnp.bfloat16)
    grad_up = lax.dot_general(up_grad, inputs, contract, preferred_element_type=jnp.float32).astype(
        jnp.bfloat16
    )
    unit_rows = full_gate.shape[0]
    delta = full_gate.astype(jnp.float32) - policy_gate.astype(jnp.float32)
    blocks = delta.reshape(unit_rows, -1, BLOCK)
    scale = (jnp.max(jnp.abs(blocks), axis=2, keepdims=True) + tiny_eps).astype(jnp.bfloat16)
    levels = (blocks / scale.astype(jnp.float32)).astype(jnp.bfloat16)
    groups = lax.axis_size("rep")
    terms = (levels.astype(jnp.float32) * scale.astype(jnp.float32)).reshape(unit_rows, -1)
    total = lax.psum_scatter(
        terms.astype(jnp.bfloat16), "rep", scatter_dimension=1, tiled=True
    ).astype(jnp.float32)
    average = total / groups
    new_moment = outer_mu * moment + average
    new_outer = (
        outer_gate.astype(jnp.float32) - outer_rate * (average + outer_mu * new_moment)
    ).astype(jnp.bfloat16)
    return (loss, grad_gate[None], grad_up[None], new_outer, new_moment)


def solution(mesh):
    return jax.shard_map(
        per_device,
        mesh=mesh,
        in_specs=(
            P(("rep", "fsdp"), None),
            P("rep", "fsdp"),
            P("rep"),
            P("rep", None),
            P("rep", "fsdp", None),
            P("rep", "fsdp", None),
            P("fsdp", "rep"),
            P("fsdp", "rep"),
            P("fsdp", "rep"),
        ),
        out_specs=(
            P("rep"),
            P("rep", "fsdp", None),
            P("rep", "fsdp", None),
            P("fsdp", "rep"),
            P("fsdp", "rep"),
        ),
        check_vma=False,
    )
```

profile of v0, /device:TPU:0, one launch (start us, length us, event | category | flops | bytes accessed | tf_op | source)
XLA Modules:
  0.0 374.9 jit_solution(752570436718770735)
XLA Ops:
  7.2 0.7 all-gather.6.cloned.1.call-update
  7.9 0.7 all-gather.4.cloned.1.call-update
  8.7 0.7 all-gather.8.cloned.1.call-update
  9.4 96.9 %all-gather.6.cloned.1.call-done = bf16[1792,4096]{1,0:T(8,128)(2,1)} async-done(((bf16[1792,1024]{1,0:T(8,128)(2,1)}), bf16[1792,4096]{1,0:T(8,128)(2,1)}) %all-gather.6.cloned.1.call-update) | async-done | bytes 14680080 | tf_op jit(solution)/shard_map/all_gather | solution.py:29
  106.3 12.6 %abs_bitcast_fusion = f32[224,8,32,128]{3,1,2,0:T(8,128)S(1)} fusion(bf16[1792,4096]{1,0:T(8,128)(2,1)} %all-gather.6.cloned.1.call-done, bf16[1,1792,4096]{2,1,0:T(8,128)(2,1)} %param.13), kind=kLoop, calls=%fused_computation.4 | loop fusion | flops 29360128 | bytes 58720256
  118.9 11.1 %copy.14 = f32[224,8,32,128]{3,2,1,0:T(8,128)} copy(f32[224,8,32,128]{3,1,2,0:T(8,128)S(1)} %abs_bitcast_fusion) | data formatting | bytes 58720256
  130.0 13.7 %reduce_max.9 = f32[1792,32]{1,0:T(8,128)S(1)} reduce(f32[1792,32,128]{2,1,0:T(8,128)} %bitcast.58, f32[]{:T(128)} %constant.26.clone.1), dimensions={2}, to_apply=%region_7.8 | reduce | flops 7282688 | bytes 29589508 | tf_op jit(solution)/shard_map/reduce_max | solution.py:78
  143.7 0.1 fusion.22
  143.8 10.2 %div.43 = f32[1792,32,128]{2,1,0:T(8,128)} broadcast(f32[1792,32]{1,0:T(8,128)S(1)} %fusion.22), dimensions={0,1} | broadcast | bytes 29589504 | tf_op jit(solution)/shard_map/div | solution.py:79
  154.0 34.4 %fusion.1 = bf16[1792,4096]{1,0:T(8,128)(2,1)} fusion(bf16[1792,4096]{1,0:T(8,128)(2,1)} %all-gather.6.cloned.1.call-done, f32[224,8,32,128]{3,2,1,0:T(8,128)} %bitcast.59, bf16[1,1792,4096]{2,1,0:T(8,128)(2,1)} %param.13), kind=kLoop, calls=%fused_computation.3 | loop fusion | flops 58720256 | bytes 73400320 | tf_op jit(solution)/shard_map/convert_element_type | solution.py:83
  188.4 0.6 copy-done.3
  189.1 0.1 slice.7
  189.2 10.7 %fusion.4 = f32[128,1792]{1,0:T(8,128)S(1)} fusion(bf16[128,4096]{1,0:T(8,128)(2,1)} %all-gather.4.cloned.1.call-done, bf16[1,1792,4096]{2,1,0:T(8,128)(2,1)} %param.13), kind=kOutput, calls=%fused_computation.10 | convolution fusion | flops 1879048192 | bytes 16646144 | tf_op jit(solution)/shard_map/dot_general | solution.py:17
  199.9 10.4 %fusion.20 = (f32[128]{0:T(128)S(1)}, f32[128,1792]{1,0:T(8,128)S(1)}) fusion(bf16[128,1792]{1,0:T(8,128)(2,1)S(1)} %copy-done.1, f32[128,1792]{1,0:T(8,128)S(1)} %fusion.4, bf16[128,4096]{1,0:T(8,128)(2,1)S(1)} %copy-done, bf16[1,1792,4096]{2,1,0:T(8,128)(2,1)} %param.14), kind=kOutput, calls=%fused_computation.35 | convolution fusion | flops 1881341824 | bytes 18022912 | tf_op jit(solution)/shard_map/dot_general | solution.py:17
  210.3 11.2 %fusion.46 = f32[128,1792]{1,0:T(8,128)} fusion(bf16[128,4096]{1,0:T(8,128)(2,1)S(1)} %copy-done, bf16[1792,4096]{1,0:T(8,128)(2,1)} %all-gather.6.cloned.1.call-done), kind=kOutput, calls=%fused_computation.69 | convolution fusion | flops 1879048192 | bytes 16646144 | tf_op jit(solution)/shard_map/dot_general | solution.py:17
  221.5 21.5 %all-gather.8.cloned.1.call-done = bf16[1792,4096]{1,0:T(8,128)(2,1)} async-done(((bf16[1792,1024]{1,0:T(8,128)(2,1)}), bf16[1792,4096]{1,0:T(8,128)(2,1)}) %all-gather.8.cloned.1.call-update) | async-done | bytes 14680080 | tf_op jit(solution)/shard_map/all_gather | solution.py:30
  243.0 10.6 %fusion.11 = f32[128]{0:T(128)S(1)} fusion(bf16[128,1792]{1,0:T(8,128)(2,1)S(1)} %copy-done.1, bf16[128,4096]{1,0:T(8,128)(2,1)S(1)} %copy-done, bf16[1792,4096]{1,0:T(8,128)(2,1)} %all-gather.8.cloned.1.call-done, f32[128,1792]{1,0:T(8,128)} %fusion.46), kind=kOutput, calls=%fused_computation.23 | convolution fusion | flops 1881341824 | bytes 17105408 | tf_op jit(solution)/shard_map/dot_general | solution.py:17
  253.6 0.1 reshape.40
  253.7 0.1 reshape.39
  253.8 0.1 reduce_sum.48
  253.9 0.1 reduce_sum.46
  254.0 0.1 slice.6
  254.1 21.4 %all-reduce = (f32[8]{0:T(128)S(1)}, f32[8]{0:T(128)S(1)}) all-reduce(f32[8]{0:T(128)S(1)} %reduce_sum.46, f32[8]{0:T(128)S(1)} %reduce_sum.48), channel_id=1, replica_groups=mesh['rep'=4,'fsdp'=8] {'fsdp'}, use_global_device_ids=true, to_apply=%region_2.3 | all-reduce | flops 16 | bytes 128 | tf_op jit(solution)/shard_map/psum | solution.py:44
  275.5 0.2 convolution_bitcast_fusion
  275.7 0.8 fusion.34
  276.5 0.2 convolution_bitcast_fusion.2
  276.7 0.1 broadcast_in_dim.6
  276.7 0.1 reshape.42
  277.5 7.7 %fusion.7 = bf16[1,1792,4096]{2,1,0:T(8,128)(2,1)} fusion(bf16[128,4096]{1,0:T(8,128)(2,1)S(1)} %copy-done, bf16[128,1792]{1,0:T(8,128)(2,1)S(1)} %copy-done.1, f32[128]{0:T(128)S(1)} %convert_multiply_fusion.3, f32[128,1792]{1,0:T(8,128)S(1)} %fusion.4), kind=kOutput, calls=%fused_computation.13 | convolution fusion | flops 1888223232 | bytes 17105408 | tf_op jit(solution)/shard_map/dot_general | solution.py:72
  285.2 7.7 %fusion.6 = bf16[1,1792,4096]{2,1,0:T(8,128)(2,1)} fusion(bf16[128,4096]{1,0:T(8,128)(2,1)S(1)} %copy-done, f32[128,1792]{1,0:T(8,128)S(1)} %get-tuple-element.12, bf16[128,1792]{1,0:T(8,128)(2,1)S(1)} %copy-done.1, f32[128,1792]{1,0:T(8,128)S(1)} %fusion.4, f32[128]{0:T(128)S(1)} %convert_multiply_fusion.3), kind=kOutput, calls=%fused_computation.12 | convolution fusion | flops 1889140736 | bytes 18022912 | tf_op jit(solution)/shard_map/dot_general | solution.py:69
  292.9 65.5 %reduce-scatter.2.cloned.1.call-done = bf16[1792,1024]{1,0:T(8,128)(2,1)} async-done(((bf16[1792,4096]{1,0:T(8,128)(2,1)}), bf16[1792,1024]{1,0:T(8,128)(2,1)}) %reduce-scatter.2.cloned.1.call-update) | async-done | bytes 3670032 | tf_op jit(solution)/shard_map/reduce_scatter | solution.py:82
  358.4 8.8 %subtract_convert_fusion = (bf16[1792,1024]{1,0:T(8,128)(2,1)}, f32[1792,1024]{1,0:T(8,128)}) fusion(bf16[1792,1024]{1,0:T(8,128)(2,1)} %reduce-scatter.2.cloned.1.call-done, bf16[1792,1024]{1,0:T(8,128)(2,1)} %param.15, f32[1792,1024]{1,0:T(8,128)} %param.17), kind=kLoop, calls=%fused_computation.14 | loop fusion | flops 18350080 | bytes 25690112 | tf_op jit(solution)/shard_map/convert_element_type | solution.py:89
  (15 shorter events, 0.2 us)
Async XLA Ops:
  7.2 99.1 %all-gather.6.cloned.1.call-start = ((), (), s32[]{:S(2)}) async-start(), calls=%async_computation.2 | async-start | bytes 18350080 | tf_op jit(solution)/shard_map/all_gather | solution.py:29
  7.9 181.3 %all-gather.4.cloned.1.call-start = ((), (), s32[]{:S(2)}) async-start(), calls=%async_computation.1 | async-start | bytes 1179648 | tf_op jit(solution)/shard_map/all_gather | solution.py:34
  8.6 234.3 %all-gather.8.cloned.1.call-start = ((), (), s32[]{:S(2)}) async-start(), calls=%async_computation.3 | async-start | bytes 18350080 | tf_op jit(solution)/shard_map/all_gather | solution.py:30
  9.4 349.0 %reduce-scatter.2.cloned.1.call-start = ((), (), s32[]{:S(2)}) async-start(), calls=%async_computation.4 | async-start | bytes 18350080 | tf_op jit(solution)/shard_map/reduce_scatter | solution.py:82
  188.4 0.7 copy-start.3
  188.4 11.5 %copy-start.1 = (bf16[128,1792]{1,0:T(8,128)(2,1)S(1)}, bf16[128,1792]{1,0:T(8,128)(2,1)}, u32[]{:S(2)}) copy-start(bf16[128,1792]{1,0:T(8,128)(2,1)} %param.10) | copy-start | bytes 1376260
  189.1 10.7 %copy-start = (bf16[128,4096]{1,0:T(8,128)(2,1)S(1)}, bf16[128,4096]{1,0:T(8,128)(2,1)}, u32[]{:S(2)}) copy-start(bf16[128,4096]{1,0:T(8,128)(2,1)} %all-gather.4.cloned.1.call-done) | copy-start | bytes 3145732
  210.3 43.3 %copy-start.2 = (s32[128]{0:T(128)S(1)}, s32[128]{0:T(128)}, u32[]{:S(2)}) copy-start(s32[128]{0:T(128)} %param.11) | copy-start | bytes 1540
Sparse Core Ops, SparseCore 0:
  9.6 96.6 all-gather.5
  108.4 40.1 all-gather.3
  150.2 92.7 all-gather.7
  245.4 112.9 reduce-scatter.1
where the time goes:
time: 375 us
  waiting for transfers between devices  186 us (50%)
  other arithmetic  69.8 us (19%)
  matrix products  59.5 us (16%)
  local copies, waits for them, and re-layouts  22.5 us (6%)
  blocking collectives  21.4 us (6%)
  between operations  15.7 us (4%)
    all_gather x1, waiting for transfers between devices, per_device(): lax.all_gather(outer_gate, 'rep', axis=1, tiled=True)  96.9 us
    reduce_scatter x1, waiting for transfers between devices, per_device(): lax.psum_scatter(terms.astype(jnp.bfloat16), 'rep', scatter_dimension=1,...  65.5 us
    dot_general x4, matrix products, project(): lax.dot_general(rows, weight, (((1,), (1,)), ((), ())), preferred_element...  42.9 us
    convert_element_type x1, other arithmetic, per_device(): terms.astype(jnp.bfloat16)  34.4 us
    all_gather x1, waiting for transfers between devices, per_device(): lax.all_gather(outer_up, 'rep', axis=1, tiled=True)  21.5 us
    psum x1, blocking collectives, per_device(): lax.psum((local_scores(hidden, readout, mask_f, seqs), local_scores(hidde...  21.4 us
    reduce_max x1, other arithmetic, per_device(): jnp.max(jnp.abs(blocks), axis=2, keepdims=True) + tiny_eps  13.7 us
    unnamed x1, other arithmetic  12.6 us
  transfers between devices with their start and end apart: 4, of which 3 were waited for; matrix products, arithmetic and copies ran while one was open for 38% of the time, Pallas kernels for 0%

commit v1 on v0

--- a/solution.py
+++ b/solution.py
@@ -1,11 +1,15 @@
+import functools
+
 import jax
 import jax.numpy as jnp
 from jax import lax
+from jax.experimental import pallas as pl
+from jax.experimental.pallas import tpu as pltpu
 from jax.sharding import PartitionSpec as P
 
 BLOCK = 128
 LEN = 16
-
+CHUNKS = 7
 
 dpo_beta = 0.1
 outer_rate = 0.7
@@ -24,19 +28,128 @@
     return jnp.sum((per_token * mask_f).reshape(seqs, LEN), axis=1)
 
 
+def outer_kernel(groups, strip, me_ref, outer_ref, moment_ref, own_ref, *refs):
+    del me_ref
+    others = refs[: groups - 1]
+    new_outer_ref, new_moment_ref = refs[-2:]
+    rows, width = outer_ref.shape
+
+    def step(index, carry):
+        at = pl.ds(pl.multiple_of(index * strip, strip), strip)
+        for block in range(width // BLOCK):
+            cols = pl.ds(block * BLOCK, BLOCK)
+            outer = outer_ref[at, cols].astype(jnp.float32)
+            total = jnp.zeros_like(outer)
+            for ref in (own_ref, *others):
+                delta = outer - ref[at, cols].astype(jnp.float32)
+                top = jnp.max(jnp.abs(delta), axis=1, keepdims=True)
+                scale = (top + tiny_eps).astype(jnp.bfloat16).astype(jnp.float32)
+                levels = (delta * (1.0 / scale)).astype(jnp.bfloat16)
+                total = total + levels.astype(jnp.float32) * scale
+            average = total * (1.0 / groups)
+            new_moment = outer_mu * moment_ref[at, cols] + average
+            new_moment_ref[at, cols] = new_moment
+            new_outer_ref[at, cols] = (
+                outer - outer_rate * (average + outer_mu * new_moment)
+            ).astype(new_outer_ref.dtype)
+        return carry
+
+    lax.fori_loop(0, rows // strip, step, 0)
+
+
+def outer_update(chunk, chunks, me, outer, moment, own, others, previous):
+    unit_rows, width = outer.shape
+    rows = unit_rows // chunks
+    tile = rows
+    while tile > 128 and tile % 32 == 0:
+        tile //= 2
+    strip = 32 if tile % 32 == 0 else 16
+    first = chunk * (rows // tile)
+    groups = len(others) + 1
+    placed = pl.BlockSpec((tile, width), lambda i, me: (first + i, 0))
+    local = pl.BlockSpec((tile, width), lambda i, me: (i, 0))
+    in_specs = [
+        placed,
+        placed,
+        pl.BlockSpec((tile, width), lambda i, me: (first + i, me[0])),
+    ] + [local] * len(others)
+    args = [me, outer, moment, own, *others]
+    aliases = {}
+    if previous is not None:
+        aliases = {len(args): 0, len(args) + 1: 1}
+        in_specs += [pl.BlockSpec(memory_space=pl.ANY)] * 2
+        args += list(previous)
+    return pl.pallas_call(
+        functools.partial(outer_kernel, groups, strip),
+        grid_spec=pltpu.PrefetchScalarGridSpec(
+            num_scalar_prefetch=1,
+            grid=(rows // tile,),
+            in_specs=in_specs,
+            out_specs=[placed, placed],
+        ),
+        out_shape=[
+            jax.ShapeDtypeStruct(outer.shape, outer.dtype),
+            jax.ShapeDtypeStruct(moment.shape, moment.dtype),
+        ],
+        input_output_aliases=aliases,
+        cost_estimate=pl.CostEstimate(
+            flops=rows * width * groups * 12,
+            bytes_accessed=rows * width * (2 * groups + 12),
+            transcendentals=0,
+        ),
+        name="outer_update",
+    )(*args)
+
+
 def per_device(tokens, readout, resp_mask, order, w_gate, w_up, outer_gate, outer_up, moment):
-    full_gate, full_up = (
-        lax.all_gather(outer_gate, "rep", axis=1, tiled=True),
-        lax.all_gather(outer_up, "rep", axis=1, tiled=True),
-    )
+    groups = lax.axis_size("rep")
+    me = lax.axis_index("rep")
+    unit_rows, width = outer_gate.shape
+    depth = tokens.shape[1]
     policy_gate = w_gate[0]
     policy_up = w_up[0]
-    inputs = lax.all_gather(tokens, "fsdp", axis=0, tiled=True)
+
+    def swap(value, bits):
+        return lax.ppermute(value, "rep", [(i, i ^ bits) for i in range(groups)])
+
+    def columns_of(value, bits):
+        return lax.dynamic_slice_in_dim(value, (me ^ bits) * width, width, 1)
+
+    shares = [columns_of(tokens, 0)] + [
+        swap(columns_of(tokens, bits), bits) for bits in range(1, groups)
+    ]
+    gathered = lax.all_gather(
+        jnp.concatenate([tokens, *shares], axis=1), "fsdp", axis=0, tiled=True
+    )
+    inputs = gathered[:, :depth]
+    group_tok = inputs.shape[0]
+
+    rows = unit_rows // CHUNKS
+    arrived = []
+    for chunk in range(CHUNKS):
+        part = policy_gate[chunk * rows : (chunk + 1) * rows]
+        arrived.append([swap(columns_of(part, bits), bits) for bits in range(1, groups)])
+
+    def reference_product(outer):
+        held = [
+            project(gathered[:, depth + k * width : depth + (k + 1) * width], outer)
+            for k in range(groups)
+        ]
+        held = dict(enumerate(held))
+        bit = 1
+        while bit < groups:
+            held = {
+                k: held[k] + swap(held[k | bit].astype(jnp.bfloat16), bit).astype(jnp.float32)
+                for k in held
+                if not k & bit
+            }
+            bit *= 2
+        return held[0]
+
+    gate_ref = reference_product(outer_gate)
+    upper_ref = reference_product(outer_up)
     gate = project(inputs, policy_gate)
     upper = project(inputs, policy_up)
-    gate_ref = project(inputs, full_gate)
-    upper_ref = project(inputs, full_up)
-    group_tok = inputs.shape[0]
     seqs = group_tok // LEN
     mask_f = resp_mask.astype(jnp.float32)
     hidden = (jax.nn.silu(gate) * upper).astype(jnp.bfloat16)
@@ -72,21 +185,14 @@
     grad_up = lax.dot_general(up_grad, inputs, contract, preferred_element_type=jnp.float32).astype(
         jnp.bfloat16
     )
-    unit_rows = full_gate.shape[0]
-    delta = full_gate.astype(jnp.float32) - policy_gate.astype(jnp.float32)
-    blocks = delta.reshape(unit_rows, -1, BLOCK)
-    scale = (jnp.max(jnp.abs(blocks), axis=2, keepdims=True) + tiny_eps).astype(jnp.bfloat16)
-    levels = (blocks / scale.astype(jnp.float32)).astype(jnp.bfloat16)
-    groups = lax.axis_size("rep")
-    terms = (levels.astype(jnp.float32) * scale.astype(jnp.float32)).reshape(unit_rows, -1)
-    total = lax.psum_scatter(
-        terms.astype(jnp.bfloat16), "rep", scatter_dimension=1, tiled=True
-    ).astype(jnp.float32)
-    average = total / groups
-    new_moment = outer_mu * moment + average
-    new_outer = (
-        outer_gate.astype(jnp.float32) - outer_rate * (average + outer_mu * new_moment)
-    ).astype(jnp.bfloat16)
+
+    place = me.reshape(1).astype(jnp.int32)
+    updated = None
+    for chunk in range(CHUNKS):
+        updated = outer_update(
+            chunk, CHUNKS, place, outer_gate, moment, policy_gate, arrived[chunk], updated
+        )
+    new_outer, new_moment = updated
     return (loss, grad_gate[None], grad_up[None], new_outer, new_moment)
 
 

time: 375 us -> 278 us (0.74)
  waiting for transfers between devices: 186 us -> 110 us
  other arithmetic: 69.8 us -> 0.25 us
  Pallas kernels: 0 us -> 30.5 us
  starting transfers between devices: 0.15 us -> 22.5 us
  local copies, waits for them, and re-layouts: 22.5 us -> 12.9 us
  matrix products: 59.5 us -> 63.3 us
    all_gather x3 -> x1, waiting for transfers between devices: 118 us -> 0.01 us  [per_device(): lax.all_gather(jnp.concatenate([tokens, *shares], axis=1), 'fsdp', axis=0...]
    ppermute x0 -> x30, waiting for transfers between devices: none -> 110 us  [swap(): return lax.ppermute(value, 'rep', [(i, i ^ bits) for i in range(groups)])]
    reduce_scatter x1 -> x0, waiting for transfers between devices: 65.5 us -> none  [per_device(): lax.psum_scatter(terms.astype(jnp.bfloat16), 'rep', scatter_dimension=1,...]
    convert_element_type x3 -> x0, other arithmetic: 43.3 us -> none  [the longest x1 34.4 us: per_device(): terms.astype(jnp.bfloat16)]
    pallas_call x0 -> x7, Pallas kernels: none -> 30.5 us  [outer_update(): pl.pallas_call(functools.partial(outer_kernel, groups, strip), grid_spec=...]
    ppermute x0 -> x30, starting transfers between devices: none -> 22.5 us  [swap(): return lax.ppermute(value, 'rep', [(i, i ^ bits) for i in range(groups)])]
    reduce_max x1 -> x0, other arithmetic: 13.7 us -> none  [per_device(): jnp.max(jnp.abs(blocks), axis=2, keepdims=True) + tiny_eps]
    unnamed x1 -> x0, other arithmetic: 12.6 us -> none
  transfers between devices with their start and end apart: 4 -> 31, of which waited for: 3 -> 15; matrix products, arithmetic and copies ran while one was open for 38% -> 21% of each run, Pallas kernels for 0% -> 9%
where the time goes in v1:
time: 278 us
  waiting for transfers between devices  110 us (40%)
  matrix products  63.3 us (23%)
  Pallas kernels  30.5 us (11%)
  starting transfers between devices  22.5 us (8%)
  blocking collectives  21.7 us (8%)
  between operations  16.1 us (6%)
  local copies, waits for them, and re-layouts  12.9 us (5%)
    ppermute x30, waiting for transfers between devices, swap(): return lax.ppermute(value, 'rep', [(i, i ^ bits) for i in range(groups)])  110 us
    dot_general x10, matrix products, project(): lax.dot_general(rows, weight, (((1,), (1,)), ((), ())), preferred_element...  46.5 us
    pallas_call x7, Pallas kernels, outer_update(): pl.pallas_call(functools.partial(outer_kernel, groups, strip), grid_spec=...  30.5 us
    ppermute x30, starting transfers between devices, swap(): return lax.ppermute(value, 'rep', [(i, i ^ bits) for i in range(groups)])  22.5 us
    psum x1, blocking collectives, per_device(): lax.psum((local_scores(hidden, readout, mask_f, seqs), local_scores(hidde...  21.7 us
    dot_general x1, matrix products, per_device(): lax.dot_general(gate_grad, inputs, contract, preferred_element_type=jnp.f...  7.86 us
    dot_general x1, matrix products, per_device(): lax.dot_general(up_grad, inputs, contract, preferred_element_type=jnp.flo...  7.75 us
    slice x1, local copies, waits for them, and re-layouts, per_device(): part = policy_gate[chunk * rows:(chunk + 1) * rows]  5.73 us
  transfers between devices with their start and end apart: 31, of which 15 were waited for; matrix products, arithmetic and copies ran while one was open for 21% of the time, Pallas kernels for 9%

profile of v1, /device:TPU:0, one launch (start us, length us, event | category | flops | bytes accessed | tf_op | source)
XLA Modules:
  0.0 277.6 jit_solution(14249746944184309659)
XLA Ops:
  16.2 5.7 %fusion.58 = (bf16[1,256,4096]{2,1,0:T(8,128)(2,1)S(1)}, bf16[1,256,4096]{2,1,0:T(8,128)(2,1)S(1)}, bf16[1,256,4096]{2,1,0:T(8,128)(2,1)S(1)}, bf16[1,256,4096]{...) fusion(bf16[1,1792,4096]{2,1,0:T(8,128)(2,1)} %param.13), kind=kLoop, calls=%fused_computation.109 | loop fusion | bytes 29360128 | tf_op jit(solution)/shard_map/slice | solution.py:130
  26.4 10.7 %collective-permute-done.28.refs_1_ = bf16[256,1024]{1,0:T(8,128)(2,1)S(1)} collective-permute-done((bf16[256,1024]{1,0:T(8,128)(2,1)S(1)}, bf16[256,1024]{1,0:T(8,128)(2,1)S(1)}, u32[]{:S(2)}, u32[]{:S(2)}) %collective-permute-start.28) | collective-permute-done | bytes 524320 | tf_op jit(solution)/shard_map/ppermute | solution.py:113
  37.1 10.1 %collective-permute-done.29.refs_2_ = bf16[256,1024]{1,0:T(8,128)(2,1)S(1)} collective-permute-done((bf16[256,1024]{1,0:T(8,128)(2,1)S(1)}, bf16[256,1024]{1,0:T(8,128)(2,1)S(1)}, u32[]{:S(2)}, u32[]{:S(2)}) %collective-permute-start.29) | collective-permute-done | bytes 524320 | tf_op jit(solution)/shard_map/ppermute | solution.py:113
  50.1 9.4 %collective-permute-done.25.refs_1_ = bf16[256,1024]{1,0:T(8,128)(2,1)S(1)} collective-permute-done((bf16[256,1024]{1,0:T(8,128)(2,1)S(1)}, bf16[256,1024]{1,0:T(8,128)(2,1)S(1)}, u32[]{:S(2)}, u32[]{:S(2)}) %collective-permute-start.25) | collective-permute-done | bytes 524320 | tf_op jit(solution)/shard_map/ppermute | solution.py:113
  60.7 8.9 %collective-permute-done.26.refs_2_ = bf16[256,1024]{1,0:T(8,128)(2,1)S(1)} collective-permute-done((bf16[256,1024]{1,0:T(8,128)(2,1)S(1)}, bf16[256,1024]{1,0:T(8,128)(2,1)S(1)}, u32[]{:S(2)}, u32[]{:S(2)}) %collective-permute-start.26) | collective-permute-done | bytes 524320 | tf_op jit(solution)/shard_map/ppermute | solution.py:113
  71.9 10.1 %collective-permute-done.22.refs_1_ = bf16[256,1024]{1,0:T(8,128)(2,1)S(1)} collective-permute-done((bf16[256,1024]{1,0:T(8,128)(2,1)S(1)}, bf16[256,1024]{1,0:T(8,128)(2,1)S(1)}, u32[]{:S(2)}, u32[]{:S(2)}) %collective-permute-start.22) | collective-permute-done | bytes 524320 | tf_op jit(solution)/shard_map/ppermute | solution.py:113
  82.0 10.1 %collective-permute-done.23.refs_2_ = bf16[256,1024]{1,0:T(8,128)(2,1)S(1)} collective-permute-done((bf16[256,1024]{1,0:T(8,128)(2,1)S(1)}, bf16[256,1024]{1,0:T(8,128)(2,1)S(1)}, u32[]{:S(2)}, u32[]{:S(2)}) %collective-permute-start.23) | collective-permute-done | bytes 524320 | tf_op jit(solution)/shard_map/ppermute | solution.py:113
  95.6 8.8 %collective-permute-done.19.refs_1_ = bf16[256,1024]{1,0:T(8,128)(2,1)S(1)} collective-permute-done((bf16[256,1024]{1,0:T(8,128)(2,1)S(1)}, bf16[256,1024]{1,0:T(8,128)(2,1)S(1)}, u32[]{:S(2)}, u32[]{:S(2)}) %collective-permute-start.19) | collective-permute-done | bytes 524320 | tf_op jit(solution)/shard_map/ppermute | solution.py:113
  104.6 10.0 %collective-permute-done.20.refs_2_ = bf16[256,1024]{1,0:T(8,128)(2,1)S(1)} collective-permute-done((bf16[256,1024]{1,0:T(8,128)(2,1)S(1)}, bf16[256,1024]{1,0:T(8,128)(2,1)S(1)}, u32[]{:S(2)}, u32[]{:S(2)}) %collective-permute-start.20) | collective-permute-done | bytes 524320 | tf_op jit(solution)/shard_map/ppermute | solution.py:113
  118.3 4.3 %outer_update.7 = (bf16[1792,1024]{1,0:T(8,128)(2,1)}, f32[1792,1024]{1,0:T(8,128)}) custom-call(s32[1]{0:T(128)} %bitcast.13.me_ref, bf16[1792,1024]{1,0:T(8,128)(2,1)} %outer_ref.13, f32[1792,1024]{1,0:T(8,128)} %moment_ref.13, bf16[1792,4096]{1,0:T(8,128)(2,1)} %bitcast.86, bf16[256,1024]{1,0:T(8,128)(2,1)} %copy-done.16, bf16[256,1024]{1,0:T(8,128)(2,1)} %copy-done.17, ...), custom_call_target="tpu_custom_call" | custom-call | flops 12582912 | bytes 5242880 | tf_op jit(solution)/shard_map/outer_update/pallas_call | solution.py:82
  122.7 4.3 %outer_update.8 = (bf16[1792,1024]{1,0:T(8,128)(2,1)}, f32[1792,1024]{1,0:T(8,128)}) custom-call(s32[1]{0:T(128)} %bitcast.13.me_ref, bf16[1792,1024]{1,0:T(8,128)(2,1)} %outer_ref.13, f32[1792,1024]{1,0:T(8,128)} %moment_ref.13, bf16[1792,4096]{1,0:T(8,128)(2,1)} %bitcast.87, ...), custom_call_target="tpu_custom_call", output_to_operand_aliasing={{0}: (7, {}), {1}: (8, {})} | custom-call | flops 12582912 | bytes 5242880 | tf_op jit(solution)/shard_map/outer_update/pallas_call | solution.py:82
  127.0 4.3 %outer_update.9 = (bf16[1792,1024]{1,0:T(8,128)(2,1)}, f32[1792,1024]{1,0:T(8,128)}) custom-call(s32[1]{0:T(128)} %bitcast.13.me_ref, bf16[1792,1024]{1,0:T(8,128)(2,1)} %outer_ref.13, f32[1792,1024]{1,0:T(8,128)} %moment_ref.13, bf16[1792,4096]{1,0:T(8,128)(2,1)} %bitcast.88, ...), custom_call_target="tpu_custom_call", output_to_operand_aliasing={{0}: (7, {}), {1}: (8, {})} | custom-call | flops 12582912 | bytes 5242880 | tf_op jit(solution)/shard_map/outer_update/pallas_call | solution.py:82
  131.4 4.3 %outer_update.10 = (bf16[1792,1024]{1,0:T(8,128)(2,1)}, f32[1792,1024]{1,0:T(8,128)}) custom-call(s32[1]{0:T(128)} %bitcast.13.me_ref, bf16[1792,1024]{1,0:T(8,128)(2,1)} %outer_ref.13, f32[1792,1024]{1,0:T(8,128)} %moment_ref.13, bf16[1792,4096]{1,0:T(8,128)(2,1)} %bitcast.89, ...), custom_call_target="tpu_custom_call", output_to_operand_aliasing={{0}: (7, {}), {1}: (8, {})} | custom-call | flops 12582912 | bytes 5242880 | tf_op jit(solution)/shard_map/outer_update/pallas_call | solution.py:82
  137.1 4.3 %outer_update.11 = (bf16[1792,1024]{1,0:T(8,128)(2,1)}, f32[1792,1024]{1,0:T(8,128)}) custom-call(s32[1]{0:T(128)} %bitcast.13.me_ref, bf16[1792,1024]{1,0:T(8,128)(2,1)} %outer_ref.13, f32[1792,1024]{1,0:T(8,128)} %moment_ref.13, bf16[1792,4096]{1,0:T(8,128)(2,1)} %bitcast.90, ...), custom_call_target="tpu_custom_call", output_to_operand_aliasing={{0}: (7, {}), {1}: (8, {})} | custom-call | flops 12582912 | bytes 5242880 | tf_op jit(solution)/shard_map/outer_update/pallas_call | solution.py:82
  141.5 8.0 %collective-permute-done.13.refs_1_ = bf16[256,1024]{1,0:T(8,128)(2,1)} collective-permute-done((bf16[256,1024]{1,0:T(8,128)(2,1)}, bf16[256,1024]{1,0:T(8,128)(2,1)}, u32[]{:S(2)}, u32[]{:S(2)}) %collective-permute-start.13) | collective-permute-done | bytes 524320 | tf_op jit(solution)/shard_map/ppermute | solution.py:113
  149.5 10.1 %collective-permute-done.14.refs_2_ = bf16[256,1024]{1,0:T(8,128)(2,1)} collective-permute-done((bf16[256,1024]{1,0:T(8,128)(2,1)}, bf16[256,1024]{1,0:T(8,128)(2,1)}, u32[]{:S(2)}, u32[]{:S(2)}) %collective-permute-start.14) | collective-permute-done | bytes 524320 | tf_op jit(solution)/shard_map/ppermute | solution.py:113
  159.6 4.3 %outer_update.12 = (bf16[1792,1024]{1,0:T(8,128)(2,1)}, f32[1792,1024]{1,0:T(8,128)}) custom-call(s32[1]{0:T(128)} %bitcast.13.me_ref, bf16[1792,1024]{1,0:T(8,128)(2,1)} %outer_ref.13, f32[1792,1024]{1,0:T(8,128)} %moment_ref.13, bf16[1792,4096]{1,0:T(8,128)(2,1)} %bitcast.91, ...), custom_call_target="tpu_custom_call", output_to_operand_aliasing={{0}: (7, {}), {1}: (8, {})} | custom-call | flops 12582912 | bytes 5242880 | tf_op jit(solution)/shard_map/outer_update/pallas_call | solution.py:82
  164.0 3.6 %convolution_convert_fusion.4 = bf16[128,1792]{1,0:T(8,128)(2,1)S(1)} fusion(bf16[1792,1024]{1,0:T(8,128)(2,1)} %outer_ref.13, bf16[128,8192]{1,0:T(8,128)(2,1)} %all-gather.2.cloned.1.call-done), kind=kOutput, calls=%fused_computation.14 | convolution fusion | flops 469991424 | bytes 4390912 | tf_op jit(solution)/shard_map/dot_general | solution.py:21
  168.6 3.1 %convolution_convert_fusion.5 = bf16[128,1792]{1,0:T(8,128)(2,1)} fusion(bf16[1792,1024]{1,0:T(8,128)(2,1)S(1)} %copy-done, bf16[128,8192]{1,0:T(8,128)(2,1)} %all-gather.2.cloned.1.call-done), kind=kOutput, calls=%fused_computation.15 | convolution fusion | flops 469991424 | bytes 4390912 | tf_op jit(solution)/shard_map/dot_general | solution.py:21
  171.7 3.1 %convolution_convert_fusion.2 = bf16[128,1792]{1,0:T(8,128)(2,1)} fusion(bf16[1792,1024]{1,0:T(8,128)(2,1)S(1)} %copy-done.1, bf16[128,8192]{1,0:T(8,128)(2,1)} %all-gather.2.cloned.1.call-done), kind=kOutput, calls=%fused_computation.12 | convolution fusion | flops 469991424 | bytes 4390912 | tf_op jit(solution)/shard_map/dot_general | solution.py:21
  175.2 3.1 %convolution_convert_fusion.3 = bf16[128,1792]{1,0:T(8,128)(2,1)} fusion(bf16[1792,1024]{1,0:T(8,128)(2,1)S(1)} %copy-done.1, bf16[128,8192]{1,0:T(8,128)(2,1)} %all-gather.2.cloned.1.call-done), kind=kOutput, calls=%fused_computation.13 | convolution fusion | flops 469991424 | bytes 4390912 | tf_op jit(solution)/shard_map/dot_general | solution.py:21
  178.3 10.5 %fusion.22 = f32[128,1792]{1,0:T(8,128)S(1)} fusion(bf16[128,8192]{1,0:T(8,128)(2,1)} %all-gather.2.cloned.1.call-done, bf16[1,1792,4096]{2,1,0:T(8,128)(2,1)} %param.13), kind=kOutput, calls=%fused_computation.41 | convolution fusion | flops 1879048192 | bytes 16646144 | tf_op jit(solution)/shard_map/dot_general | solution.py:21
  188.8 3.1 %fusion.6 = bf16[128,1792]{1,0:T(8,128)(2,1)} fusion(bf16[1792,1024]{1,0:T(8,128)(2,1)S(1)} %copy-done, bf16[128,1792]{1,0:T(8,128)(2,1)S(1)} %collective-permute-done.4, bf16[128,8192]{1,0:T(8,128)(2,1)} %all-gather.2.cloned.1.call-done), kind=kOutput, calls=%fused_computation.16 | convolution fusion | flops 470450176 | bytes 4849664 | tf_op jit(solution)/shard_map/dot_general | solution.py:21
  192.6 3.0 %fusion.7 = bf16[128,1792]{1,0:T(8,128)(2,1)} fusion(bf16[1792,1024]{1,0:T(8,128)(2,1)S(1)} %copy-done.1, bf16[128,1792]{1,0:T(8,128)(2,1)S(1)} %collective-permute-done.7, bf16[128,8192]{1,0:T(8,128)(2,1)} %all-gather.2.cloned.1.call-done), kind=kOutput, calls=%fused_computation.17 | convolution fusion | flops 470450176 | bytes 4849664 | tf_op jit(solution)/shard_map/dot_general | solution.py:21
  197.0 11.7 %fusion.16 = (f32[128]{0:T(128)S(1)}, f32[128,1792]{1,0:T(8,128)}) fusion(bf16[128,1792]{1,0:T(8,128)(2,1)} %param.10, f32[128,1792]{1,0:T(8,128)S(1)} %fusion.22, bf16[1,1792,4096]{2,1,0:T(8,128)(2,1)} %param.14, bf16[128,8192]{1,0:T(8,128)(2,1)} %all-gather.2.cloned.1.call-done), kind=kOutput, calls=%fused_computation.32 | convolution fusion | flops 1881341824 | bytes 18022912 | tf_op jit(solution)/shard_map/dot_general | solution.py:21
  212.1 3.2 %collective-permute-done.8 = bf16[128,1792]{1,0:T(8,128)(2,1)} collective-permute-done((bf16[128,1792]{1,0:T(8,128)(2,1)}, bf16[128,1792]{1,0:T(8,128)(2,1)}, u32[]{:S(2)}, u32[]{:S(2)}) %collective-permute-start.8) | collective-permute-done | bytes 458784 | tf_op jit(solution)/shard_map/ppermute | solution.py:113
  215.3 2.9 %fusion.17 = f32[128]{0:T(128)S(1)} fusion(bf16[128,1792]{1,0:T(8,128)(2,1)S(1)} %copy-done.3, f32[128,1792]{1,0:T(8,128)S(1)} %fusion.4, bf16[128,1792]{1,0:T(8,128)(2,1)} %collective-permute-done.8, bf16[128,1792]{1,0:T(8,128)(2,1)} %collective-permute-done.6, bf16[1792,1024]{1,0:T(8,128)(2,1)S(1)} %copy-done.1, ...), kind=kOutput, calls=%fused_computation.33 | convolution fusion | flops 472973184 | bytes 6226432 | tf_op jit(solution)/shard_map/dot_general | solution.py:21
  218.6 7.1 %collective-permute-done.11.refs_2_ = bf16[256,1024]{1,0:T(8,128)(2,1)} collective-permute-done((bf16[256,1024]{1,0:T(8,128)(2,1)}, bf16[256,1024]{1,0:T(8,128)(2,1)}, u32[]{:S(2)}, u32[]{:S(2)}) %collective-permute-start.11) | collective-permute-done | bytes 524320 | tf_op jit(solution)/shard_map/ppermute | solution.py:113
  225.8 4.5 %outer_update.13 = (bf16[1792,1024]{1,0:T(8,128)(2,1)}, f32[1792,1024]{1,0:T(8,128)}) custom-call(s32[1]{0:T(128)} %bitcast.13.me_ref, bf16[1792,1024]{1,0:T(8,128)(2,1)} %outer_ref.13, f32[1792,1024]{1,0:T(8,128)} %moment_ref.13, bf16[1792,4096]{1,0:T(8,128)(2,1)} %bitcast.92, ...), custom_call_target="tpu_custom_call", output_to_operand_aliasing={{0}: (7, {}), {1}: (8, {})} | custom-call | flops 12582912 | bytes 5242880 | tf_op jit(solution)/shard_map/outer_update/pallas_call | solution.py:82
  230.3 21.7 %all-reduce = (f32[8]{0:T(128)S(1)}, f32[8]{0:T(128)S(1)}) all-reduce(f32[8]{0:T(128)S(1)} %reduce_sum.46, f32[8]{0:T(128)S(1)} %reduce_sum.48), channel_id=1, replica_groups=mesh['rep'=4,'fsdp'=8] {'fsdp'}, use_global_device_ids=true, to_apply=%region_2.3 | all-reduce | flops 16 | bytes 128 | tf_op jit(solution)/shard_map/psum | solution.py:157
  254.0 7.7 %fusion.3 = bf16[1,1792,4096]{2,1,0:T(8,128)(2,1)} fusion(bf16[128,8192]{1,0:T(8,128)(2,1)S(1)} %copy-done.2, bf16[128,1792]{1,0:T(8,128)(2,1)S(1)} %copy-done.4, f32[128]{0:T(128)S(1)} %convert_multiply_fusion.3, f32[128,1792]{1,0:T(8,128)S(1)} %fusion.22), kind=kOutput, calls=%fused_computation.5 | convolution fusion | flops 1888223232 | bytes 17105408 | tf_op jit(solution)/shard_map/dot_general | solution.py:185
  261.7 7.9 %fusion.2 = bf16[1,1792,4096]{2,1,0:T(8,128)(2,1)} fusion(bf16[128,8192]{1,0:T(8,128)(2,1)S(1)} %copy-done.2, f32[128,1792]{1,0:T(8,128)S(1)} %copy-done.5, bf16[128,1792]{1,0:T(8,128)(2,1)S(1)} %copy-done.4, f32[128,1792]{1,0:T(8,128)S(1)} %fusion.22, f32[128]{0:T(128)S(1)} %convert_multiply_fusion.3), kind=kOutput, calls=%fused_computation.4 | convolution fusion | flops 1889140736 | bytes 18022912 | tf_op jit(solution)/shard_map/dot_general | solution.py:182
  (119 shorter events, 37.5 us)
Async XLA Ops:
  7.2 156.8 %all-gather.2.cloned.1.call-start = ((), (), s32[]{:S(2)}) async-start(), calls=%async_computation | async-start | bytes 2359296 | tf_op jit(solution)/shard_map/all_gather | solution.py:121
  9.0 3.2 %collective-permute-start = (bf16[16,1024]{1,0:T(8,128)(2,1)S(1)}, bf16[16,1024]{1,0:T(8,128)(2,1)S(1)}, u32[]{:S(2)}, u32[]{:S(2)}) collective-permute-start(bf16[16,1024]{1,0:T(8,128)(2,1)S(1)} %get-tuple-element.65), channel_id=1, source_target_pairs={{0,8},{8,0},{16,24},{24,16},{1,9},{9,1},{17,25},{25,17},{2,10},{10... | collective-permute-start | bytes 98312 | tf_op jit(solution)/shard_map/ppermute | solution.py:113
  9.5 4.5 %collective-permute-start.1 = (bf16[16,1024]{1,0:T(8,128)(2,1)S(1)}, bf16[16,1024]{1,0:T(8,128)(2,1)S(1)}, u32[]{:S(2)}, u32[]{:S(2)}) collective-permute-start(bf16[16,1024]{1,0:T(8,128)(2,1)S(1)} %get-tuple-element.64), channel_id=1, source_target_pairs={{0,16},{8,24},{16,0},{24,8},{1,17},{9,25},{17,1},{25,9},{2,18},{10... | collective-permute-start | bytes 98312 | tf_op jit(solution)/shard_map/ppermute | solution.py:113
  12.1 3.3 %collective-permute-start.2 = (bf16[16,1024]{1,0:T(8,128)(2,1)S(1)}, bf16[16,1024]{1,0:T(8,128)(2,1)S(1)}, u32[]{:S(2)}, u32[]{:S(2)}) collective-permute-start(bf16[16,1024]{1,0:T(8,128)(2,1)S(1)} %get-tuple-element.63), channel_id=1, source_target_pairs={{0,24},{8,16},{16,8},{24,0},{1,25},{9,17},{17,9},{25,1},{2,26},{10... | collective-permute-start | bytes 98312 | tf_op jit(solution)/shard_map/ppermute | solution.py:113
  22.1 3.5 %collective-permute-start.27 = (bf16[256,1024]{1,0:T(8,128)(2,1)S(1)}, bf16[256,1024]{1,0:T(8,128)(2,1)S(1)}, u32[]{:S(2)}, u32[]{:S(2)}) collective-permute-start(bf16[256,1024]{1,0:T(8,128)(2,1)S(1)} %get-tuple-element.44), channel_id=1, source_target_pairs={{0,8},{8,0},{16,24},{24,16},{1,9},{9,1},{17,25},{25,17},{2,10},{10... | collective-permute-start | bytes 1572872 | tf_op jit(solution)/shard_map/ppermute | solution.py:113
  22.3 14.7 %collective-permute-start.28 = (bf16[256,1024]{1,0:T(8,128)(2,1)S(1)}, bf16[256,1024]{1,0:T(8,128)(2,1)S(1)}, u32[]{:S(2)}, u32[]{:S(2)}) collective-permute-start(bf16[256,1024]{1,0:T(8,128)(2,1)S(1)} %get-tuple-element.43), channel_id=1, source_target_pairs={{0,16},{8,24},{16,0},{24,8},{1,17},{9,25},{17,1},{25,9},{2,18},{10... | collective-permute-start | bytes 1572872 | tf_op jit(solution)/shard_map/ppermute | solution.py:113
  23.1 24.1 %collective-permute-start.29 = (bf16[256,1024]{1,0:T(8,128)(2,1)S(1)}, bf16[256,1024]{1,0:T(8,128)(2,1)S(1)}, u32[]{:S(2)}, u32[]{:S(2)}) collective-permute-start(bf16[256,1024]{1,0:T(8,128)(2,1)S(1)} %get-tuple-element.42), channel_id=1, source_target_pairs={{0,24},{8,16},{16,8},{24,0},{1,25},{9,17},{17,9},{25,1},{2,26},{10... | collective-permute-start | bytes 1572872 | tf_op jit(solution)/shard_map/ppermute | solution.py:113
  24.2 23.9 %collective-permute-start.24 = (bf16[256,1024]{1,0:T(8,128)(2,1)S(1)}, bf16[256,1024]{1,0:T(8,128)(2,1)S(1)}, u32[]{:S(2)}, u32[]{:S(2)}) collective-permute-start(bf16[256,1024]{1,0:T(8,128)(2,1)S(1)} %get-tuple-element.47), channel_id=1, source_target_pairs={{0,8},{8,0},{16,24},{24,16},{1,9},{9,1},{17,25},{25,17},{2,10},{10... | collective-permute-start | bytes 1572872 | tf_op jit(solution)/shard_map/ppermute | solution.py:113
  24.7 34.8 %collective-permute-start.25 = (bf16[256,1024]{1,0:T(8,128)(2,1)S(1)}, bf16[256,1024]{1,0:T(8,128)(2,1)S(1)}, u32[]{:S(2)}, u32[]{:S(2)}) collective-permute-start(bf16[256,1024]{1,0:T(8,128)(2,1)S(1)} %get-tuple-element.46), channel_id=1, source_target_pairs={{0,16},{8,24},{16,0},{24,8},{1,17},{9,25},{17,1},{25,9},{2,18},{10... | collective-permute-start | bytes 1572872 | tf_op jit(solution)/shard_map/ppermute | solution.py:113
  25.6 44.0 %collective-permute-start.26 = (bf16[256,1024]{1,0:T(8,128)(2,1)S(1)}, bf16[256,1024]{1,0:T(8,128)(2,1)S(1)}, u32[]{:S(2)}, u32[]{:S(2)}) collective-permute-start(bf16[256,1024]{1,0:T(8,128)(2,1)S(1)} %get-tuple-element.45), channel_id=1, source_target_pairs={{0,24},{8,16},{16,8},{24,0},{1,25},{9,17},{17,9},{25,1},{2,26},{10... | collective-permute-start | bytes 1572872 | tf_op jit(solution)/shard_map/ppermute | solution.py:113
  37.1 33.3 %collective-permute-start.21 = (bf16[256,1024]{1,0:T(8,128)(2,1)S(1)}, bf16[256,1024]{1,0:T(8,128)(2,1)S(1)}, u32[]{:S(2)}, u32[]{:S(2)}) collective-permute-start(bf16[256,1024]{1,0:T(8,128)(2,1)S(1)} %get-tuple-element.50), channel_id=1, source_target_pairs={{0,8},{8,0},{16,24},{24,16},{1,9},{9,1},{17,25},{25,17},{2,10},{10... | collective-permute-start | bytes 1572872 | tf_op jit(solution)/shard_map/ppermute | solution.py:113
  47.1 34.9 %collective-permute-start.22 = (bf16[256,1024]{1,0:T(8,128)(2,1)S(1)}, bf16[256,1024]{1,0:T(8,128)(2,1)S(1)}, u32[]{:S(2)}, u32[]{:S(2)}) collective-permute-start(bf16[256,1024]{1,0:T(8,128)(2,1)S(1)} %get-tuple-element.49), channel_id=1, source_target_pairs={{0,16},{8,24},{16,0},{24,8},{1,17},{9,25},{17,1},{25,9},{2,18},{10... | collective-permute-start | bytes 1572872 | tf_op jit(solution)/shard_map/ppermute | solution.py:113
  48.1 70.2 %copy-start.7 = (bf16[256,1024]{1,0:T(8,128)(2,1)}, bf16[256,1024]{1,0:T(8,128)(2,1)S(1)}, u32[]{:S(2)}) copy-start(bf16[256,1024]{1,0:T(8,128)(2,1)S(1)} %collective-permute-done.24.refs_0_) | copy-start | bytes 1572868
  48.1 44.0 %collective-permute-start.23 = (bf16[256,1024]{1,0:T(8,128)(2,1)S(1)}, bf16[256,1024]{1,0:T(8,128)(2,1)S(1)}, u32[]{:S(2)}, u32[]{:S(2)}) collective-permute-start(bf16[256,1024]{1,0:T(8,128)(2,1)S(1)} %get-tuple-element.48), channel_id=1, source_target_pairs={{0,24},{8,16},{16,8},{24,0},{1,25},{9,17},{17,9},{25,1},{2,26},{10... | collective-permute-start | bytes 1572872 | tf_op jit(solution)/shard_map/ppermute | solution.py:113
  59.5 33.3 %collective-permute-start.18 = (bf16[256,1024]{1,0:T(8,128)(2,1)S(1)}, bf16[256,1024]{1,0:T(8,128)(2,1)S(1)}, u32[]{:S(2)}, u32[]{:S(2)}) collective-permute-start(bf16[256,1024]{1,0:T(8,128)(2,1)S(1)} %get-tuple-element.53), channel_id=1, source_target_pairs={{0,8},{8,0},{16,24},{24,16},{1,9},{9,1},{17,25},{25,17},{2,10},{10... | collective-permute-start | bytes 1572872 | tf_op jit(solution)/shard_map/ppermute | solution.py:113
  69.6 34.9 %collective-permute-start.19 = (bf16[256,1024]{1,0:T(8,128)(2,1)S(1)}, bf16[256,1024]{1,0:T(8,128)(2,1)S(1)}, u32[]{:S(2)}, u32[]{:S(2)}) collective-permute-start(bf16[256,1024]{1,0:T(8,128)(2,1)S(1)} %get-tuple-element.52), channel_id=1, source_target_pairs={{0,16},{8,24},{16,0},{24,8},{1,17},{9,25},{17,1},{25,9},{2,18},{10... | collective-permute-start | bytes 1572872 | tf_op jit(solution)/shard_map/ppermute | solution.py:113
  70.4 44.2 %collective-permute-start.20 = (bf16[256,1024]{1,0:T(8,128)(2,1)S(1)}, bf16[256,1024]{1,0:T(8,128)(2,1)S(1)}, u32[]{:S(2)}, u32[]{:S(2)}) collective-permute-start(bf16[256,1024]{1,0:T(8,128)(2,1)S(1)} %get-tuple-element.51), channel_id=1, source_target_pairs={{0,24},{8,16},{16,8},{24,0},{1,25},{9,17},{17,9},{25,1},{2,26},{10... | collective-permute-start | bytes 1572872 | tf_op jit(solution)/shard_map/ppermute | solution.py:113
  82.0 33.4 %collective-permute-start.15 = (bf16[256,1024]{1,0:T(8,128)(2,1)S(1)}, bf16[256,1024]{1,0:T(8,128)(2,1)}, u32[]{:S(2)}, u32[]{:S(2)}) collective-permute-start(bf16[256,1024]{1,0:T(8,128)(2,1)S(1)} %get-tuple-element.56), channel_id=1, source_target_pairs={{0,8},{8,0},{16,24},{24,16},{1,9},{9,1},{17,25},{25,17},{2,10},{10... | collective-permute-start | bytes 1572872 | tf_op jit(solution)/shard_map/ppermute | solution.py:113
  92.1 43.6 %collective-permute-start.16 = (bf16[256,1024]{1,0:T(8,128)(2,1)}, bf16[256,1024]{1,0:T(8,128)(2,1)}, u32[]{:S(2)}, u32[]{:S(2)}) collective-permute-start(bf16[256,1024]{1,0:T(8,128)(2,1)} %get-tuple-element.55), channel_id=1, source_target_pairs={{0,16},{8,24},{16,0},{24,8},{1,17},{9,25},{17,1},{25,9},{2,18},{10... | collective-permute-start | bytes 1572872 | tf_op jit(solution)/shard_map/ppermute | solution.py:113
  92.9 44.3 %collective-permute-start.17 = (bf16[256,1024]{1,0:T(8,128)(2,1)}, bf16[256,1024]{1,0:T(8,128)(2,1)}, u32[]{:S(2)}, u32[]{:S(2)}) collective-permute-start(bf16[256,1024]{1,0:T(8,128)(2,1)} %get-tuple-element.54), channel_id=1, source_target_pairs={{0,24},{8,16},{16,8},{24,0},{1,25},{9,17},{17,9},{25,1},{2,26},{10... | collective-permute-start | bytes 1572872 | tf_op jit(solution)/shard_map/ppermute | solution.py:113
  104.5 37.0 %collective-permute-start.12 = (bf16[256,1024]{1,0:T(8,128)(2,1)}, bf16[256,1024]{1,0:T(8,128)(2,1)}, u32[]{:S(2)}, u32[]{:S(2)}) collective-permute-start(bf16[256,1024]{1,0:T(8,128)(2,1)} %get-tuple-element.59), channel_id=1, source_target_pairs={{0,8},{8,0},{16,24},{24,16},{1,9},{9,1},{17,25},{25,17},{2,10},{10... | collective-permute-start | bytes 1572872 | tf_op jit(solution)/shard_map/ppermute | solution.py:113
  114.6 35.0 %collective-permute-start.13 = (bf16[256,1024]{1,0:T(8,128)(2,1)}, bf16[256,1024]{1,0:T(8,128)(2,1)}, u32[]{:S(2)}, u32[]{:S(2)}) collective-permute-start(bf16[256,1024]{1,0:T(8,128)(2,1)} %get-tuple-element.58), channel_id=1, source_target_pairs={{0,16},{8,24},{16,0},{24,8},{1,17},{9,25},{17,1},{25,9},{2,18},{10... | collective-permute-start | bytes 1572872 | tf_op jit(solution)/shard_map/ppermute | solution.py:113
  115.4 44.2 %collective-permute-start.14 = (bf16[256,1024]{1,0:T(8,128)(2,1)}, bf16[256,1024]{1,0:T(8,128)(2,1)}, u32[]{:S(2)}, u32[]{:S(2)}) collective-permute-start(bf16[256,1024]{1,0:T(8,128)(2,1)} %get-tuple-element.57), channel_id=1, source_target_pairs={{0,24},{8,16},{16,8},{24,0},{1,25},{9,17},{17,9},{25,1},{2,26},{10... | collective-permute-start | bytes 1572872 | tf_op jit(solution)/shard_map/ppermute | solution.py:113
  135.7 82.9 %collective-permute-start.10 = (bf16[256,1024]{1,0:T(8,128)(2,1)}, bf16[256,1024]{1,0:T(8,128)(2,1)}, u32[]{:S(2)}, u32[]{:S(2)}) collective-permute-start(bf16[256,1024]{1,0:T(8,128)(2,1)} %get-tuple-element.61), channel_id=1, source_target_pairs={{0,16},{8,24},{16,0},{24,8},{1,17},{9,25},{17,1},{25,9},{2,18},{10... | collective-permute-start | bytes 1572872 | tf_op jit(solution)/shard_map/ppermute | solution.py:113
  167.6 21.2 %collective-permute-start.4 = (bf16[128,1792]{1,0:T(8,128)(2,1)S(1)}, bf16[128,1792]{1,0:T(8,128)(2,1)S(1)}, u32[]{:S(2)}, u32[]{:S(2)}) collective-permute-start(bf16[128,1792]{1,0:T(8,128)(2,1)S(1)} %convolution_convert_fusion.4), channel_id=1, source_target_pairs={{0,8},{8,0},{16,24},{24,16},{1,9},{9,1},{17,25},{25,17},{2,10},{10... | collective-permute-start | bytes 1376264 | tf_op jit(solution)/shard_map/ppermute | solution.py:113
  171.7 37.0 %collective-permute-start.3 = (bf16[128,1792]{1,0:T(8,128)(2,1)}, bf16[128,1792]{1,0:T(8,128)(2,1)}, u32[]{:S(2)}, u32[]{:S(2)}) collective-permute-start(bf16[128,1792]{1,0:T(8,128)(2,1)} %convolution_convert_fusion.5), channel_id=1, source_target_pairs={{0,8},{8,0},{16,24},{24,16},{1,9},{9,1},{17,25},{25,17},{2,10},{10... | collective-permute-start | bytes 1376264 | tf_op jit(solution)/shard_map/ppermute | solution.py:113
  174.7 17.9 %collective-permute-start.7 = (bf16[128,1792]{1,0:T(8,128)(2,1)}, bf16[128,1792]{1,0:T(8,128)(2,1)S(1)}, u32[]{:S(2)}, u32[]{:S(2)}) collective-permute-start(bf16[128,1792]{1,0:T(8,128)(2,1)} %convolution_convert_fusion.2), channel_id=1, source_target_pairs={{0,8},{8,0},{16,24},{24,16},{1,9},{9,1},{17,25},{25,17},{2,10},{10... | collective-permute-start | bytes 1376264 | tf_op jit(solution)/shard_map/ppermute | solution.py:113
  178.3 33.8 %collective-permute-start.6 = (bf16[128,1792]{1,0:T(8,128)(2,1)}, bf16[128,1792]{1,0:T(8,128)(2,1)}, u32[]{:S(2)}, u32[]{:S(2)}) collective-permute-start(bf16[128,1792]{1,0:T(8,128)(2,1)} %convolution_convert_fusion.3), channel_id=1, source_target_pairs={{0,8},{8,0},{16,24},{24,16},{1,9},{9,1},{17,25},{25,17},{2,10},{10... | collective-permute-start | bytes 1376264 | tf_op jit(solution)/shard_map/ppermute | solution.py:113
  191.9 17.0 %collective-permute-start.5 = (bf16[128,1792]{1,0:T(8,128)(2,1)}, bf16[128,1792]{1,0:T(8,128)(2,1)}, u32[]{:S(2)}, u32[]{:S(2)}) collective-permute-start(bf16[128,1792]{1,0:T(8,128)(2,1)} %fusion.6), channel_id=1, source_target_pairs={{0,16},{8,24},{16,0},{24,8},{1,17},{9,25},{17,1},{25,9},{2,18},{10... | collective-permute-start | bytes 1376264 | tf_op jit(solution)/shard_map/ppermute | solution.py:113
  195.7 19.7 %collective-permute-start.8 = (bf16[128,1792]{1,0:T(8,128)(2,1)}, bf16[128,1792]{1,0:T(8,128)(2,1)}, u32[]{:S(2)}, u32[]{:S(2)}) collective-permute-start(bf16[128,1792]{1,0:T(8,128)(2,1)} %fusion.7), channel_id=1, source_target_pairs={{0,16},{8,24},{16,0},{24,8},{1,17},{9,25},{17,1},{25,9},{2,18},{10... | collective-permute-start | bytes 1376264 | tf_op jit(solution)/shard_map/ppermute | solution.py:113
  208.6 17.1 %collective-permute-start.11 = (bf16[256,1024]{1,0:T(8,128)(2,1)}, bf16[256,1024]{1,0:T(8,128)(2,1)}, u32[]{:S(2)}, u32[]{:S(2)}) collective-permute-start(bf16[256,1024]{1,0:T(8,128)(2,1)} %get-tuple-element.60), channel_id=1, source_target_pairs={{0,24},{8,16},{16,8},{24,0},{1,25},{9,17},{17,9},{25,1},{2,26},{10... | collective-permute-start | bytes 1572872 | tf_op jit(solution)/shard_map/ppermute | solution.py:113
  208.9 16.9 %collective-permute-start.9 = (bf16[256,1024]{1,0:T(8,128)(2,1)}, bf16[256,1024]{1,0:T(8,128)(2,1)}, u32[]{:S(2)}, u32[]{:S(2)}) collective-permute-start(bf16[256,1024]{1,0:T(8,128)(2,1)} %get-tuple-element.62), channel_id=1, source_target_pairs={{0,8},{8,0},{16,24},{24,16},{1,9},{9,1},{17,25},{25,17},{2,10},{10... | collective-permute-start | bytes 1572872 | tf_op jit(solution)/shard_map/ppermute | solution.py:113
  (20 other events, 522.5 us)
Sparse Core Ops, SparseCore 0:
  16.3 49.9 all-gather.1

commit v2 on v1

v2 whole, which is shorter than its diff:
```python
import functools

import jax
import jax.numpy as jnp
from jax import lax
from jax.experimental import pallas as pl
from jax.experimental.pallas import tpu as pltpu
from jax.sharding import PartitionSpec as P

BLOCK = 128
LEN = 16
CHUNKS = 7
VMEM_LIMIT = 60 * 1024 * 1024

dpo_beta = 0.1
outer_rate = 0.7
outer_mu = 0.9
tiny_eps = 1e-06


def project(rows, weight):
    return lax.dot_general(
        rows, weight, (((1,), (1,)), ((), ())), preferred_element_type=jnp.float32
    )


def local_scores(hidden, readout, mask_f, seqs):
    per_token = jnp.sum(hidden.astype(jnp.float32) * readout.astype(jnp.float32), axis=1)
    return jnp.sum((per_token * mask_f).reshape(seqs, LEN), axis=1)


def mark(token_ref):
    token_ref[...] = jnp.zeros_like(token_ref)


TOKEN = jax.ShapeDtypeStruct((8, 128), jnp.float32)
TOKEN_SPEC = pl.BlockSpec((8, 128), lambda *_: (0, 0))
STAY = pl.BlockSpec(memory_space=pltpu.HBM)


def pick_kernel(first, width, masks, me_ref, weight_ref, *refs):
    *_, token_ref, sems = refs
    targets = refs[-2 - len(masks) : -2]
    rows = targets[0].shape[0]
    copies = []
    for index, (mask, target) in enumerate(zip(masks, targets)):
        column = pl.multiple_of((me_ref[0] ^ mask) * width, width)
        source = weight_ref.at[0, pl.ds(first, rows), pl.ds(column, width)]
        copies.append(pltpu.make_async_copy(source, target, sems.at[index]))
    for copy in copies:
        copy.start()
    mark(token_ref)
    for copy in copies:
        copy.wait()


def pick(chunk, chunks, me, weight, masks, width, *after):
    rows = weight.shape[1] // chunks
    count = len(masks)
    *parts, token = pl.pallas_call(
        functools.partial(pick_kernel, chunk * rows, width, masks),
        grid_spec=pltpu.PrefetchScalarGridSpec(
            num_scalar_prefetch=1,
            grid=(1,),
            in_specs=[STAY] * (1 + len(after)),
            out_specs=[pl.BlockSpec(memory_space=pl.ANY)] * count + [TOKEN_SPEC],
            scratch_shapes=[pltpu.SemaphoreType.DMA((count,))],
        ),
        out_shape=[jax.ShapeDtypeStruct((rows, width), weight.dtype)] * count + [TOKEN],
        cost_estimate=pl.CostEstimate(
            flops=0, bytes_accessed=rows * width * 4 * count, transcendentals=0
        ),
        compiler_params=pltpu.CompilerParams(vmem_limit_bytes=VMEM_LIMIT),
        name="pick",
    )(me, weight, *after)
    return parts, token


def assemble_kernel(groups, me_ref, tokens_ref, *refs):
    out_ref = refs[-1]
    width = out_ref.shape[2]
    for block in range(groups):
        out_ref[block] = tokens_ref[:, block * width : (block + 1) * width]
    out_ref[groups] = tokens_ref[:, pl.ds(pl.multiple_of(me_ref[0] * width, width), width)]
    for k in range(1, groups):
        out_ref[groups + k] = refs[k - 1][...]


def assemble(me, tokens, others):
    groups = len(others) + 1
    rows, depth = tokens.shape
    width = depth // groups
    whole = pl.BlockSpec((rows, width), lambda i, me: (0, 0))
    return pl.pallas_call(
        functools.partial(assemble_kernel, groups),
        grid_spec=pltpu.PrefetchScalarGridSpec(
            num_scalar_prefetch=1,
            grid=(1,),
            in_specs=[pl.BlockSpec((rows, depth), lambda i, me: (0, 0))] + [whole] * (groups - 1),
            out_specs=pl.BlockSpec((2 * groups, rows, width), lambda i, me: (0, 0, 0)),
        ),
        out_shape=jax.ShapeDtypeStruct((2 * groups, rows, width), tokens.dtype),
        compiler_params=pltpu.CompilerParams(vmem_limit_bytes=VMEM_LIMIT),
        name="assemble",
    )(me, tokens, *others)


def tile_of(rows):
    return 256 if rows % 256 == 0 else rows


def partial_kernel(shares_ref, gate_ref, up_ref, *refs):
    keep_ref, leave_ref, token_ref = refs[-3:]
    ranks, groups, rows, width = shares_ref.shape
    shares = shares_ref[...].reshape(ranks * groups * rows, width)
    mark(token_ref)
    for which, weight_ref in enumerate((gate_ref, up_ref)):
        product = project(shares, weight_ref[...])
        product = product.reshape(ranks, groups, rows, product.shape[1])
        for k in range(groups):
            part = product[:, k].reshape(ranks * rows, product.shape[3])
            if k % 2:
                leave_ref[which, k // 2] = part.astype(leave_ref.dtype)
            else:
                keep_ref[which, k // 2] = part


def partial_products(gathered, outer_gate, outer_up, *after):
    ranks, doubled, rows, width = gathered.shape
    groups = doubled // 2
    unit_rows = outer_gate.shape[0]
    tile = tile_of(unit_rows)
    group_tok = ranks * rows
    weight = pl.BlockSpec((tile, width), lambda i: (i, 0))
    result = pl.BlockSpec((2, groups // 2, group_tok, tile), lambda i: (0, 0, 0, i))
    shape = (2, groups // 2, group_tok, unit_rows)
    return pl.pallas_call(
        partial_kernel,
        grid=(unit_rows // tile,),
        in_specs=[
            pl.BlockSpec(
                (ranks, groups, rows, width),
                lambda i: (0, 1, 0, 0),
                pipeline_mode=pl.Buffered(1),
            ),
            weight,
            weight,
        ]
        + [STAY] * len(after),
        out_specs=[result, result, TOKEN_SPEC],
        out_shape=[
            jax.ShapeDtypeStruct(shape, jnp.float32),
            jax.ShapeDtypeStruct(shape, jnp.bfloat16),
            TOKEN,
        ],
        compiler_params=pltpu.CompilerParams(vmem_limit_bytes=VMEM_LIMIT),
        cost_estimate=pl.CostEstimate(
            flops=4 * groups * group_tok * width * unit_rows,
            bytes_accessed=unit_rows * (4 * width + 6 * groups * group_tok),
            transcendentals=0,
        ),
        name="partial_products",
    )(gathered, outer_gate, outer_up, *after)


def policy_kernel(blocks_ref, w_gate_ref, w_up_ref, *refs):
    gate_ref, up_ref, inputs_ref, token_ref = refs[-4:]
    ranks, groups, rows, width = blocks_ref.shape

    @pl.when(pl.program_id(0) == 0)
    def _():
        mark(token_ref)
        for block in range(groups):
            inputs_ref[:, block * width : (block + 1) * width] = blocks_ref[:, block].reshape(
                ranks * rows, width
            )

    inputs = inputs_ref[...]
    gate_ref[...] = project(inputs, w_gate_ref[0])
    up_ref[...] = project(inputs, w_up_ref[0])


def policy_products(gathered, w_gate, w_up, *after):
    ranks, doubled, rows, width = gathered.shape
    groups = doubled // 2
    unit_rows, depth = w_gate.shape[1:]
    tile = tile_of(unit_rows)
    group_tok = ranks * rows
    weight = pl.BlockSpec((1, tile, depth), lambda i: (0, i, 0))
    result = pl.BlockSpec((group_tok, tile), lambda i: (0, i))
    return pl.pallas_call(
        policy_kernel,
        grid=(unit_rows // tile,),
        in_specs=[
            pl.BlockSpec(
                (ranks, groups, rows, width),
                lambda i: (0, 0, 0, 0),
                pipeline_mode=pl.Buffered(1),
            ),
            weight,
            weight,
        ]
        + [STAY] * len(after),
        out_specs=[result, result, pl.BlockSpec((group_tok, depth), lambda i: (0, 0)), TOKEN_SPEC],
        out_shape=[
            jax.ShapeDtypeStruct((group_tok, unit_rows), jnp.float32),
            jax.ShapeDtypeStruct((group_tok, unit_rows), jnp.float32),
            jax.ShapeDtypeStruct((group_tok, depth), gathered.dtype),
            TOKEN,
        ],
        compiler_params=pltpu.CompilerParams(vmem_limit_bytes=VMEM_LIMIT),
        cost_estimate=pl.CostEstimate(
            flops=4 * group_tok * depth * unit_rows,
            bytes_accessed=unit_rows * (4 * depth + 8 * group_tok),
            transcendentals=0,
        ),
        name="policy_products",
    )(gathered, w_gate, w_up, *after)


def outer_kernel(groups, strip, me_ref, outer_ref, moment_ref, *refs):
    del me_ref
    inner = refs[:groups]
    new_outer_ref, new_moment_ref, token_ref = refs[-3:]
    rows, width = outer_ref.shape
    mark(token_ref)

    def step(index, carry):
        at = pl.ds(pl.multiple_of(index * strip, strip), strip)
        for block in range(width // BLOCK):
            cols = pl.ds(block * BLOCK, BLOCK)
            outer = outer_ref[at, cols].astype(jnp.float32)
            total = jnp.zeros_like(outer)
            for ref in inner:
                delta = outer - ref[at, cols].astype(jnp.float32)
                top = jnp.max(jnp.abs(delta), axis=1, keepdims=True)
                scale = (top + tiny_eps).astype(jnp.bfloat16).astype(jnp.float32)
                levels = (delta * (1.0 / scale)).astype(jnp.bfloat16)
                total = total + levels.astype(jnp.float32) * scale
            average = total * (1.0 / groups)
            new_moment = outer_mu * moment_ref[at, cols] + average
            new_moment_ref[at, cols] = new_moment
            new_outer_ref[at, cols] = (
                outer - outer_rate * (average + outer_mu * new_moment)
            ).astype(new_outer_ref.dtype)
        return carry

    lax.fori_loop(0, rows // strip, step, 0)


def outer_update(chunk, chunks, me, outer, moment, near, far, previous, *after):
    unit_rows, width = outer.shape
    rows = unit_rows // chunks
    tile = rows // 2 if rows % 64 == 0 else rows
    strip = 32 if tile % 32 == 0 else 16
    first = chunk * (rows // tile)
    groups = len(near) + len(far)
    placed = pl.BlockSpec((tile, width), lambda i, me: (first + i, 0))
    local = pl.BlockSpec((tile, width), lambda i, me: (i, 0))
    in_specs = [placed] * (2 + len(near)) + [local] * len(far)
    args = [me, outer, moment, *near, *far]
    aliases = {}
    if previous is not None:
        aliases = {len(args): 0, len(args) + 1: 1}
        in_specs += [STAY] * 2
        args += list(previous)
    in_specs += [STAY] * len(after)
    args += list(after)
    *updated, token = pl.pallas_call(
        functools.partial(outer_kernel, groups, strip),
        grid_spec=pltpu.PrefetchScalarGridSpec(
            num_scalar_prefetch=1,
            grid=(rows // tile,),
            in_specs=in_specs,
            out_specs=[placed, placed, TOKEN_SPEC],
        ),
        out_shape=[
            jax.ShapeDtypeStruct(outer.shape, outer.dtype),
            jax.ShapeDtypeStruct(moment.shape, moment.dtype),
            TOKEN,
        ],
        input_output_aliases=aliases,
        cost_estimate=pl.CostEstimate(
            flops=rows * width * groups * 12,
            bytes_accessed=rows * width * (2 * groups + 12),
            transcendentals=0,
        ),
        compiler_params=pltpu.CompilerParams(vmem_limit_bytes=VMEM_LIMIT),
        name="outer_update",
    )(*args)
    return updated, token


def per_device(tokens, readout, resp_mask, order, w_gate, w_up, outer_gate, outer_up, moment):
    groups = lax.axis_size("rep")
    ranks = lax.axis_size("fsdp")
    place = lax.axis_index("rep").reshape(1).astype(jnp.int32)
    width = outer_gate.shape[1]

    def swap(value, bits):
        return lax.ppermute(value, "rep", [(i, i ^ bits) for i in range(groups)])

    far_masks = tuple(range(2, groups))

    def send(chunk, *after):
        parts, token = pick(chunk, CHUNKS, place, w_gate, far_masks, width, *after)
        return [swap(part, bits) for part, bits in zip(parts, far_masks)], token

    far = [None] * CHUNKS
    updated = None

    def update(chunk, *after):
        return outer_update(
            chunk, CHUNKS, place, outer_gate, moment, near, far[chunk], updated, *after
        )

    shares, token = pick(0, 1, place, tokens[None], tuple(range(1, groups)), width)
    others = [swap(share, bits) for bits, share in enumerate(shares, 1)]
    far[0], token = send(0, token)
    far[1], token = send(1, token)
    gathered = lax.all_gather(assemble(place, tokens, others), "fsdp", axis=0, tiled=False)
    (own, mate), token = pick(0, 1, place, w_gate, (0, 1), width, token)
    near = [own, swap(mate, 1)]

    updated, token = update(0)
    far[2], token = send(2, token)
    updated, token = update(1, token)
    far[3], token = send(3, token)

    keep, leave, token = partial_products(gathered, outer_gate, outer_up, token)
    held = keep + swap(leave, 1).astype(jnp.float32)
    leaving = held[:, 1].astype(jnp.bfloat16)
    both_ref = held[:, 0] + swap(leaving, 2).astype(jnp.float32)
    gate_ref, upper_ref = both_ref[0], both_ref[1]

    gate, upper, inputs, token = policy_products(gathered, w_gate, w_up, leaving)
    updated, token = update(2, token)
    far[4], token = send(4, token)
    updated, token = update(3, token)
    far[5], token = send(5, token)

    group_tok = inputs.shape[0]
    seqs = group_tok // LEN
    mask_f = resp_mask.astype(jnp.float32)
    hidden = (jax.nn.silu(gate) * upper).astype(jnp.bfloat16)
    hidden_ref = (jax.nn.silu(gate_ref) * upper_ref).astype(jnp.bfloat16)
    relative = local_scores(hidden, readout, mask_f, seqs) - local_scores(
        hidden_ref, readout, mask_f, seqs
    )
    hop = 1
    while hop < ranks:
        relative = relative + lax.ppermute(
            relative, "fsdp", [(i, i ^ hop) for i in range(ranks)]
        )
        hop *= 2
    places = jnp.arange(seqs, dtype=jnp.int32)
    pick_chosen = (order[0, 0::2][:, None] == places[None, :]).astype(jnp.float32)
    pick_rejected = (order[0, 1::2][:, None] == places[None, :]).astype(jnp.float32)
    highest = lax.Precision.HIGHEST
    margin = dpo_beta * (
        jnp.dot(pick_chosen, relative, precision=highest)
        - jnp.dot(pick_rejected, relative, precision=highest)
    )
    loss = jnp.mean(jax.nn.softplus(-margin)).reshape(1)
    weight = dpo_beta * jax.nn.sigmoid(-margin) / pick_chosen.shape[0]
    coef = jnp.dot(weight, pick_rejected - pick_chosen, precision=highest)
    token_grad = jnp.broadcast_to(coef[:, None], (seqs, LEN)).reshape(-1) * mask_f
    hidden_grad = token_grad[:, None] * readout.astype(jnp.float32)
    sigma = jax.nn.sigmoid(gate)
    gate_grad = (hidden_grad * upper * sigma * (1.0 + gate * (1.0 - sigma))).astype(jnp.bfloat16)
    up_grad = (hidden_grad * jax.nn.silu(gate)).astype(jnp.bfloat16)
    contract = (((0,), (0,)), ((), ()))
    grad_gate = lax.dot_general(
        gate_grad, inputs, contract, preferred_element_type=jnp.float32
    ).astype(jnp.bfloat16)
    grad_up = lax.dot_general(up_grad, inputs, contract, preferred_element_type=jnp.float32).astype(
        jnp.bfloat16
    )

    updated, token = update(4, token, grad_gate)
    far[6], token = send(6, token)
    updated, token = update(5, token, grad_up)
    updated, token = update(6, token)
    new_outer, new_moment = updated
    return (loss, grad_gate[None], grad_up[None], new_outer, new_moment)


def solution(mesh):
    return jax.shard_map(
        per_device,
        mesh=mesh,
        in_specs=(
            P(("rep", "fsdp"), None),
            P("rep", "fsdp"),
            P("rep"),
            P("rep", None),
            P("rep", "fsdp", None),
            P("rep", "fsdp", None),
            P("fsdp", "rep"),
            P("fsdp", "rep"),
            P("fsdp", "rep"),
        ),
        out_specs=(
            P("rep"),
            P("rep", "fsdp", None),
            P("rep", "fsdp", None),
            P("fsdp", "rep"),
            P("fsdp", "rep"),
        ),
        check_vma=False,
    )
```

time: 278 us -> 655 us (2.36)
  Pallas kernels: 30.5 us -> 521 us
  waiting for transfers between devices: 110 us -> 63.2 us
  matrix products: 63.3 us -> 16.6 us
  blocking collectives: 21.7 us -> 0 us
    pallas_call x0 -> x12, Pallas kernels: none -> 491 us  [the longest x9 463 us: pick(): pl.pallas_call(functools.partial(pick_kernel, chunk * rows, width, masks)...]
    ppermute x30 -> x20, waiting for transfers between devices: 110 us -> 57.2 us  [swap(): return lax.ppermute(value, 'rep', [(i, i ^ bits) for i in range(groups)])]
    dot_general x10 -> x0, matrix products: 46.5 us -> none  [project(): lax.dot_general(rows, weight, (((1,), (1,)), ((), ())), preferred_element...]
    psum x1 -> x0, blocking collectives: 21.7 us -> none  [per_device(): lax.psum((local_scores(hidden, readout, mask_f, seqs), local_scores(hidde...]
    ppermute x30 -> x20, starting transfers between devices: 22.5 us -> 17.9 us  [swap(): return lax.ppermute(value, 'rep', [(i, i ^ bits) for i in range(groups)])]
  transfers between devices with their start and end apart: 31 -> 24, of which waited for: 15 -> 10; matrix products, arithmetic and copies ran while one was open for 21% -> 3% of each run, Pallas kernels for 9% -> 77%
where the time goes in v2:
time: 655 us; the launch traced here: 654 us
  Pallas kernels  521 us (80%)
  waiting for transfers between devices  63.2 us (10%)
  starting transfers between devices  23.5 us (4%)
  matrix products  16.6 us (3%)
  between operations  16.2 us (2%)
  local copies, waits for them, and re-layouts  9.95 us (2%)
    pallas_call x9, Pallas kernels, pick(): pl.pallas_call(functools.partial(pick_kernel, chunk * rows, width, masks)...  463 us
    ppermute x20, waiting for transfers between devices, swap(): return lax.ppermute(value, 'rep', [(i, i ^ bits) for i in range(groups)])  57.2 us
    pallas_call x7, Pallas kernels, outer_update(): pl.pallas_call(functools.partial(outer_kernel, groups, strip), grid_spec=...  30.3 us
    ppermute x20, starting transfers between devices, swap(): return lax.ppermute(value, 'rep', [(i, i ^ bits) for i in range(groups)])  17.9 us
    pallas_call x1, Pallas kernels, policy_products(): pl.pallas_call(policy_kernel, grid=(unit_rows // tile,), in_specs=[pl.Blo...  16.5 us
  transfers between devices with their start and end apart: 24, of which 10 were waited for; matrix products, arithmetic and copies ran while one was open for 3% of the time, Pallas kernels for 77%

profile of v2, /device:TPU:0, one launch (start us, length us, event | category | flops | bytes accessed | tf_op | source)
XLA Modules:
  0.0 654.1 jit_solution(4757577674160917370)
XLA Ops:
  7.2 4.7 pick.9
  12.4 2.6 collective-permute-start.1
  15.1 33.5 %pick.10 = (bf16[256,1024]{1,0:T(8,128)(2,1)}, bf16[256,1024]{1,0:T(8,128)(2,1)}, f32[8,128]{1,0:T(8,128)}) custom-call(s32[1]{0:T(128)} %bitcast.1.me_ref, bf16[1,1792,4096]{2,1,0:T(8,128)(2,1)} %weight_ref.15, f32[8,128]{1,0:T(8,128)} %get-tuple-element.61.refs_0_), custom_call_target="tpu_custom_call" | custom-call | bytes 2097152 | tf_op jit(solution)/shard_map/pick/pallas_call | solution.py:60
  48.6 33.5 %pick.11 = (bf16[256,1024]{1,0:T(8,128)(2,1)}, bf16[256,1024]{1,0:T(8,128)(2,1)}, f32[8,128]{1,0:T(8,128)}) custom-call(s32[1]{0:T(128)} %bitcast.1.me_ref, bf16[1,1792,4096]{2,1,0:T(8,128)(2,1)} %weight_ref.15, f32[8,128]{1,0:T(8,128)} %get-tuple-element.62.refs_0_), custom_call_target="tpu_custom_call" | custom-call | bytes 2097152 | tf_op jit(solution)/shard_map/pick/pallas_call | solution.py:60
  82.1 224.1 %pick.12 = (bf16[1792,1024]{1,0:T(8,128)(2,1)}, bf16[1792,1024]{1,0:T(8,128)(2,1)}, f32[8,128]{1,0:T(8,128)}) custom-call(s32[1]{0:T(128)} %bitcast.1.me_ref, bf16[1,1792,4096]{2,1,0:T(8,128)(2,1)} %weight_ref.15, f32[8,128]{1,0:T(8,128)} %get-tuple-element.63.refs_0_), custom_call_target="tpu_custom_call" | custom-call | bytes 14680064 | tf_op jit(solution)/shard_map/pick/pallas_call | solution.py:60
  309.3 2.0 collective-permute-start.6
  313.1 11.2 %collective-permute-done.6.refs_2_ = bf16[256,1024]{1,0:T(8,128)(2,1)S(1)} collective-permute-done((bf16[256,1024]{1,0:T(8,128)(2,1)}, bf16[256,1024]{1,0:T(8,128)(2,1)S(1)}, u32[]{:S(2)}, u32[]{:S(2)}) %collective-permute-start.6) | collective-permute-done | bytes 524320 | tf_op jit(solution)/shard_map/ppermute | solution.py:301
  324.3 10.7 %collective-permute-done.7.refs_3_ = bf16[256,1024]{1,0:T(8,128)(2,1)S(1)} collective-permute-done((bf16[256,1024]{1,0:T(8,128)(2,1)S(1)}, bf16[256,1024]{1,0:T(8,128)(2,1)S(1)}, u32[]{:S(2)}, u32[]{:S(2)}) %collective-permute-start.7) | collective-permute-done | bytes 524320 | tf_op jit(solution)/shard_map/ppermute | solution.py:301
  335.8 4.3 outer_update.7
  340.2 33.5 %pick.13 = (bf16[256,1024]{1,0:T(8,128)(2,1)}, bf16[256,1024]{1,0:T(8,128)(2,1)}, f32[8,128]{1,0:T(8,128)}) custom-call(s32[1]{0:T(128)} %bitcast.1.me_ref, bf16[1,1792,4096]{2,1,0:T(8,128)(2,1)} %weight_ref.15, f32[8,128]{1,0:T(8,128)} %get-tuple-element.72.refs_0_), custom_call_target="tpu_custom_call" | custom-call | bytes 2097152 | tf_op jit(solution)/shard_map/pick/pallas_call | solution.py:60
  374.6 4.3 outer_update.8
  378.9 33.5 %pick.14 = (bf16[256,1024]{1,0:T(8,128)(2,1)}, bf16[256,1024]{1,0:T(8,128)(2,1)}, f32[8,128]{1,0:T(8,128)}) custom-call(s32[1]{0:T(128)} %bitcast.1.me_ref, bf16[1,1792,4096]{2,1,0:T(8,128)(2,1)} %weight_ref.15, f32[8,128]{1,0:T(8,128)} %get-tuple-element.74.refs_0_), custom_call_target="tpu_custom_call" | custom-call | bytes 2097152 | tf_op jit(solution)/shard_map/pick/pallas_call | solution.py:60
  412.4 10.0 %partial_products.1 = (f32[2,2,128,1792]{3,2,1,0:T(8,128)}, bf16[2,2,128,1792]{3,2,1,0:T(8,128)(2,1)}, f32[8,128]{1,0:T(8,128)}) custom-call(bf16[8,8,16,1024]{3,2,1,0:T(8,128)(2,1)} %bitcast.52, bf16[1792,1024]{1,0:T(8,128)(2,1)} %outer_ref.13, bf16[1792,1024]{1,0:T(8,128)(2,1)} %up_ref.1, f32[8,128]{1,0:T(8,128)} %get-tuple-element.75.refs_0_), custom_call_target="tpu_custom_call" | custom-call | flops 3758096384 | bytes 12845056 | tf_op jit(solution)/shard_map/partial_products/pallas_call | solution.py:137
  424.6 3.4 collective-permute-done.8
  436.9 16.5 %policy_products.1 = (f32[128,1792]{1,0:T(8,128)}, f32[128,1792]{1,0:T(8,128)}, bf16[128,4096]{1,0:T(8,128)(2,1)}, f32[8,128]{1,0:T(8,128)}) custom-call(bf16[8,8,16,1024]{3,2,1,0:T(8,128)(2,1)} %bitcast.53, bf16[1,1792,4096]{2,1,0:T(8,128)(2,1)} %weight_ref.15, bf16[1,1792,4096]{2,1,0:T(8,128)(2,1)} %w_up_ref.1, bf16[2,128,1792]{2,1,0:T(8,128)(2,1)} %fusion.11.refs_0_), custom_call_target="tpu_custom_call" | custom-call | flops 3758096384 | bytes 31195136 | tf_op jit(solution)/shard_map/policy_products/pallas_call | solution.py:191
  453.4 12.5 %collective-permute-done.13.refs_2_ = bf16[256,1024]{1,0:T(8,128)(2,1)S(1)} collective-permute-done((bf16[256,1024]{1,0:T(8,128)(2,1)}, bf16[256,1024]{1,0:T(8,128)(2,1)S(1)}, u32[]{:S(2)}, u32[]{:S(2)}) %collective-permute-start.13) | collective-permute-done | bytes 524320 | tf_op jit(solution)/shard_map/ppermute | solution.py:301
  465.8 10.8 %collective-permute-done.14.refs_3_ = bf16[256,1024]{1,0:T(8,128)(2,1)S(1)} collective-permute-done((bf16[256,1024]{1,0:T(8,128)(2,1)}, bf16[256,1024]{1,0:T(8,128)(2,1)S(1)}, u32[]{:S(2)}, u32[]{:S(2)}) %collective-permute-start.14) | collective-permute-done | bytes 524320 | tf_op jit(solution)/shard_map/ppermute | solution.py:301
  477.5 4.3 outer_update.9
  481.8 33.5 %pick.15 = (bf16[256,1024]{1,0:T(8,128)(2,1)}, bf16[256,1024]{1,0:T(8,128)(2,1)}, f32[8,128]{1,0:T(8,128)}) custom-call(s32[1]{0:T(128)} %bitcast.1.me_ref, bf16[1,1792,4096]{2,1,0:T(8,128)(2,1)} %weight_ref.15, f32[8,128]{1,0:T(8,128)} %get-tuple-element.86.refs_0_), custom_call_target="tpu_custom_call" | custom-call | bytes 2097152 | tf_op jit(solution)/shard_map/pick/pallas_call | solution.py:60
  518.3 4.3 outer_update.10
  522.6 33.5 %pick.16 = (bf16[256,1024]{1,0:T(8,128)(2,1)}, bf16[256,1024]{1,0:T(8,128)(2,1)}, f32[8,128]{1,0:T(8,128)}) custom-call(s32[1]{0:T(128)} %bitcast.1.me_ref, bf16[1,1792,4096]{2,1,0:T(8,128)(2,1)} %weight_ref.15, f32[8,128]{1,0:T(8,128)} %get-tuple-element.96.refs_0_), custom_call_target="tpu_custom_call" | custom-call | bytes 2097152 | tf_op jit(solution)/shard_map/pick/pallas_call | solution.py:60
  557.8 2.0 fusion
  562.5 2.1 collective-permute-done.10
  566.1 2.0 collective-permute-done.11
  568.1 2.6 collective-permute-start.12
  573.9 7.7 %convolution_convert_fusion.1.refs_7_ = bf16[1792,4096]{1,0:T(8,128)(2,1)} fusion(bf16[128,4096]{1,0:T(8,128)(2,1)S(1)} %copy-done.4, f32[128,1792]{1,0:T(8,128)S(1)} %copy-done.3, bf16[128,1792]{1,0:T(8,128)(2,1)S(1)} %copy-done.2, f32[128,1792]{1,0:T(8,128)S(1)} %copy-done, f32[128]{0:T(128)S(1)} %convert_multiply_fusion.3), kind=kOutput, calls=%fused_computation.1 | convolution fusion | flops 1889140736 | bytes 18022912 | tf_op jit(solution)/shard_map/dot_general | solution.py:373
  581.6 4.3 outer_update.11
  586.0 33.5 %pick.17 = (bf16[256,1024]{1,0:T(8,128)(2,1)}, bf16[256,1024]{1,0:T(8,128)(2,1)}, f32[8,128]{1,0:T(8,128)}) custom-call(s32[1]{0:T(128)} %bitcast.1.me_ref, bf16[1,1792,4096]{2,1,0:T(8,128)(2,1)} %weight_ref.15, f32[8,128]{1,0:T(8,128)} %get-tuple-element.98.refs_0_), custom_call_target="tpu_custom_call" | custom-call | bytes 2097152 | tf_op jit(solution)/shard_map/pick/pallas_call | solution.py:60
  620.6 7.6 %convolution_convert_fusion.refs_7_ = bf16[1792,4096]{1,0:T(8,128)(2,1)} fusion(bf16[128,4096]{1,0:T(8,128)(2,1)S(1)} %copy-done.4, bf16[128,1792]{1,0:T(8,128)(2,1)S(1)} %copy-done.2, f32[128]{0:T(128)S(1)} %convert_multiply_fusion.3, f32[128,1792]{1,0:T(8,128)S(1)} %copy-done), kind=kOutput, calls=%fused_computation | convolution fusion | flops 1888223232 | bytes 17105408 | tf_op jit(solution)/shard_map/dot_general | solution.py:376
  628.9 4.3 outer_update.12
  634.6 7.2 %collective-permute-done.20.refs_3_ = bf16[256,1024]{1,0:T(8,128)(2,1)} collective-permute-done((bf16[256,1024]{1,0:T(8,128)(2,1)}, bf16[256,1024]{1,0:T(8,128)(2,1)}, u32[]{:S(2)}, u32[]{:S(2)}) %collective-permute-start.20) | collective-permute-done | bytes 524320 | tf_op jit(solution)/shard_map/ppermute | solution.py:301
  641.8 4.3 outer_update.13
  (109 shorter events, 33.8 us)
Async XLA Ops:
  7.2 405.2 %all-gather.3.cloned.1.call-start = ((), (), s32[]{:S(2)}) async-start(), calls=%async_computation | async-start | bytes 2359296 | tf_op jit(solution)/shard_map/all_gather | solution.py:321
  11.9 294.4 %collective-permute-start = (bf16[16,1024]{1,0:T(8,128)(2,1)}, bf16[16,1024]{1,0:T(8,128)(2,1)S(1)}, u32[]{:S(2)}, u32[]{:S(2)}) collective-permute-start(bf16[16,1024]{1,0:T(8,128)(2,1)} %get-tuple-element.58), channel_id=1, source_target_pairs={{0,8},{8,0},{16,24},{24,16},{1,9},{9,1},{17,25},{25,17},{2,10},{10... | collective-permute-start | bytes 98312 | tf_op jit(solution)/shard_map/ppermute | solution.py:301
  12.4 293.9 %collective-permute-start.1 = (bf16[16,1024]{1,0:T(8,128)(2,1)}, bf16[16,1024]{1,0:T(8,128)(2,1)S(1)}, u32[]{:S(2)}, u32[]{:S(2)}) collective-permute-start(bf16[16,1024]{1,0:T(8,128)(2,1)} %get-tuple-element.59), channel_id=1, source_target_pairs={{0,16},{8,24},{16,0},{24,8},{1,17},{9,25},{17,1},{25,9},{2,18},{10... | collective-permute-start | bytes 98312 | tf_op jit(solution)/shard_map/ppermute | solution.py:301
  15.0 291.4 %collective-permute-start.2 = (bf16[16,1024]{1,0:T(8,128)(2,1)}, bf16[16,1024]{1,0:T(8,128)(2,1)S(1)}, u32[]{:S(2)}, u32[]{:S(2)}) collective-permute-start(bf16[16,1024]{1,0:T(8,128)(2,1)} %get-tuple-element.60), channel_id=1, source_target_pairs={{0,24},{8,16},{16,8},{24,0},{1,25},{9,17},{17,9},{25,1},{2,26},{10... | collective-permute-start | bytes 98312 | tf_op jit(solution)/shard_map/ppermute | solution.py:301
  82.0 229.3 %copy-start.23 = (bf16[256,1024]{1,0:T(8,128)(2,1)S(1)}, bf16[256,1024]{1,0:T(8,128)(2,1)}, u32[]{:S(2)}) copy-start(bf16[256,1024]{1,0:T(8,128)(2,1)} %get-tuple-element.69) | copy-start | bytes 1572868
  82.1 229.3 %copy-start.22 = (bf16[256,1024]{1,0:T(8,128)(2,1)S(1)}, bf16[256,1024]{1,0:T(8,128)(2,1)}, u32[]{:S(2)}) copy-start(bf16[256,1024]{1,0:T(8,128)(2,1)} %get-tuple-element.66) | copy-start | bytes 1572868
  82.1 230.8 %copy-start.21 = (bf16[256,1024]{1,0:T(8,128)(2,1)S(1)}, bf16[256,1024]{1,0:T(8,128)(2,1)}, u32[]{:S(2)}) copy-start(bf16[256,1024]{1,0:T(8,128)(2,1)} %get-tuple-element.67) | copy-start | bytes 1572868
  306.2 28.9 %collective-permute-start.3 = (bf16[1792,1024]{1,0:T(8,128)(2,1)}, bf16[1792,1024]{1,0:T(8,128)(2,1)}, u32[]{:S(2)}, u32[]{:S(2)}) collective-permute-start(bf16[1792,1024]{1,0:T(8,128)(2,1)} %get-tuple-element.65), channel_id=1, source_target_pairs={{0,8},{8,0},{16,24},{24,16},{1,9},{9,1},{17,25},{25,17},{2,10},{10... | collective-permute-start | bytes 11010056 | tf_op jit(solution)/shard_map/ppermute | solution.py:301
  309.3 15.0 %collective-permute-start.6 = (bf16[256,1024]{1,0:T(8,128)(2,1)}, bf16[256,1024]{1,0:T(8,128)(2,1)S(1)}, u32[]{:S(2)}, u32[]{:S(2)}) collective-permute-start(bf16[256,1024]{1,0:T(8,128)(2,1)} %get-tuple-element.68), channel_id=1, source_target_pairs={{0,16},{8,24},{16,0},{24,8},{1,17},{9,25},{17,1},{25,9},{2,18},{10... | collective-permute-start | bytes 1572872 | tf_op jit(solution)/shard_map/ppermute | solution.py:301
  311.3 23.7 %collective-permute-start.7 = (bf16[256,1024]{1,0:T(8,128)(2,1)S(1)}, bf16[256,1024]{1,0:T(8,128)(2,1)S(1)}, u32[]{:S(2)}, u32[]{:S(2)}) collective-permute-start(bf16[256,1024]{1,0:T(8,128)(2,1)S(1)} %copy-done.23), channel_id=1, source_target_pairs={{0,24},{8,16},{16,8},{24,0},{1,25},{9,17},{17,9},{25,1},{2,26},{10... | collective-permute-start | bytes 1572872 | tf_op jit(solution)/shard_map/ppermute | solution.py:301
  311.3 62.3 %collective-permute-start.4 = (bf16[256,1024]{1,0:T(8,128)(2,1)S(1)}, bf16[256,1024]{1,0:T(8,128)(2,1)S(1)}, u32[]{:S(2)}, u32[]{:S(2)}) collective-permute-start(bf16[256,1024]{1,0:T(8,128)(2,1)S(1)} %copy-done.22), channel_id=1, source_target_pairs={{0,16},{8,24},{16,0},{24,8},{1,17},{9,25},{17,1},{25,9},{2,18},{10... | collective-permute-start | bytes 1572872 | tf_op jit(solution)/shard_map/ppermute | solution.py:301
  312.8 60.8 %collective-permute-start.5 = (bf16[256,1024]{1,0:T(8,128)(2,1)S(1)}, bf16[256,1024]{1,0:T(8,128)(2,1)S(1)}, u32[]{:S(2)}, u32[]{:S(2)}) collective-permute-start(bf16[256,1024]{1,0:T(8,128)(2,1)S(1)} %copy-done.21), channel_id=1, source_target_pairs={{0,24},{8,16},{16,8},{24,0},{1,25},{9,17},{17,9},{25,1},{2,26},{10... | collective-permute-start | bytes 1572872 | tf_op jit(solution)/shard_map/ppermute | solution.py:301
  324.3 10.7 %copy-start.13 = (bf16[256,1024]{1,0:T(8,128)(2,1)}, bf16[256,1024]{1,0:T(8,128)(2,1)S(1)}, u32[]{:S(2)}) copy-start(bf16[256,1024]{1,0:T(8,128)(2,1)S(1)} %collective-permute-done.6.refs_2_) | copy-start | bytes 1572868
  424.2 3.9 collective-permute-start.8
  428.0 7.2 %copy-start.19 = (bf16[256,1024]{1,0:T(8,128)(2,1)S(1)}, bf16[256,1024]{1,0:T(8,128)(2,1)}, u32[]{:S(2)}) copy-start(bf16[256,1024]{1,0:T(8,128)(2,1)} %get-tuple-element.90) | copy-start | bytes 1572868
  428.0 8.7 %copy-start.24 = (s32[1,8]{1,0:T(1,128)S(1)}, s32[1,8]{1,0:T(1,128)}, u32[]{:S(2)}) copy-start(s32[1,8]{1,0:T(1,128)} %param.12) | copy-start | bytes 100
  431.2 126.6 %collective-permute-start.9 = (bf16[2,128,1792]{2,1,0:T(8,128)(2,1)}, bf16[2,128,1792]{2,1,0:T(8,128)(2,1)}, u32[]{:S(2)}, u32[]{:S(2)}) collective-permute-start(bf16[2,128,1792]{2,1,0:T(8,128)(2,1)} %fusion.11.refs_0_), channel_id=1, source_target_pairs={{0,16},{8,24},{16,0},{24,8},{1,17},{9,25},{17,1},{25,9},{2,18},{10... | collective-permute-start | bytes 2752520 | tf_op jit(solution)/shard_map/ppermute | solution.py:301
  433.2 32.6 %collective-permute-start.13 = (bf16[256,1024]{1,0:T(8,128)(2,1)}, bf16[256,1024]{1,0:T(8,128)(2,1)S(1)}, u32[]{:S(2)}, u32[]{:S(2)}) collective-permute-start(bf16[256,1024]{1,0:T(8,128)(2,1)} %get-tuple-element.81), channel_id=1, source_target_pairs={{0,16},{8,24},{16,0},{24,8},{1,17},{9,25},{17,1},{25,9},{2,18},{10... | collective-permute-start | bytes 1572872 | tf_op jit(solution)/shard_map/ppermute | solution.py:301
  433.3 43.4 %collective-permute-start.14 = (bf16[256,1024]{1,0:T(8,128)(2,1)}, bf16[256,1024]{1,0:T(8,128)(2,1)S(1)}, u32[]{:S(2)}, u32[]{:S(2)}) collective-permute-start(bf16[256,1024]{1,0:T(8,128)(2,1)} %get-tuple-element.82), channel_id=1, source_target_pairs={{0,24},{8,16},{16,8},{24,0},{1,25},{9,17},{17,9},{25,1},{2,26},{10... | collective-permute-start | bytes 1572872 | tf_op jit(solution)/shard_map/ppermute | solution.py:301
  434.6 82.7 %collective-permute-start.17 = (bf16[256,1024]{1,0:T(8,128)(2,1)S(1)}, bf16[256,1024]{1,0:T(8,128)(2,1)S(1)}, u32[]{:S(2)}, u32[]{:S(2)}) collective-permute-start(bf16[256,1024]{1,0:T(8,128)(2,1)S(1)} %copy-done.20), channel_id=1, source_target_pairs={{0,16},{8,24},{16,0},{24,8},{1,17},{9,25},{17,1},{25,9},{2,18},{10... | collective-permute-start | bytes 1572872 | tf_op jit(solution)/shard_map/ppermute | solution.py:301
  435.3 82.0 %collective-permute-start.18 = (bf16[256,1024]{1,0:T(8,128)(2,1)S(1)}, bf16[256,1024]{1,0:T(8,128)(2,1)S(1)}, u32[]{:S(2)}, u32[]{:S(2)}) collective-permute-start(bf16[256,1024]{1,0:T(8,128)(2,1)S(1)} %copy-done.19), channel_id=1, source_target_pairs={{0,24},{8,16},{16,8},{24,0},{1,25},{9,17},{17,9},{25,1},{2,26},{10... | collective-permute-start | bytes 1572872 | tf_op jit(solution)/shard_map/ppermute | solution.py:301
  465.8 10.8 %copy-start.11 = (bf16[256,1024]{1,0:T(8,128)(2,1)}, bf16[256,1024]{1,0:T(8,128)(2,1)S(1)}, u32[]{:S(2)}) copy-start(bf16[256,1024]{1,0:T(8,128)(2,1)S(1)} %collective-permute-done.13.refs_2_) | copy-start | bytes 1572868
  515.3 66.3 %collective-permute-start.15 = (bf16[256,1024]{1,0:T(8,128)(2,1)}, bf16[256,1024]{1,0:T(8,128)(2,1)}, u32[]{:S(2)}, u32[]{:S(2)}) collective-permute-start(bf16[256,1024]{1,0:T(8,128)(2,1)} %get-tuple-element.87), channel_id=1, source_target_pairs={{0,16},{8,24},{16,0},{24,8},{1,17},{9,25},{17,1},{25,9},{2,18},{10... | collective-permute-start | bytes 1572872 | tf_op jit(solution)/shard_map/ppermute | solution.py:301
  516.6 65.0 %collective-permute-start.16 = (bf16[256,1024]{1,0:T(8,128)(2,1)}, bf16[256,1024]{1,0:T(8,128)(2,1)}, u32[]{:S(2)}, u32[]{:S(2)}) collective-permute-start(bf16[256,1024]{1,0:T(8,128)(2,1)} %get-tuple-element.88), channel_id=1, source_target_pairs={{0,24},{8,16},{16,8},{24,0},{1,25},{9,17},{17,9},{25,1},{2,26},{10... | collective-permute-start | bytes 1572872 | tf_op jit(solution)/shard_map/ppermute | solution.py:301
  556.1 72.8 %collective-permute-start.21 = (bf16[256,1024]{1,0:T(8,128)(2,1)}, bf16[256,1024]{1,0:T(8,128)(2,1)}, u32[]{:S(2)}, u32[]{:S(2)}) collective-permute-start(bf16[256,1024]{1,0:T(8,128)(2,1)} %get-tuple-element.101), channel_id=1, source_target_pairs={{0,16},{8,24},{16,0},{24,8},{1,17},{9,25},{17,1},{25,9},{2,18},{10... | collective-permute-start | bytes 1572872 | tf_op jit(solution)/shard_map/ppermute | solution.py:301
  557.8 16.1 %copy-start.4 = (bf16[128,4096]{1,0:T(8,128)(2,1)S(1)}, bf16[128,4096]{1,0:T(8,128)(2,1)}, u32[]{:S(2)}) copy-start(bf16[128,4096]{1,0:T(8,128)(2,1)} %get-tuple-element.80) | copy-start | bytes 3145732
  557.8 71.1 %collective-permute-start.22 = (bf16[256,1024]{1,0:T(8,128)(2,1)}, bf16[256,1024]{1,0:T(8,128)(2,1)}, u32[]{:S(2)}, u32[]{:S(2)}) collective-permute-start(bf16[256,1024]{1,0:T(8,128)(2,1)} %get-tuple-element.102), channel_id=1, source_target_pairs={{0,24},{8,16},{16,8},{24,0},{1,25},{9,17},{17,9},{25,1},{2,26},{10... | collective-permute-start | bytes 1572872 | tf_op jit(solution)/shard_map/ppermute | solution.py:301
  560.9 3.6 collective-permute-start.10
  564.5 3.5 collective-permute-start.11
  568.1 4.4 collective-permute-start.12
  619.4 15.1 %collective-permute-start.19 = (bf16[256,1024]{1,0:T(8,128)(2,1)}, bf16[256,1024]{1,0:T(8,128)(2,1)S(1)}, u32[]{:S(2)}, u32[]{:S(2)}) collective-permute-start(bf16[256,1024]{1,0:T(8,128)(2,1)} %get-tuple-element.99), channel_id=1, source_target_pairs={{0,16},{8,24},{16,0},{24,8},{1,17},{9,25},{17,1},{25,9},{2,18},{10... | collective-permute-start | bytes 1572872 | tf_op jit(solution)/shard_map/ppermute | solution.py:301
  620.6 21.2 %collective-permute-start.20 = (bf16[256,1024]{1,0:T(8,128)(2,1)}, bf16[256,1024]{1,0:T(8,128)(2,1)}, u32[]{:S(2)}, u32[]{:S(2)}) collective-permute-start(bf16[256,1024]{1,0:T(8,128)(2,1)} %get-tuple-element.100), channel_id=1, source_target_pairs={{0,24},{8,16},{16,8},{24,0},{1,25},{9,17},{17,9},{25,1},{2,26},{10... | collective-permute-start | bytes 1572872 | tf_op jit(solution)/shard_map/ppermute | solution.py:301
  (17 other events, 42.2 us)
Sparse Core Ops, SparseCore 0:
  309.4 50.9 all-gather.2

commit v3 on v2

--- a/solution.py
+++ b/solution.py
@@ -29,6 +29,10 @@
     return jnp.sum((per_token * mask_f).reshape(seqs, LEN), axis=1)
 
 
+def tile_of(rows):
+    return 256 if rows % 256 == 0 else rows
+
+
 def mark(token_ref):
     token_ref[...] = jnp.zeros_like(token_ref)
 
@@ -38,33 +42,32 @@
 STAY = pl.BlockSpec(memory_space=pltpu.HBM)
 
 
-def pick_kernel(first, width, masks, me_ref, weight_ref, *refs):
-    *_, token_ref, sems = refs
-    targets = refs[-2 - len(masks) : -2]
-    rows = targets[0].shape[0]
-    copies = []
-    for index, (mask, target) in enumerate(zip(masks, targets)):
-        column = pl.multiple_of((me_ref[0] ^ mask) * width, width)
-        source = weight_ref.at[0, pl.ds(first, rows), pl.ds(column, width)]
-        copies.append(pltpu.make_async_copy(source, target, sems.at[index]))
-    for copy in copies:
-        copy.start()
+def pick_kernel(count, me_ref, *refs):
+    del me_ref
+    token_ref = refs[-1]
     mark(token_ref)
-    for copy in copies:
-        copy.wait()
+    for source_ref, target_ref in zip(refs[:count], refs[-1 - count : -1]):
+        target_ref[...] = source_ref[0]
 
 
 def pick(chunk, chunks, me, weight, masks, width, *after):
     rows = weight.shape[1] // chunks
+    tile = tile_of(rows)
+    first = chunk * (rows // tile)
     count = len(masks)
     *parts, token = pl.pallas_call(
-        functools.partial(pick_kernel, chunk * rows, width, masks),
+        functools.partial(pick_kernel, count),
         grid_spec=pltpu.PrefetchScalarGridSpec(
             num_scalar_prefetch=1,
-            grid=(1,),
-            in_specs=[STAY] * (1 + len(after)),
-            out_specs=[pl.BlockSpec(memory_space=pl.ANY)] * count + [TOKEN_SPEC],
-            scratch_shapes=[pltpu.SemaphoreType.DMA((count,))],
+            grid=(rows // tile,),
+            in_specs=[
+                pl.BlockSpec(
+                    (1, tile, width), lambda i, me, mask=mask: (0, first + i, me[0] ^ mask)
+                )
+                for mask in masks
+            ]
+            + [STAY] * len(after),
+            out_specs=[pl.BlockSpec((tile, width), lambda i, me: (i, 0))] * count + [TOKEN_SPEC],
         ),
         out_shape=[jax.ShapeDtypeStruct((rows, width), weight.dtype)] * count + [TOKEN],
         cost_estimate=pl.CostEstimate(
@@ -72,7 +75,7 @@
         ),
         compiler_params=pltpu.CompilerParams(vmem_limit_bytes=VMEM_LIMIT),
         name="pick",
-    )(me, weight, *after)
+    )(me, *[weight] * count, *after)
     return parts, token
 
 
@@ -103,10 +106,6 @@
         compiler_params=pltpu.CompilerParams(vmem_limit_bytes=VMEM_LIMIT),
         name="assemble",
     )(me, tokens, *others)
-
-
-def tile_of(rows):
-    return 256 if rows % 256 == 0 else rows
 
 
 def partial_kernel(shares_ref, gate_ref, up_ref, *refs):

time: 655 us -> 250 us (0.38)
  Pallas kernels: 521 us -> 84.2 us
  waiting for transfers between devices: 63.2 us -> 95.1 us
    pallas_call x9, Pallas kernels: 463 us -> 25.8 us  [pick(): pl.pallas_call(functools.partial(pick_kernel, count), grid_spec=pltpu.Pre...]
    ppermute x20, waiting for transfers between devices: 57.2 us -> 89.5 us  [swap(): return lax.ppermute(value, 'rep', [(i, i ^ bits) for i in range(groups)])]
  transfers between devices with their start and end apart: 24 -> 24, of which waited for: 10 -> 14; matrix products, arithmetic and copies ran while one was open for 3% -> 8% of each run, Pallas kernels for 77% -> 27%
where the time goes in v3:
time: 250 us; the launch traced here: 249 us
  waiting for transfers between devices  95.1 us (38%)
  Pallas kernels  84.2 us (34%)
  starting transfers between devices  24.5 us (10%)
  matrix products  16.6 us (7%)
  between operations  16 us (6%)
  local copies, waits for them, and re-layouts  9.63 us (4%)
  other arithmetic  3.15 us (1%)
    ppermute x20, waiting for transfers between devices, swap(): return lax.ppermute(value, 'rep', [(i, i ^ bits) for i in range(groups)])  89.5 us
    pallas_call x7, Pallas kernels, outer_update(): pl.pallas_call(functools.partial(outer_kernel, groups, strip), grid_spec=...  30.3 us
    pallas_call x9, Pallas kernels, pick(): pl.pallas_call(functools.partial(pick_kernel, count), grid_spec=pltpu.Pre...  25.8 us
    ppermute x20, starting transfers between devices, swap(): return lax.ppermute(value, 'rep', [(i, i ^ bits) for i in range(groups)])  18.5 us
    pallas_call x1, Pallas kernels, policy_products(): pl.pallas_call(policy_kernel, grid=(unit_rows // tile,), in_specs=[pl.Blo...  16.5 us
    pallas_call x1, Pallas kernels, partial_products(): pl.pallas_call(partial_kernel, grid=(unit_rows // tile,), in_specs=[pl.Bl...  9.96 us
    dot_general x1, matrix products, per_device(): lax.dot_general(gate_grad, inputs, contract, preferred_element_type=jnp.f...  7.72 us
    dot_general x1, matrix products, per_device(): lax.dot_general(up_grad, inputs, contract, preferred_element_type=jnp.flo...  7.65 us
  transfers between devices with their start and end apart: 24, of which 14 were waited for; matrix products, arithmetic and copies ran while one was open for 8% of the time, Pallas kernels for 27%

profile of v3, /device:TPU:0, one launch (start us, length us, event | category | flops | bytes accessed | tf_op | source)
XLA Modules:
  0.0 249.2 jit_solution(2736027735525761388)
XLA Ops:
  9.1 2.5 collective-permute-start.1
  11.7 2.2 pick.10
  13.9 2.2 pick.11
  16.2 8.7 %pick.12 = (bf16[1792,1024]{1,0:T(8,128)(2,1)}, bf16[1792,1024]{1,0:T(8,128)(2,1)}, f32[8,128]{1,0:T(8,128)}) custom-call(s32[1]{0:T(128)} %bitcast.1.me_ref, bf16[1,1792,4096]{2,1,0:T(8,128)(2,1)} %refs_1_.15, bf16[1,1792,4096]{2,1,0:T(8,128)(2,1)} %refs_1_.15, f32[8,128]{1,0:T(8,128)} %get-tuple-element.63.refs_2_), custom_call_target="tpu_custom_call" | custom-call | bytes 14680064 | tf_op jit(solution)/shard_map/pick/pallas_call | solution.py:58
  31.7 11.2 %collective-permute-done.6.refs_2_ = bf16[256,1024]{1,0:T(8,128)(2,1)S(1)} collective-permute-done((bf16[256,1024]{1,0:T(8,128)(2,1)}, bf16[256,1024]{1,0:T(8,128)(2,1)S(1)}, u32[]{:S(2)}, u32[]{:S(2)}) %collective-permute-start.6) | collective-permute-done | bytes 524320 | tf_op jit(solution)/shard_map/ppermute | solution.py:300
  42.9 10.7 %collective-permute-done.7.refs_3_ = bf16[256,1024]{1,0:T(8,128)(2,1)S(1)} collective-permute-done((bf16[256,1024]{1,0:T(8,128)(2,1)S(1)}, bf16[256,1024]{1,0:T(8,128)(2,1)S(1)}, u32[]{:S(2)}, u32[]{:S(2)}) %collective-permute-start.7) | collective-permute-done | bytes 524320 | tf_op jit(solution)/shard_map/ppermute | solution.py:300
  54.3 4.3 %outer_update.7 = (bf16[1792,1024]{1,0:T(8,128)(2,1)}, f32[1792,1024]{1,0:T(8,128)}, f32[8,128]{1,0:T(8,128)}) custom-call(s32[1]{0:T(128)} %bitcast.1.me_ref, bf16[1792,1024]{1,0:T(8,128)(2,1)} %outer_ref.13, f32[1792,1024]{1,0:T(8,128)} %moment_ref.13, bf16[1792,1024]{1,0:T(8,128)(2,1)} %get-tuple-element.64.refs_0_, ...), custom_call_target="tpu_custom_call" | custom-call | flops 12582912 | bytes 5242880 | tf_op jit(solution)/shard_map/outer_update/pallas_call | solution.py:268
  58.7 2.2 pick.13
  60.9 4.4 %collective-permute-done.4.refs_2_ = bf16[256,1024]{1,0:T(8,128)(2,1)S(1)} collective-permute-done((bf16[256,1024]{1,0:T(8,128)(2,1)S(1)}, bf16[256,1024]{1,0:T(8,128)(2,1)S(1)}, u32[]{:S(2)}, u32[]{:S(2)}) %collective-permute-start.4) | collective-permute-done | bytes 524320 | tf_op jit(solution)/shard_map/ppermute | solution.py:300
  65.3 10.3 %collective-permute-done.5.refs_3_ = bf16[256,1024]{1,0:T(8,128)(2,1)S(1)} collective-permute-done((bf16[256,1024]{1,0:T(8,128)(2,1)S(1)}, bf16[256,1024]{1,0:T(8,128)(2,1)S(1)}, u32[]{:S(2)}, u32[]{:S(2)}) %collective-permute-start.5) | collective-permute-done | bytes 524320 | tf_op jit(solution)/shard_map/ppermute | solution.py:300
  76.4 4.3 %outer_update.8 = (bf16[1792,1024]{1,0:T(8,128)(2,1)}, f32[1792,1024]{1,0:T(8,128)}, f32[8,128]{1,0:T(8,128)}) custom-call(s32[1]{0:T(128)} %bitcast.1.me_ref, bf16[1792,1024]{1,0:T(8,128)(2,1)} %outer_ref.13, f32[1792,1024]{1,0:T(8,128)} %moment_ref.13, bf16[1792,1024]{1,0:T(8,128)(2,1)} %get-tuple-element.64.refs_0_, ...), custom_call_target="tpu_custom_call", output_to_operand_aliasing={{0}: (7, {}), {1}: (8, {})} | custom-call | flops 12582912 | bytes 5242880 | tf_op jit(solution)/shard_map/outer_update/pallas_call | solution.py:268
  80.7 2.3 pick.14
  83.0 10.0 %partial_products.1 = (f32[2,2,128,1792]{3,2,1,0:T(8,128)}, bf16[2,2,128,1792]{3,2,1,0:T(8,128)(2,1)}, f32[8,128]{1,0:T(8,128)}) custom-call(bf16[8,8,16,1024]{3,2,1,0:T(8,128)(2,1)} %bitcast.52, bf16[1792,1024]{1,0:T(8,128)(2,1)} %outer_ref.13, bf16[1792,1024]{1,0:T(8,128)(2,1)} %up_ref.1, f32[8,128]{1,0:T(8,128)} %get-tuple-element.75.refs_0_), custom_call_target="tpu_custom_call" | custom-call | flops 3758096384 | bytes 12845056 | tf_op jit(solution)/shard_map/partial_products/pallas_call | solution.py:136
  95.5 3.4 %collective-permute-done.8 = bf16[2,2,128,1792]{3,2,0,1:T(8,128)(2,1)S(1)} collective-permute-done((bf16[2,2,128,1792]{3,2,0,1:T(8,128)(2,1)S(1)}, bf16[2,2,128,1792]{3,2,0,1:T(8,128)(2,1)S(1)}, u32[]{:S(2)}, u32[]{:S(2)}) %collective-permute-start.8) | collective-permute-done | bytes 1835040 | tf_op jit(solution)/shard_map/ppermute | solution.py:300
  107.6 16.5 %policy_products.1 = (f32[128,1792]{1,0:T(8,128)}, f32[128,1792]{1,0:T(8,128)}, bf16[128,4096]{1,0:T(8,128)(2,1)}, f32[8,128]{1,0:T(8,128)}) custom-call(bf16[8,8,16,1024]{3,2,1,0:T(8,128)(2,1)} %bitcast.53, bf16[1,1792,4096]{2,1,0:T(8,128)(2,1)} %refs_1_.15, bf16[1,1792,4096]{2,1,0:T(8,128)(2,1)} %w_up_ref.1, bf16[2,128,1792]{2,1,0:T(8,128)(2,1)} %fusion.11.refs_0_), custom_call_target="tpu_custom_call" | custom-call | flops 3758096384 | bytes 31195136 | tf_op jit(solution)/shard_map/policy_products/pallas_call | solution.py:190
  124.0 12.7 %collective-permute-done.13.refs_2_ = bf16[256,1024]{1,0:T(8,128)(2,1)S(1)} collective-permute-done((bf16[256,1024]{1,0:T(8,128)(2,1)}, bf16[256,1024]{1,0:T(8,128)(2,1)S(1)}, u32[]{:S(2)}, u32[]{:S(2)}) %collective-permute-start.13) | collective-permute-done | bytes 524320 | tf_op jit(solution)/shard_map/ppermute | solution.py:300
  136.8 10.6 %collective-permute-done.14.refs_3_ = bf16[256,1024]{1,0:T(8,128)(2,1)S(1)} collective-permute-done((bf16[256,1024]{1,0:T(8,128)(2,1)}, bf16[256,1024]{1,0:T(8,128)(2,1)S(1)}, u32[]{:S(2)}, u32[]{:S(2)}) %collective-permute-start.14) | collective-permute-done | bytes 524320 | tf_op jit(solution)/shard_map/ppermute | solution.py:300
  148.2 4.3 %outer_update.9 = (bf16[1792,1024]{1,0:T(8,128)(2,1)}, f32[1792,1024]{1,0:T(8,128)}, f32[8,128]{1,0:T(8,128)}) custom-call(s32[1]{0:T(128)} %bitcast.1.me_ref, bf16[1792,1024]{1,0:T(8,128)(2,1)} %outer_ref.13, f32[1792,1024]{1,0:T(8,128)} %moment_ref.13, bf16[1792,1024]{1,0:T(8,128)(2,1)} %get-tuple-element.64.refs_0_, ...), custom_call_target="tpu_custom_call", output_to_operand_aliasing={{0}: (7, {}), {1}: (8, {})} | custom-call | flops 12582912 | bytes 5242880 | tf_op jit(solution)/shard_map/outer_update/pallas_call | solution.py:268
  152.5 2.3 pick.15
  156.6 2.6 %collective-permute-done.17.refs_2_ = bf16[256,1024]{1,0:T(8,128)(2,1)S(1)} collective-permute-done((bf16[256,1024]{1,0:T(8,128)(2,1)S(1)}, bf16[256,1024]{1,0:T(8,128)(2,1)S(1)}, u32[]{:S(2)}, u32[]{:S(2)}) %collective-permute-start.17) | collective-permute-done | bytes 524320 | tf_op jit(solution)/shard_map/ppermute | solution.py:300
  159.2 10.5 %collective-permute-done.18.refs_3_ = bf16[256,1024]{1,0:T(8,128)(2,1)S(1)} collective-permute-done((bf16[256,1024]{1,0:T(8,128)(2,1)S(1)}, bf16[256,1024]{1,0:T(8,128)(2,1)S(1)}, u32[]{:S(2)}, u32[]{:S(2)}) %collective-permute-start.18) | collective-permute-done | bytes 524320 | tf_op jit(solution)/shard_map/ppermute | solution.py:300
  170.5 4.3 %outer_update.10 = (bf16[1792,1024]{1,0:T(8,128)(2,1)}, f32[1792,1024]{1,0:T(8,128)}, f32[8,128]{1,0:T(8,128)}) custom-call(s32[1]{0:T(128)} %bitcast.1.me_ref, bf16[1792,1024]{1,0:T(8,128)(2,1)} %outer_ref.13, f32[1792,1024]{1,0:T(8,128)} %moment_ref.13, ...), custom_call_target="tpu_custom_call", output_to_operand_aliasing={{0}: (7, {}), {1}: (8, {})} | custom-call | flops 12582912 | bytes 5242880 | tf_op jit(solution)/shard_map/outer_update/pallas_call | solution.py:268
  174.8 2.2 pick.16
  189.3 2.7 %collective-permute-start.12 = (f32[8]{0:T(128)S(1)}, f32[8]{0:T(128)S(1)}, u32[]{:S(2)}, u32[]{:S(2)}) collective-permute-start(f32[8]{0:T(128)S(1)} %add.39), channel_id=1, source_target_pairs={{0,4},{1,5},{2,6},{3,7},{4,0},{5,1},{6,2},{7,3},{8,12},{9,13},{10,... | collective-permute-start | bytes 104 | tf_op jit(solution)/shard_map/ppermute | solution.py:351
  195.1 7.7 %convolution_convert_fusion.1.refs_7_ = bf16[1792,4096]{1,0:T(8,128)(2,1)} fusion(bf16[128,4096]{1,0:T(8,128)(2,1)S(1)} %copy-done.4, f32[128,1792]{1,0:T(8,128)S(1)} %copy-done.3, bf16[128,1792]{1,0:T(8,128)(2,1)S(1)} %copy-done.2, f32[128,1792]{1,0:T(8,128)S(1)} %copy-done, f32[128]{0:T(128)S(1)} %convert_multiply_fusion.3), kind=kOutput, calls=%fused_computation.1 | convolution fusion | flops 1889140736 | bytes 18022912 | tf_op jit(solution)/shard_map/dot_general | solution.py:372
  202.8 4.3 %outer_update.11 = (bf16[1792,1024]{1,0:T(8,128)(2,1)}, f32[1792,1024]{1,0:T(8,128)}, f32[8,128]{1,0:T(8,128)}) custom-call(s32[1]{0:T(128)} %bitcast.1.me_ref, bf16[1792,1024]{1,0:T(8,128)(2,1)} %outer_ref.13, f32[1792,1024]{1,0:T(8,128)} %moment_ref.13, ...), custom_call_target="tpu_custom_call", output_to_operand_aliasing={{0}: (7, {}), {1}: (8, {})} | custom-call | flops 12582912 | bytes 5242880 | tf_op jit(solution)/shard_map/outer_update/pallas_call | solution.py:268
  207.1 2.3 pick.17
  211.1 7.7 %convolution_convert_fusion.refs_7_ = bf16[1792,4096]{1,0:T(8,128)(2,1)} fusion(bf16[128,4096]{1,0:T(8,128)(2,1)S(1)} %copy-done.4, bf16[128,1792]{1,0:T(8,128)(2,1)S(1)} %copy-done.2, f32[128]{0:T(128)S(1)} %convert_multiply_fusion.3, f32[128,1792]{1,0:T(8,128)S(1)} %copy-done), kind=kOutput, calls=%fused_computation | convolution fusion | flops 1888223232 | bytes 17105408 | tf_op jit(solution)/shard_map/dot_general | solution.py:375
  219.4 4.3 %outer_update.12 = (bf16[1792,1024]{1,0:T(8,128)(2,1)}, f32[1792,1024]{1,0:T(8,128)}, f32[8,128]{1,0:T(8,128)}) custom-call(s32[1]{0:T(128)} %bitcast.1.me_ref, bf16[1792,1024]{1,0:T(8,128)(2,1)} %outer_ref.13, f32[1792,1024]{1,0:T(8,128)} %moment_ref.13, ...), custom_call_target="tpu_custom_call", output_to_operand_aliasing={{0}: (7, {}), {1}: (8, {})} | custom-call | flops 12582912 | bytes 5242880 | tf_op jit(solution)/shard_map/outer_update/pallas_call | solution.py:268
  223.8 2.9 %collective-permute-done.19.refs_2_ = bf16[256,1024]{1,0:T(8,128)(2,1)S(1)} collective-permute-done((bf16[256,1024]{1,0:T(8,128)(2,1)}, bf16[256,1024]{1,0:T(8,128)(2,1)S(1)}, u32[]{:S(2)}, u32[]{:S(2)}) %collective-permute-start.19) | collective-permute-done | bytes 524320 | tf_op jit(solution)/shard_map/ppermute | solution.py:300
  226.6 10.2 %collective-permute-done.20.refs_3_ = bf16[256,1024]{1,0:T(8,128)(2,1)} collective-permute-done((bf16[256,1024]{1,0:T(8,128)(2,1)}, bf16[256,1024]{1,0:T(8,128)(2,1)}, u32[]{:S(2)}, u32[]{:S(2)}) %collective-permute-start.20) | collective-permute-done | bytes 524320 | tf_op jit(solution)/shard_map/ppermute | solution.py:300
  236.9 4.3 %outer_update.13 = (bf16[1792,1024]{1,0:T(8,128)(2,1)}, f32[1792,1024]{1,0:T(8,128)}, f32[8,128]{1,0:T(8,128)}) custom-call(s32[1]{0:T(128)} %bitcast.1.me_ref, bf16[1792,1024]{1,0:T(8,128)(2,1)} %outer_ref.13, f32[1792,1024]{1,0:T(8,128)} %moment_ref.13, ...), custom_call_target="tpu_custom_call", output_to_operand_aliasing={{0}: (7, {}), {1}: (8, {})} | custom-call | flops 12582912 | bytes 5242880 | tf_op jit(solution)/shard_map/outer_update/pallas_call | solution.py:268
  (109 shorter events, 42.0 us)
Async XLA Ops:
  7.2 75.8 %all-gather.3.cloned.1.call-start = ((), (), s32[]{:S(2)}) async-start(), calls=%async_computation | async-start | bytes 2359296 | tf_op jit(solution)/shard_map/all_gather | solution.py:320
  8.6 16.3 %collective-permute-start = (bf16[16,1024]{1,0:T(8,128)(2,1)}, bf16[16,1024]{1,0:T(8,128)(2,1)S(1)}, u32[]{:S(2)}, u32[]{:S(2)}) collective-permute-start(bf16[16,1024]{1,0:T(8,128)(2,1)} %get-tuple-element.58), channel_id=1, source_target_pairs={{0,8},{8,0},{16,24},{24,16},{1,9},{9,1},{17,25},{25,17},{2,10},{10... | collective-permute-start | bytes 98312 | tf_op jit(solution)/shard_map/ppermute | solution.py:300
  9.1 15.8 %collective-permute-start.1 = (bf16[16,1024]{1,0:T(8,128)(2,1)}, bf16[16,1024]{1,0:T(8,128)(2,1)S(1)}, u32[]{:S(2)}, u32[]{:S(2)}) collective-permute-start(bf16[16,1024]{1,0:T(8,128)(2,1)} %get-tuple-element.59), channel_id=1, source_target_pairs={{0,16},{8,24},{16,0},{24,8},{1,17},{9,25},{17,1},{25,9},{2,18},{10... | collective-permute-start | bytes 98312 | tf_op jit(solution)/shard_map/ppermute | solution.py:300
  11.6 13.4 %collective-permute-start.2 = (bf16[16,1024]{1,0:T(8,128)(2,1)}, bf16[16,1024]{1,0:T(8,128)(2,1)S(1)}, u32[]{:S(2)}, u32[]{:S(2)}) collective-permute-start(bf16[16,1024]{1,0:T(8,128)(2,1)} %get-tuple-element.60), channel_id=1, source_target_pairs={{0,24},{8,16},{16,8},{24,0},{1,25},{9,17},{17,9},{25,1},{2,26},{10... | collective-permute-start | bytes 98312 | tf_op jit(solution)/shard_map/ppermute | solution.py:300
  16.1 13.7 %copy-start.23 = (bf16[256,1024]{1,0:T(8,128)(2,1)S(1)}, bf16[256,1024]{1,0:T(8,128)(2,1)}, u32[]{:S(2)}) copy-start(bf16[256,1024]{1,0:T(8,128)(2,1)} %get-tuple-element.69) | copy-start | bytes 1572868
  16.1 13.7 %copy-start.22 = (bf16[256,1024]{1,0:T(8,128)(2,1)S(1)}, bf16[256,1024]{1,0:T(8,128)(2,1)}, u32[]{:S(2)}) copy-start(bf16[256,1024]{1,0:T(8,128)(2,1)} %get-tuple-element.66) | copy-start | bytes 1572868
  16.2 15.3 %copy-start.21 = (bf16[256,1024]{1,0:T(8,128)(2,1)S(1)}, bf16[256,1024]{1,0:T(8,128)(2,1)}, u32[]{:S(2)}) copy-start(bf16[256,1024]{1,0:T(8,128)(2,1)} %get-tuple-element.67) | copy-start | bytes 1572868
  24.8 28.7 %collective-permute-start.3 = (bf16[1792,1024]{1,0:T(8,128)(2,1)}, bf16[1792,1024]{1,0:T(8,128)(2,1)}, u32[]{:S(2)}, u32[]{:S(2)}) collective-permute-start(bf16[1792,1024]{1,0:T(8,128)(2,1)} %get-tuple-element.65), channel_id=1, source_target_pairs={{0,8},{8,0},{16,24},{24,16},{1,9},{9,1},{17,25},{25,17},{2,10},{10... | collective-permute-start | bytes 11010056 | tf_op jit(solution)/shard_map/ppermute | solution.py:300
  27.9 15.0 %collective-permute-start.6 = (bf16[256,1024]{1,0:T(8,128)(2,1)}, bf16[256,1024]{1,0:T(8,128)(2,1)S(1)}, u32[]{:S(2)}, u32[]{:S(2)}) collective-permute-start(bf16[256,1024]{1,0:T(8,128)(2,1)} %get-tuple-element.68), channel_id=1, source_target_pairs={{0,16},{8,24},{16,0},{24,8},{1,17},{9,25},{17,1},{25,9},{2,18},{10... | collective-permute-start | bytes 1572872 | tf_op jit(solution)/shard_map/ppermute | solution.py:300
  29.8 23.7 %collective-permute-start.7 = (bf16[256,1024]{1,0:T(8,128)(2,1)S(1)}, bf16[256,1024]{1,0:T(8,128)(2,1)S(1)}, u32[]{:S(2)}, u32[]{:S(2)}) collective-permute-start(bf16[256,1024]{1,0:T(8,128)(2,1)S(1)} %copy-done.23), channel_id=1, source_target_pairs={{0,24},{8,16},{16,8},{24,0},{1,25},{9,17},{17,9},{25,1},{2,26},{10... | collective-permute-start | bytes 1572872 | tf_op jit(solution)/shard_map/ppermute | solution.py:300
  29.8 35.5 %collective-permute-start.4 = (bf16[256,1024]{1,0:T(8,128)(2,1)S(1)}, bf16[256,1024]{1,0:T(8,128)(2,1)S(1)}, u32[]{:S(2)}, u32[]{:S(2)}) collective-permute-start(bf16[256,1024]{1,0:T(8,128)(2,1)S(1)} %copy-done.22), channel_id=1, source_target_pairs={{0,16},{8,24},{16,0},{24,8},{1,17},{9,25},{17,1},{25,9},{2,18},{10... | collective-permute-start | bytes 1572872 | tf_op jit(solution)/shard_map/ppermute | solution.py:300
  31.4 44.2 %collective-permute-start.5 = (bf16[256,1024]{1,0:T(8,128)(2,1)S(1)}, bf16[256,1024]{1,0:T(8,128)(2,1)S(1)}, u32[]{:S(2)}, u32[]{:S(2)}) collective-permute-start(bf16[256,1024]{1,0:T(8,128)(2,1)S(1)} %copy-done.21), channel_id=1, source_target_pairs={{0,24},{8,16},{16,8},{24,0},{1,25},{9,17},{17,9},{25,1},{2,26},{10... | collective-permute-start | bytes 1572872 | tf_op jit(solution)/shard_map/ppermute | solution.py:300
  42.9 10.7 %copy-start.13 = (bf16[256,1024]{1,0:T(8,128)(2,1)}, bf16[256,1024]{1,0:T(8,128)(2,1)S(1)}, u32[]{:S(2)}) copy-start(bf16[256,1024]{1,0:T(8,128)(2,1)S(1)} %collective-permute-done.6.refs_2_) | copy-start | bytes 1572868
  65.3 10.3 %copy-start.9 = (bf16[256,1024]{1,0:T(8,128)(2,1)}, bf16[256,1024]{1,0:T(8,128)(2,1)S(1)}, u32[]{:S(2)}) copy-start(bf16[256,1024]{1,0:T(8,128)(2,1)S(1)} %collective-permute-done.4.refs_2_) | copy-start | bytes 1572868
  94.7 4.2 %collective-permute-start.8 = (bf16[2,2,128,1792]{3,2,0,1:T(8,128)(2,1)S(1)}, bf16[2,2,128,1792]{3,2,0,1:T(8,128)(2,1)S(1)}, u32[]{:S(2)}, u32[]{:S(2)}) collective-permute-start(bf16[2,2,128,1792]{3,2,0,1:T(8,128)(2,1)S(1)} %copy.28), channel_id=1, source_target_pairs={{0,8},{8,0},{16,24},{24,16},{1,9},{9,1},{17,25},{25,17},{2,10},{10... | collective-permute-start | bytes 5505032 | tf_op jit(solution)/shard_map/ppermute | solution.py:300
  102.1 77.0 %collective-permute-start.9 = (bf16[2,128,1792]{2,1,0:T(8,128)(2,1)}, bf16[2,128,1792]{2,1,0:T(8,128)(2,1)}, u32[]{:S(2)}, u32[]{:S(2)}) collective-permute-start(bf16[2,128,1792]{2,1,0:T(8,128)(2,1)} %fusion.11.refs_0_), channel_id=1, source_target_pairs={{0,16},{8,24},{16,0},{24,8},{1,17},{9,25},{17,1},{25,9},{2,18},{10... | collective-permute-start | bytes 2752520 | tf_op jit(solution)/shard_map/ppermute | solution.py:300
  103.9 32.9 %collective-permute-start.13 = (bf16[256,1024]{1,0:T(8,128)(2,1)}, bf16[256,1024]{1,0:T(8,128)(2,1)S(1)}, u32[]{:S(2)}, u32[]{:S(2)}) collective-permute-start(bf16[256,1024]{1,0:T(8,128)(2,1)} %get-tuple-element.81), channel_id=1, source_target_pairs={{0,16},{8,24},{16,0},{24,8},{1,17},{9,25},{17,1},{25,9},{2,18},{10... | collective-permute-start | bytes 1572872 | tf_op jit(solution)/shard_map/ppermute | solution.py:300
  104.2 43.2 %collective-permute-start.14 = (bf16[256,1024]{1,0:T(8,128)(2,1)}, bf16[256,1024]{1,0:T(8,128)(2,1)S(1)}, u32[]{:S(2)}, u32[]{:S(2)}) collective-permute-start(bf16[256,1024]{1,0:T(8,128)(2,1)} %get-tuple-element.82), channel_id=1, source_target_pairs={{0,24},{8,16},{16,8},{24,0},{1,25},{9,17},{17,9},{25,1},{2,26},{10... | collective-permute-start | bytes 1572872 | tf_op jit(solution)/shard_map/ppermute | solution.py:300
  105.3 53.9 %collective-permute-start.17 = (bf16[256,1024]{1,0:T(8,128)(2,1)S(1)}, bf16[256,1024]{1,0:T(8,128)(2,1)S(1)}, u32[]{:S(2)}, u32[]{:S(2)}) collective-permute-start(bf16[256,1024]{1,0:T(8,128)(2,1)S(1)} %copy-done.20), channel_id=1, source_target_pairs={{0,16},{8,24},{16,0},{24,8},{1,17},{9,25},{17,1},{25,9},{2,18},{10... | collective-permute-start | bytes 1572872 | tf_op jit(solution)/shard_map/ppermute | solution.py:300
  105.9 63.8 %collective-permute-start.18 = (bf16[256,1024]{1,0:T(8,128)(2,1)S(1)}, bf16[256,1024]{1,0:T(8,128)(2,1)S(1)}, u32[]{:S(2)}, u32[]{:S(2)}) collective-permute-start(bf16[256,1024]{1,0:T(8,128)(2,1)S(1)} %copy-done.19), channel_id=1, source_target_pairs={{0,24},{8,16},{16,8},{24,0},{1,25},{9,17},{17,9},{25,1},{2,26},{10... | collective-permute-start | bytes 1572872 | tf_op jit(solution)/shard_map/ppermute | solution.py:300
  136.8 10.6 %copy-start.11 = (bf16[256,1024]{1,0:T(8,128)(2,1)}, bf16[256,1024]{1,0:T(8,128)(2,1)S(1)}, u32[]{:S(2)}) copy-start(bf16[256,1024]{1,0:T(8,128)(2,1)S(1)} %collective-permute-done.13.refs_2_) | copy-start | bytes 1572868
  154.8 48.0 %collective-permute-start.15 = (bf16[256,1024]{1,0:T(8,128)(2,1)}, bf16[256,1024]{1,0:T(8,128)(2,1)}, u32[]{:S(2)}, u32[]{:S(2)}) collective-permute-start(bf16[256,1024]{1,0:T(8,128)(2,1)} %get-tuple-element.87), channel_id=1, source_target_pairs={{0,16},{8,24},{16,0},{24,8},{1,17},{9,25},{17,1},{25,9},{2,18},{10... | collective-permute-start | bytes 1572872 | tf_op jit(solution)/shard_map/ppermute | solution.py:300
  156.1 46.8 %collective-permute-start.16 = (bf16[256,1024]{1,0:T(8,128)(2,1)}, bf16[256,1024]{1,0:T(8,128)(2,1)}, u32[]{:S(2)}, u32[]{:S(2)}) collective-permute-start(bf16[256,1024]{1,0:T(8,128)(2,1)} %get-tuple-element.88), channel_id=1, source_target_pairs={{0,24},{8,16},{16,8},{24,0},{1,25},{9,17},{17,9},{25,1},{2,26},{10... | collective-permute-start | bytes 1572872 | tf_op jit(solution)/shard_map/ppermute | solution.py:300
  159.2 10.5 %copy-start.6 = (bf16[256,1024]{1,0:T(8,128)(2,1)}, bf16[256,1024]{1,0:T(8,128)(2,1)S(1)}, u32[]{:S(2)}) copy-start(bf16[256,1024]{1,0:T(8,128)(2,1)S(1)} %collective-permute-done.17.refs_2_) | copy-start | bytes 1572868
  177.1 42.4 %collective-permute-start.21 = (bf16[256,1024]{1,0:T(8,128)(2,1)}, bf16[256,1024]{1,0:T(8,128)(2,1)}, u32[]{:S(2)}, u32[]{:S(2)}) collective-permute-start(bf16[256,1024]{1,0:T(8,128)(2,1)} %get-tuple-element.101), channel_id=1, source_target_pairs={{0,16},{8,24},{16,0},{24,8},{1,17},{9,25},{17,1},{25,9},{2,18},{10... | collective-permute-start | bytes 1572872 | tf_op jit(solution)/shard_map/ppermute | solution.py:300
  178.5 16.6 %copy-start.4 = (bf16[128,4096]{1,0:T(8,128)(2,1)S(1)}, bf16[128,4096]{1,0:T(8,128)(2,1)}, u32[]{:S(2)}) copy-start(bf16[128,4096]{1,0:T(8,128)(2,1)} %get-tuple-element.80) | copy-start | bytes 3145732
  178.5 40.9 %collective-permute-start.22 = (bf16[256,1024]{1,0:T(8,128)(2,1)}, bf16[256,1024]{1,0:T(8,128)(2,1)}, u32[]{:S(2)}, u32[]{:S(2)}) collective-permute-start(bf16[256,1024]{1,0:T(8,128)(2,1)} %get-tuple-element.102), channel_id=1, source_target_pairs={{0,24},{8,16},{16,8},{24,0},{1,25},{9,17},{17,9},{25,1},{2,26},{10... | collective-permute-start | bytes 1572872 | tf_op jit(solution)/shard_map/ppermute | solution.py:300
  182.1 3.6 %collective-permute-start.10 = (f32[8]{0:T(128)S(1)}, f32[8]{0:T(128)S(1)}, u32[]{:S(2)}, u32[]{:S(2)}) collective-permute-start(f32[8]{0:T(128)S(1)} %sub.12), channel_id=1, source_target_pairs={{0,1},{1,0},{2,3},{3,2},{4,5},{5,4},{6,7},{7,6},{8,9},{9,8},{10,11... | collective-permute-start | bytes 104 | tf_op jit(solution)/shard_map/ppermute | solution.py:351
  185.7 3.5 %collective-permute-start.11 = (f32[8]{0:T(128)S(1)}, f32[8]{0:T(128)S(1)}, u32[]{:S(2)}, u32[]{:S(2)}) collective-permute-start(f32[8]{0:T(128)S(1)} %add.38), channel_id=1, source_target_pairs={{0,2},{1,3},{2,0},{3,1},{4,6},{5,7},{6,4},{7,5},{8,10},{9,11},{10,... | collective-permute-start | bytes 104 | tf_op jit(solution)/shard_map/ppermute | solution.py:351
  189.3 4.4 %collective-permute-start.12 = (f32[8]{0:T(128)S(1)}, f32[8]{0:T(128)S(1)}, u32[]{:S(2)}, u32[]{:S(2)}) collective-permute-start(f32[8]{0:T(128)S(1)} %add.39), channel_id=1, source_target_pairs={{0,4},{1,5},{2,6},{3,7},{4,0},{5,1},{6,2},{7,3},{8,12},{9,13},{10,... | collective-permute-start | bytes 104 | tf_op jit(solution)/shard_map/ppermute | solution.py:351
  209.5 17.2 %collective-permute-start.19 = (bf16[256,1024]{1,0:T(8,128)(2,1)}, bf16[256,1024]{1,0:T(8,128)(2,1)S(1)}, u32[]{:S(2)}, u32[]{:S(2)}) collective-permute-start(bf16[256,1024]{1,0:T(8,128)(2,1)} %get-tuple-element.99), channel_id=1, source_target_pairs={{0,16},{8,24},{16,0},{24,8},{1,17},{9,25},{17,1},{25,9},{2,18},{10... | collective-permute-start | bytes 1572872 | tf_op jit(solution)/shard_map/ppermute | solution.py:300
  211.1 25.8 %collective-permute-start.20 = (bf16[256,1024]{1,0:T(8,128)(2,1)}, bf16[256,1024]{1,0:T(8,128)(2,1)}, u32[]{:S(2)}, u32[]{:S(2)}) collective-permute-start(bf16[256,1024]{1,0:T(8,128)(2,1)} %get-tuple-element.100), channel_id=1, source_target_pairs={{0,24},{8,16},{16,8},{24,0},{1,25},{9,17},{17,9},{25,1},{2,26},{10... | collective-permute-start | bytes 1572872 | tf_op jit(solution)/shard_map/ppermute | solution.py:300
  (17 other events, 60.1 us)
Sparse Core Ops, SparseCore 0:
  28.0 50.9 all-gather.2

commit v4 on v3

--- a/solution.py
+++ b/solution.py
@@ -9,8 +9,9 @@
 
 BLOCK = 128
 LEN = 16
-CHUNKS = 7
+CHUNKS = (4, 5, 3, 1, 1)
 VMEM_LIMIT = 60 * 1024 * 1024
+BRIEF = pl.CostEstimate(flops=1, bytes_accessed=1, transcendentals=0)
 
 dpo_beta = 0.1
 outer_rate = 0.7
@@ -50,16 +51,14 @@
         target_ref[...] = source_ref[0]
 
 
-def pick(chunk, chunks, me, weight, masks, width, *after):
-    rows = weight.shape[1] // chunks
-    tile = tile_of(rows)
-    first = chunk * (rows // tile)
+def pick(first, steps, tile, me, weight, masks, width, *after):
+    rows = steps * tile
     count = len(masks)
     *parts, token = pl.pallas_call(
         functools.partial(pick_kernel, count),
         grid_spec=pltpu.PrefetchScalarGridSpec(
             num_scalar_prefetch=1,
-            grid=(rows // tile,),
+            grid=(steps,),
             in_specs=[
                 pl.BlockSpec(
                     (1, tile, width), lambda i, me, mask=mask: (0, first + i, me[0] ^ mask)
@@ -70,9 +69,7 @@
             out_specs=[pl.BlockSpec((tile, width), lambda i, me: (i, 0))] * count + [TOKEN_SPEC],
         ),
         out_shape=[jax.ShapeDtypeStruct((rows, width), weight.dtype)] * count + [TOKEN],
-        cost_estimate=pl.CostEstimate(
-            flops=0, bytes_accessed=rows * width * 4 * count, transcendentals=0
-        ),
+        cost_estimate=BRIEF,
         compiler_params=pltpu.CompilerParams(vmem_limit_bytes=VMEM_LIMIT),
         name="pick",
     )(me, *[weight] * count, *after)
@@ -80,8 +77,9 @@
 
 
 def assemble_kernel(groups, me_ref, tokens_ref, *refs):
-    out_ref = refs[-1]
+    out_ref, token_ref = refs[-2:]
     width = out_ref.shape[2]
+    mark(token_ref)
     for block in range(groups):
         out_ref[block] = tokens_ref[:, block * width : (block + 1) * width]
     out_ref[groups] = tokens_ref[:, pl.ds(pl.multiple_of(me_ref[0] * width, width), width)]
@@ -89,7 +87,7 @@
         out_ref[groups + k] = refs[k - 1][...]
 
 
-def assemble(me, tokens, others):
+def assemble(me, tokens, others, *after):
     groups = len(others) + 1
     rows, depth = tokens.shape
     width = depth // groups
@@ -99,17 +97,22 @@
         grid_spec=pltpu.PrefetchScalarGridSpec(
             num_scalar_prefetch=1,
             grid=(1,),
-            in_specs=[pl.BlockSpec((rows, depth), lambda i, me: (0, 0))] + [whole] * (groups - 1),
-            out_specs=pl.BlockSpec((2 * groups, rows, width), lambda i, me: (0, 0, 0)),
+            in_specs=[pl.BlockSpec((rows, depth), lambda i, me: (0, 0))] + [whole] * (groups - 1)
+            + [STAY] * len(after),
+            out_specs=[
+                pl.BlockSpec((2 * groups, rows, width), lambda i, me: (0, 0, 0)),
+                TOKEN_SPEC,
+            ],
         ),
-        out_shape=jax.ShapeDtypeStruct((2 * groups, rows, width), tokens.dtype),
+        out_shape=[jax.ShapeDtypeStruct((2 * groups, rows, width), tokens.dtype), TOKEN],
+        cost_estimate=BRIEF,
         compiler_params=pltpu.CompilerParams(vmem_limit_bytes=VMEM_LIMIT),
         name="assemble",
-    )(me, tokens, *others)
+    )(me, tokens, *others, *after)
 
 
 def partial_kernel(shares_ref, gate_ref, up_ref, *refs):
-    keep_ref, leave_ref, token_ref = refs[-3:]
+    *results, token_ref = refs[-1 - 2 * shares_ref.shape[1] :]
     ranks, groups, rows, width = shares_ref.shape
     shares = shares_ref[...].reshape(ranks * groups * rows, width)
     mark(token_ref)
@@ -118,10 +121,8 @@
         product = product.reshape(ranks, groups, rows, product.shape[1])
         for k in range(groups):
             part = product[:, k].reshape(ranks * rows, product.shape[3])
-            if k % 2:
-                leave_ref[which, k // 2] = part.astype(leave_ref.dtype)
-            else:
-                keep_ref[which, k // 2] = part
+            target_ref = results[which * groups + k]
+            target_ref[...] = part.astype(target_ref.dtype)
 
 
 def partial_products(gathered, outer_gate, outer_up, *after):
@@ -131,8 +132,7 @@
     tile = tile_of(unit_rows)
     group_tok = ranks * rows
     weight = pl.BlockSpec((tile, width), lambda i: (i, 0))
-    result = pl.BlockSpec((2, groups // 2, group_tok, tile), lambda i: (0, 0, 0, i))
-    shape = (2, groups // 2, group_tok, unit_rows)
+    result = pl.BlockSpec((group_tok, tile), lambda i: (0, i))
     return pl.pallas_call(
         partial_kernel,
         grid=(unit_rows // tile,),
@@ -146,20 +146,49 @@
             weight,
         ]
         + [STAY] * len(after),
-        out_specs=[result, result, TOKEN_SPEC],
+        out_specs=[result] * (2 * groups) + [TOKEN_SPEC],
         out_shape=[
-            jax.ShapeDtypeStruct(shape, jnp.float32),
-            jax.ShapeDtypeStruct(shape, jnp.bfloat16),
-            TOKEN,
-        ],
-        compiler_params=pltpu.CompilerParams(vmem_limit_bytes=VMEM_LIMIT),
-        cost_estimate=pl.CostEstimate(
-            flops=4 * groups * group_tok * width * unit_rows,
-            bytes_accessed=unit_rows * (4 * width + 6 * groups * group_tok),
-            transcendentals=0,
-        ),
+            jax.ShapeDtypeStruct(
+                (group_tok, unit_rows), jnp.bfloat16 if k % 2 else jnp.float32
+            )
+            for _ in range(2)
+            for k in range(groups)
+        ]
+        + [TOKEN],
+        compiler_params=pltpu.CompilerParams(vmem_limit_bytes=VMEM_LIMIT),
+        cost_estimate=BRIEF,
         name="partial_products",
     )(gathered, outer_gate, outer_up, *after)
+
+
+def join_kernel(*refs):
+    *parts, leave_gate_ref, leave_up_ref, stay_gate_ref, stay_up_ref, token_ref = refs
+    mark(token_ref)
+    targets = ((leave_gate_ref, stay_gate_ref), (leave_up_ref, stay_up_ref))
+    for which, (leave_ref, target_ref) in enumerate(targets):
+        stay_ref, mate_ref, far_ref, both_ref = parts[4 * which : 4 * which + 4]
+        target_ref[...] = stay_ref[...] + mate_ref[...].astype(jnp.float32)
+        leave_ref[...] = (far_ref[...] + both_ref[...].astype(jnp.float32)).astype(
+            leave_ref.dtype
+        )
+
+
+def join(parts):
+    group_tok, unit_rows = parts[0].shape
+    tile = tile_of(unit_rows)
+    block = pl.BlockSpec((group_tok, tile), lambda i: (0, i))
+    leave = jax.ShapeDtypeStruct((group_tok, unit_rows), jnp.bfloat16)
+    stay = jax.ShapeDtypeStruct((group_tok, unit_rows), jnp.float32)
+    return pl.pallas_call(
+        join_kernel,
+        grid=(unit_rows // tile,),
+        in_specs=[block] * len(parts),
+        out_specs=[block] * 4 + [TOKEN_SPEC],
+        out_shape=[leave, leave, stay, stay, TOKEN],
+        compiler_params=pltpu.CompilerParams(vmem_limit_bytes=VMEM_LIMIT),
+        cost_estimate=BRIEF,
+        name="join",
+    )(*parts)
 
 
 def policy_kernel(blocks_ref, w_gate_ref, w_up_ref, *refs):
@@ -208,18 +237,60 @@
             TOKEN,
         ],
         compiler_params=pltpu.CompilerParams(vmem_limit_bytes=VMEM_LIMIT),
-        cost_estimate=pl.CostEstimate(
-            flops=4 * group_tok * depth * unit_rows,
-            bytes_accessed=unit_rows * (4 * depth + 8 * group_tok),
-            transcendentals=0,
-        ),
+        cost_estimate=BRIEF,
         name="policy_products",
     )(gathered, w_gate, w_up, *after)
 
 
+def grads_kernel(gate_ref, up_ref, readout_ref, token_grad_ref, inputs_ref, *refs):
+    grad_gate_ref, grad_up_ref, token_ref = refs[-3:]
+    mark(token_ref)
+    gate = gate_ref[...]
+    hidden_grad = token_grad_ref[...] * readout_ref[...].astype(jnp.float32)
+    sigma = jax.nn.sigmoid(gate)
+    gate_grad = hidden_grad * up_ref[...] * sigma * (1.0 + gate * (1.0 - sigma))
+    up_grad = hidden_grad * (gate * sigma)
+    contract = (((0,), (0,)), ((), ()))
+    for target_ref, grad in ((grad_gate_ref, gate_grad), (grad_up_ref, up_grad)):
+        target_ref[0] = lax.dot_general(
+            grad.astype(jnp.bfloat16),
+            inputs_ref[...],
+            contract,
+            preferred_element_type=jnp.float32,
+        ).astype(target_ref.dtype)
+
+
+def weight_grads(gate, upper, readout, token_grad, inputs, *after):
+    group_tok, unit_rows = gate.shape
+    depth = inputs.shape[1]
+    tile = tile_of(unit_rows)
+    units = pl.BlockSpec((group_tok, tile), lambda i: (0, i))
+    result = pl.BlockSpec((1, tile, depth), lambda i: (0, i, 0))
+    shape = jax.ShapeDtypeStruct((1, unit_rows, depth), jnp.bfloat16)
+    return pl.pallas_call(
+        grads_kernel,
+        grid=(unit_rows // tile,),
+        in_specs=[
+            units,
+            units,
+            units,
+            pl.BlockSpec((group_tok, 1), lambda i: (0, 0)),
+            pl.BlockSpec(
+                (group_tok, depth), lambda i: (0, 0), pipeline_mode=pl.Buffered(1)
+            ),
+        ]
+        + [STAY] * len(after),
+        out_specs=[result, result, TOKEN_SPEC],
+        out_shape=[shape, shape, TOKEN],
+        compiler_params=pltpu.CompilerParams(vmem_limit_bytes=VMEM_LIMIT),
+        cost_estimate=BRIEF,
+        name="weight_grads",
+    )(gate, upper, readout, token_grad[:, None], inputs, *after)
+
+
 def outer_kernel(groups, strip, me_ref, outer_ref, moment_ref, *refs):
     del me_ref
-    inner = refs[:groups]
+    inner = (refs[0].at[0], *refs[1:groups])
     new_outer_ref, new_moment_ref, token_ref = refs[-3:]
     rows, width = outer_ref.shape
     mark(token_ref)
@@ -247,17 +318,20 @@
     lax.fori_loop(0, rows // strip, step, 0)
 
 
-def outer_update(chunk, chunks, me, outer, moment, near, far, previous, *after):
-    unit_rows, width = outer.shape
-    rows = unit_rows // chunks
-    tile = rows // 2 if rows % 64 == 0 else rows
+def outer_update(first, steps, tile, me, outer, moment, weight, pieces, previous, *after):
+    width = outer.shape[1]
     strip = 32 if tile % 32 == 0 else 16
-    first = chunk * (rows // tile)
-    groups = len(near) + len(far)
+    groups = len(pieces) + 1
     placed = pl.BlockSpec((tile, width), lambda i, me: (first + i, 0))
-    local = pl.BlockSpec((tile, width), lambda i, me: (i, 0))
-    in_specs = [placed] * (2 + len(near)) + [local] * len(far)
-    args = [me, outer, moment, *near, *far]
+    in_specs = [
+        placed,
+        placed,
+        pl.BlockSpec((1, tile, width), lambda i, me: (0, first + i, me[0])),
+    ] + [
+        pl.BlockSpec((tile, width), lambda i, me, skip=first - begin: (skip + i, 0))
+        for _, begin in pieces
+    ]
+    args = [me, outer, moment, weight] + [piece for piece, _ in pieces]
     aliases = {}
     if previous is not None:
         aliases = {len(args): 0, len(args) + 1: 1}
@@ -269,7 +343,7 @@
         functools.partial(outer_kernel, groups, strip),
         grid_spec=pltpu.PrefetchScalarGridSpec(
             num_scalar_prefetch=1,
-            grid=(rows // tile,),
+            grid=(steps,),
             in_specs=in_specs,
             out_specs=[placed, placed, TOKEN_SPEC],
         ),
@@ -279,11 +353,7 @@
             TOKEN,
         ],
         input_output_aliases=aliases,
-        cost_estimate=pl.CostEstimate(
-            flops=rows * width * groups * 12,
-            bytes_accessed=rows * width * (2 * groups + 12),
-            transcendentals=0,
-        ),
+        cost_estimate=BRIEF,
         compiler_params=pltpu.CompilerParams(vmem_limit_bytes=VMEM_LIMIT),
         name="outer_update",
     )(*args)
@@ -299,44 +369,54 @@
     def swap(value, bits):
         return lax.ppermute(value, "rep", [(i, i ^ bits) for i in range(groups)])
 
-    far_masks = tuple(range(2, groups))
-
-    def send(chunk, *after):
-        parts, token = pick(chunk, CHUNKS, place, w_gate, far_masks, width, *after)
-        return [swap(part, bits) for part, bits in zip(parts, far_masks)], token
-
-    far = [None] * CHUNKS
+    tile = outer_gate.shape[0] // sum(CHUNKS)
+    starts = [sum(CHUNKS[:chunk]) for chunk in range(len(CHUNKS))]
+    pieces = [[] for _ in CHUNKS]
     updated = None
+
+    def send(chunks, masks, *after):
+        steps = sum(CHUNKS[chunk] for chunk in chunks)
+        begin = starts[chunks[0]]
+        parts, token = pick(begin, steps, tile, place, w_gate, masks, width, *after)
+        came = [swap(part, bits) for part, bits in zip(parts, masks)]
+        for chunk in chunks:
+            pieces[chunk] += [(piece, begin) for piece in came]
+        return came, token
 
     def update(chunk, *after):
         return outer_update(
-            chunk, CHUNKS, place, outer_gate, moment, near, far[chunk], updated, *after
+            starts[chunk],
+            CHUNKS[chunk],
+            tile,
+            place,
+            outer_gate,
+            moment,
+            w_gate,
+            pieces[chunk],
+            updated,
+            *after,
         )
 
-    shares, token = pick(0, 1, place, tokens[None], tuple(range(1, groups)), width)
+    first, token = send((0,), (2,))
+    shares, token = pick(
+        0, 1, tokens.shape[0], place, tokens[None], tuple(range(1, groups)), width, token
+    )
     others = [swap(share, bits) for bits, share in enumerate(shares, 1)]
-    far[0], token = send(0, token)
-    far[1], token = send(1, token)
-    gathered = lax.all_gather(assemble(place, tokens, others), "fsdp", axis=0, tiled=False)
-    (own, mate), token = pick(0, 1, place, w_gate, (0, 1), width, token)
-    near = [own, swap(mate, 1)]
-
-    updated, token = update(0)
-    far[2], token = send(2, token)
-    updated, token = update(1, token)
-    far[3], token = send(3, token)
-
-    keep, leave, token = partial_products(gathered, outer_gate, outer_up, token)
-    held = keep + swap(leave, 1).astype(jnp.float32)
-    leaving = held[:, 1].astype(jnp.bfloat16)
-    both_ref = held[:, 0] + swap(leaving, 2).astype(jnp.float32)
-    gate_ref, upper_ref = both_ref[0], both_ref[1]
-
-    gate, upper, inputs, token = policy_products(gathered, w_gate, w_up, leaving)
-    updated, token = update(2, token)
-    far[4], token = send(4, token)
-    updated, token = update(3, token)
-    far[5], token = send(5, token)
+    assembled, token = assemble(place, tokens, others, token)
+    gathered = lax.all_gather(assembled, "fsdp", axis=0, tiled=False)
+    _, token = send((0,), (1, 3), token)
+    second, token = send((1,), (2,), token, *first)
+    updated, token = update(0, token)
+
+    *parts, token = partial_products(gathered, outer_gate, outer_up, token)
+    for at in (1, 3, 5, 7):
+        parts[at] = swap(parts[at], 1)
+    leave_gate, leave_up, stay_gate, stay_up, token = join(parts)
+    gate_ref = stay_gate + swap(leave_gate, 2).astype(jnp.float32)
+    upper_ref = stay_up + swap(leave_up, 2).astype(jnp.float32)
+    _, token = send((1,), (1, 3), token)
+    third, token = send((2,), (2,), token, *second)
+    gate, upper, inputs, token = policy_products(gathered, w_gate, w_up, token)
 
     group_tok = inputs.shape[0]
     seqs = group_tok // LEN
@@ -364,24 +444,16 @@
     weight = dpo_beta * jax.nn.sigmoid(-margin) / pick_chosen.shape[0]
     coef = jnp.dot(weight, pick_rejected - pick_chosen, precision=highest)
     token_grad = jnp.broadcast_to(coef[:, None], (seqs, LEN)).reshape(-1) * mask_f
-    hidden_grad = token_grad[:, None] * readout.astype(jnp.float32)
-    sigma = jax.nn.sigmoid(gate)
-    gate_grad = (hidden_grad * upper * sigma * (1.0 + gate * (1.0 - sigma))).astype(jnp.bfloat16)
-    up_grad = (hidden_grad * jax.nn.silu(gate)).astype(jnp.bfloat16)
-    contract = (((0,), (0,)), ((), ()))
-    grad_gate = lax.dot_general(
-        gate_grad, inputs, contract, preferred_element_type=jnp.float32
-    ).astype(jnp.bfloat16)
-    grad_up = lax.dot_general(up_grad, inputs, contract, preferred_element_type=jnp.float32).astype(
-        jnp.bfloat16
-    )
-
-    updated, token = update(4, token, grad_gate)
-    far[6], token = send(6, token)
-    updated, token = update(5, token, grad_up)
-    updated, token = update(6, token)
+    grad_gate, grad_up, token = weight_grads(gate, upper, readout, token_grad, inputs, token)
+    _, token = send((2,), (1, 3), token)
+    updated, token = update(1, token)
+    _, token = send((3,), (1, 2, 3), token)
+    updated, token = update(2, token)
+    _, token = send((4,), (1, 2, 3), token)
+    updated, token = update(3, token)
+    updated, token = update(4, token)
     new_outer, new_moment = updated
-    return (loss, grad_gate[None], grad_up[None], new_outer, new_moment)
+    return (loss, grad_gate, grad_up, new_outer, new_moment)
 
 
 def solution(mesh):

time: 250 us -> 218 us (0.87)
  waiting for transfers between devices: 95.1 us -> 61.3 us
  Pallas kernels: 84.2 us -> 103 us
  matrix products: 16.6 us -> 1.19 us
    ppermute x20 -> x24, waiting for transfers between devices: 89.5 us -> 55.1 us  [swap(): return lax.ppermute(value, 'rep', [(i, i ^ bits) for i in range(groups)])]
    pallas_call x0 -> x2, Pallas kernels: none -> 18.9 us  [the longest x1 12.7 us: weight_grads(): pl.pallas_call(grads_kernel, grid=(unit_rows // tile,), in_specs=[units,...]
    dot_general x2 -> x0, matrix products: 15.4 us -> none  [the longest x1 7.72 us: per_device(): lax.dot_general(gate_grad, inputs, contract, preferred_element_type=jnp.f...]
    pallas_call x7 -> x5, Pallas kernels: 30.3 us -> 28.5 us  [outer_update(): pl.pallas_call(functools.partial(outer_kernel, groups, strip), grid_spec=...]
    unnamed x50 -> x46, local copies, waits for them, and re-layouts: 6.35 us -> 6 us
    ppermute x20 -> x24, starting transfers between devices: 18.5 us -> 18.5 us  [swap(): return lax.ppermute(value, 'rep', [(i, i ^ bits) for i in range(groups)])]
  transfers between devices with their start and end apart: 24 -> 28, of which waited for: 14 -> 16; matrix products, arithmetic and copies ran while one was open for 8% -> 3% of each run, Pallas kernels for 27% -> 43%
where the time goes in v4:
time: 218 us; the launch traced here: 216 us
  Pallas kernels  103 us (47%)
  waiting for transfers between devices  61.3 us (28%)
  starting transfers between devices  23.9 us (11%)
  between operations  16 us (7%)
  local copies, waits for them, and re-layouts  7.25 us (3%)
  other arithmetic  3.03 us (1%)
    ppermute x24, waiting for transfers between devices, swap(): return lax.ppermute(value, 'rep', [(i, i ^ bits) for i in range(groups)])  55.1 us
    pallas_call x5, Pallas kernels, outer_update(): pl.pallas_call(functools.partial(outer_kernel, groups, strip), grid_spec=...  28.5 us
    pallas_call x9, Pallas kernels, pick(): pl.pallas_call(functools.partial(pick_kernel, count), grid_spec=pltpu.Pre...  27.6 us
    ppermute x24, starting transfers between devices, swap(): return lax.ppermute(value, 'rep', [(i, i ^ bits) for i in range(groups)])  18.5 us
    pallas_call x1, Pallas kernels, policy_products(): pl.pallas_call(policy_kernel, grid=(unit_rows // tile,), in_specs=[pl.Blo...  16.6 us
    pallas_call x1, Pallas kernels, weight_grads(): pl.pallas_call(grads_kernel, grid=(unit_rows // tile,), in_specs=[units,...  12.7 us
    pallas_call x1, Pallas kernels, partial_products(): pl.pallas_call(partial_kernel, grid=(unit_rows // tile,), in_specs=[pl.Bl...  9.94 us
    pallas_call x1, Pallas kernels, join(): pl.pallas_call(join_kernel, grid=(unit_rows // tile,), in_specs=[block] *...  6.19 us
  transfers between devices with their start and end apart: 28, of which 16 were waited for; matrix products, arithmetic and copies ran while one was open for 3% of the time, Pallas kernels for 43%

profile of v4, /device:TPU:0, one launch (start us, length us, event | category | flops | bytes accessed | tf_op | source)
XLA Modules:
  0.0 215.8 jit_solution(14703309338494879768)
XLA Ops:
  7.2 3.4 %pick.9 = (bf16[512,1024]{1,0:T(8,128)(2,1)}, f32[8,128]{1,0:T(8,128)}) custom-call(s32[1]{0:T(128)} %bitcast.1.me_ref, bf16[1,1792,4096]{2,1,0:T(8,128)(2,1)} %refs_0_.25), custom_call_target="tpu_custom_call" | custom-call | flops 1 | bytes 1 | tf_op jit(solution)/shard_map/pick/pallas_call | solution.py:57
  12.5 2.5 %collective-permute-start.1 = (bf16[16,1024]{1,0:T(8,128)(2,1)}, bf16[16,1024]{1,0:T(8,128)(2,1)S(1)}, u32[]{:S(2)}, u32[]{:S(2)}) collective-permute-start(bf16[16,1024]{1,0:T(8,128)(2,1)} %get-tuple-element.70), channel_id=1, source_target_pairs={{0,16},{8,24},{16,0},{24,8},{1,17},{9,25},{17,1},{25,9},{2,18},{10... | collective-permute-start | bytes 98312 | tf_op jit(solution)/shard_map/ppermute | solution.py:370
  15.1 2.1 collective-permute-done.1.refs_1_
  19.1 1.6 assemble.1
  21.7 3.8 %pick.11 = (bf16[512,1024]{1,0:T(8,128)(2,1)}, bf16[512,1024]{1,0:T(8,128)(2,1)}, f32[8,128]{1,0:T(8,128)}) custom-call(s32[1]{0:T(128)} %bitcast.1.me_ref, bf16[1,1792,4096]{2,1,0:T(8,128)(2,1)} %refs_0_.25, bf16[1,1792,4096]{2,1,0:T(8,128)(2,1)} %refs_0_.25, f32[8,128]{1,0:T(8,128)} %get-tuple-element.75.refs_2_), custom_call_target="tpu_custom_call" | custom-call | flops 1 | bytes 1 | tf_op jit(solution)/shard_map/pick/pallas_call | solution.py:57
  26.8 20.3 %collective-permute-done.3.refs_2_.refs_1_ = bf16[512,1024]{1,0:T(8,128)(2,1)S(1)} collective-permute-done((bf16[512,1024]{1,0:T(8,128)(2,1)}, bf16[512,1024]{1,0:T(8,128)(2,1)S(1)}, u32[]{:S(2)}, u32[]{:S(2)}) %collective-permute-start.3) | collective-permute-done | bytes 1048608 | tf_op jit(solution)/shard_map/ppermute | solution.py:370
  48.0 4.0 %pick.12 = (bf16[640,1024]{1,0:T(8,128)(2,1)}, f32[8,128]{1,0:T(8,128)}) custom-call(s32[1]{0:T(128)} %bitcast.1.me_ref, bf16[1,1792,4096]{2,1,0:T(8,128)(2,1)} %refs_0_.25, f32[8,128]{1,0:T(8,128)} %get-tuple-element.78.refs_1_, bf16[512,1024]{1,0:T(8,128)(2,1)} %copy-done.1), custom_call_target="tpu_custom_call" | custom-call | flops 1 | bytes 1 | tf_op jit(solution)/shard_map/pick/pallas_call | solution.py:57
  52.9 15.4 %collective-permute-done.5.refs_3_ = bf16[512,1024]{1,0:T(8,128)(2,1)} collective-permute-done((bf16[512,1024]{1,0:T(8,128)(2,1)}, bf16[512,1024]{1,0:T(8,128)(2,1)}, u32[]{:S(2)}, u32[]{:S(2)}) %collective-permute-start.5) | collective-permute-done | bytes 1048608 | tf_op jit(solution)/shard_map/ppermute | solution.py:370
  68.3 7.2 %outer_update.5 = (bf16[1792,1024]{1,0:T(8,128)(2,1)}, f32[1792,1024]{1,0:T(8,128)}, f32[8,128]{1,0:T(8,128)}) custom-call(s32[1]{0:T(128)} %bitcast.1.me_ref, bf16[1792,1024]{1,0:T(8,128)(2,1)} %outer_ref.9, f32[1792,1024]{1,0:T(8,128)} %moment_ref.9, bf16[1,1792,4096]{2,1,0:T(8,128)(2,1)} %refs_0_.25, bf16[512,1024]{1,0:T(8,128)(2,1)} %copy-done.1, ...), custom_call_target="tpu_custom_call" | custom-call | flops 1 | bytes 1 | tf_op jit(solution)/shard_map/outer_update/pallas_call | solution.py:342
  75.5 9.9 %partial_products.1 = (f32[128,1792]{1,0:T(8,128)}, bf16[128,1792]{1,0:T(8,128)(2,1)}, f32[128,1792]{1,0:T(8,128)}, bf16[128,1792]{1,0:T(8,128)(2,1)}, f32[128,1...) custom-call(bf16[8,8,16,1024]{3,2,1,0:T(8,128)(2,1)} %bitcast.28, ...), custom_call_target="tpu_custom_call" | custom-call | flops 1 | bytes 1 | tf_op jit(solution)/shard_map/partial_products/pallas_call | solution.py:136
  85.4 1.6 collective-permute-start.6
  91.4 6.2 %join.1 = (bf16[128,1792]{1,0:T(8,128)(2,1)}, bf16[128,1792]{1,0:T(8,128)(2,1)}, f32[128,1792]{1,0:T(8,128)}, f32[128,1792]{1,0:T(8,128)}, f32[8,128]{1,0:T(8,128)}) custom-call(f32[128,1792]{1,0:T(8,128)} %get-tuple-element.81.refs_0_, bf16[128,1792]{1,0:T(8,128)(2,1)} %copy-done.8, f32[128,1792]{1,0:T(8,128)} %get-tuple-element.83.refs_2_, ...), custom_call_target="tpu_custom_call" | custom-call | flops 1 | bytes 1 | tf_op jit(solution)/shard_map/join/pallas_call | solution.py:182
  99.9 4.7 %pick.13 = (bf16[640,1024]{1,0:T(8,128)(2,1)}, bf16[640,1024]{1,0:T(8,128)(2,1)}, f32[8,128]{1,0:T(8,128)}) custom-call(s32[1]{0:T(128)} %bitcast.1.me_ref, bf16[1,1792,4096]{2,1,0:T(8,128)(2,1)} %refs_0_.25, bf16[1,1792,4096]{2,1,0:T(8,128)(2,1)} %refs_0_.25, f32[8,128]{1,0:T(8,128)} %get-tuple-element.89.refs_2_), custom_call_target="tpu_custom_call" | custom-call | flops 1 | bytes 1 | tf_op jit(solution)/shard_map/pick/pallas_call | solution.py:57
  105.6 2.9 %pick.14 = (bf16[384,1024]{1,0:T(8,128)(2,1)}, f32[8,128]{1,0:T(8,128)}) custom-call(s32[1]{0:T(128)} %bitcast.1.me_ref, bf16[1,1792,4096]{2,1,0:T(8,128)(2,1)} %refs_0_.25, f32[8,128]{1,0:T(8,128)} %get-tuple-element.90.refs_1_, bf16[640,1024]{1,0:T(8,128)(2,1)} %copy-done), custom_call_target="tpu_custom_call" | custom-call | flops 1 | bytes 1 | tf_op jit(solution)/shard_map/pick/pallas_call | solution.py:57
  110.6 16.6 %policy_products.1 = (f32[128,1792]{1,0:T(8,128)}, f32[128,1792]{1,0:T(8,128)}, bf16[128,4096]{1,0:T(8,128)(2,1)}, f32[8,128]{1,0:T(8,128)}) custom-call(bf16[8,8,16,1024]{3,2,1,0:T(8,128)(2,1)} %bitcast.29, bf16[1,1792,4096]{2,1,0:T(8,128)(2,1)} %refs_0_.25, bf16[1,1792,4096]{2,1,0:T(8,128)(2,1)} %w_up_ref.1, f32[8,128]{1,0:T(8,128)} %get-tuple-element.92.refs_0_), custom_call_target="tpu_custom_call" | custom-call | flops 1 | bytes 1 | tf_op jit(solution)/shard_map/policy_products/pallas_call | solution.py:219
  127.3 2.8 %fusion.3 = (f32[128]{0:T(128)S(1)}, f32[128]{0:T(128)S(1)}) fusion(bf16[128,1792]{1,0:T(8,128)(2,1)S(1)} %copy-done.2, f32[128,1792]{1,0:T(8,128)} %get-tuple-element.97, bf16[128,1792]{1,0:T(8,128)(2,1)} %collective-permute-done.12, f32[128,1792]{1,0:T(8,128)S(1)} %copy-done.6, bf16[128,1792]{1,0:T(8,128)(2,1)} %collective-permute-done.11, ...), kind=kLoop, calls=%fused_computation.8 | loop fusion | flops 5275392 | bytes 5047296 | tf_op jit(solution)/shard_map/reduce_sum | solution.py:29
  132.0 2.0 collective-permute-done.13
  135.3 2.3 %collective-permute-done.14 = f32[8]{0:T(128)S(1)} collective-permute-done((f32[8]{0:T(128)S(1)}, f32[8]{0:T(128)S(1)}, u32[]{:S(2)}, u32[]{:S(2)}) %collective-permute-start.14) | collective-permute-done | bytes 64 | tf_op jit(solution)/shard_map/ppermute | solution.py:431
  137.6 2.6 %collective-permute-start.15 = (f32[8]{0:T(128)S(1)}, f32[8]{0:T(128)S(1)}, u32[]{:S(2)}, u32[]{:S(2)}) collective-permute-start(f32[8]{0:T(128)S(1)} %add.34), channel_id=1, source_target_pairs={{0,4},{1,5},{2,6},{3,7},{4,0},{5,1},{6,2},{7,3},{8,12},{9,13},{10,... | collective-permute-start | bytes 104 | tf_op jit(solution)/shard_map/ppermute | solution.py:431
  140.2 1.8 collective-permute-done.15
  144.2 12.7 %weight_grads.1 = (bf16[1,1792,4096]{2,1,0:T(8,128)(2,1)}, bf16[1,1792,4096]{2,1,0:T(8,128)(2,1)}, f32[8,128]{1,0:T(8,128)}) custom-call(f32[128,1792]{1,0:T(8,128)} %get-tuple-element.93.gate_ref, f32[128,1792]{1,0:T(8,128)} %get-tuple-element.94.up_ref, bf16[128,1792]{1,0:T(8,128)(2,1)} %readout_ref.1, f32[128,1]{1,0:T(8,128)} %copy.23.token_grad_ref, ...), custom_call_target="tpu_custom_call" | custom-call | flops 1 | bytes 1 | tf_op jit(solution)/shard_map/weight_grads/pallas_call | solution.py:270
  156.9 3.4 %pick.15 = (bf16[384,1024]{1,0:T(8,128)(2,1)}, bf16[384,1024]{1,0:T(8,128)(2,1)}, f32[8,128]{1,0:T(8,128)}) custom-call(s32[1]{0:T(128)} %bitcast.1.me_ref, bf16[1,1792,4096]{2,1,0:T(8,128)(2,1)} %refs_0_.25, bf16[1,1792,4096]{2,1,0:T(8,128)(2,1)} %refs_0_.25, f32[8,128]{1,0:T(8,128)} %get-tuple-element.104.refs_2_), custom_call_target="tpu_custom_call" | custom-call | flops 1 | bytes 1 | tf_op jit(solution)/shard_map/pick/pallas_call | solution.py:57
  161.2 3.6 %collective-permute-done.20.refs_3_ = bf16[640,1024]{1,0:T(8,128)(2,1)S(1)} collective-permute-done((bf16[640,1024]{1,0:T(8,128)(2,1)}, bf16[640,1024]{1,0:T(8,128)(2,1)S(1)}, u32[]{:S(2)}, u32[]{:S(2)}) %collective-permute-start.20) | collective-permute-done | bytes 1310752 | tf_op jit(solution)/shard_map/ppermute | solution.py:370
  165.9 8.7 %outer_update.6 = (bf16[1792,1024]{1,0:T(8,128)(2,1)}, f32[1792,1024]{1,0:T(8,128)}, f32[8,128]{1,0:T(8,128)}) custom-call(s32[1]{0:T(128)} %bitcast.1.me_ref, bf16[1792,1024]{1,0:T(8,128)(2,1)} %outer_ref.9, f32[1792,1024]{1,0:T(8,128)} %moment_ref.9, bf16[1,1792,4096]{2,1,0:T(8,128)(2,1)} %refs_0_.25, ...), custom_call_target="tpu_custom_call", output_to_operand_aliasing={{0}: (7, {}), {1}: (8, {})} | custom-call | flops 1 | bytes 1 | tf_op jit(solution)/shard_map/outer_update/pallas_call | solution.py:342
  174.7 2.1 pick.16
  179.5 2.4 %collective-permute-done.18.refs_3_ = bf16[384,1024]{1,0:T(8,128)(2,1)} collective-permute-done((bf16[384,1024]{1,0:T(8,128)(2,1)}, bf16[384,1024]{1,0:T(8,128)(2,1)}, u32[]{:S(2)}, u32[]{:S(2)}) %collective-permute-start.18) | collective-permute-done | bytes 786464 | tf_op jit(solution)/shard_map/ppermute | solution.py:370
  181.8 6.0 %outer_update.7 = (bf16[1792,1024]{1,0:T(8,128)(2,1)}, f32[1792,1024]{1,0:T(8,128)}, f32[8,128]{1,0:T(8,128)}) custom-call(s32[1]{0:T(128)} %bitcast.1.me_ref, bf16[1792,1024]{1,0:T(8,128)(2,1)} %outer_ref.9, f32[1792,1024]{1,0:T(8,128)} %moment_ref.9, bf16[1,1792,4096]{2,1,0:T(8,128)(2,1)} %refs_0_.25, ...), custom_call_target="tpu_custom_call", output_to_operand_aliasing={{0}: (7, {}), {1}: (8, {})} | custom-call | flops 1 | bytes 1 | tf_op jit(solution)/shard_map/outer_update/pallas_call | solution.py:342
  187.8 2.0 pick.17
  193.7 3.3 %outer_update.8 = (bf16[1792,1024]{1,0:T(8,128)(2,1)}, f32[1792,1024]{1,0:T(8,128)}, f32[8,128]{1,0:T(8,128)}) custom-call(s32[1]{0:T(128)} %bitcast.1.me_ref, bf16[1792,1024]{1,0:T(8,128)(2,1)} %outer_ref.9, f32[1792,1024]{1,0:T(8,128)} %moment_ref.9, bf16[1,1792,4096]{2,1,0:T(8,128)(2,1)} %refs_0_.25, ...), custom_call_target="tpu_custom_call", output_to_operand_aliasing={{0}: (7, {}), {1}: (8, {})} | custom-call | flops 1 | bytes 1 | tf_op jit(solution)/shard_map/outer_update/pallas_call | solution.py:342
  196.9 3.2 %collective-permute-done.22.refs_2_ = bf16[128,1024]{1,0:T(8,128)(2,1)S(1)} collective-permute-done((bf16[128,1024]{1,0:T(8,128)(2,1)}, bf16[128,1024]{1,0:T(8,128)(2,1)S(1)}, u32[]{:S(2)}, u32[]{:S(2)}) %collective-permute-start.22) | collective-permute-done | bytes 262176 | tf_op jit(solution)/shard_map/ppermute | solution.py:370
  200.2 3.7 %collective-permute-done.23.refs_3_ = bf16[128,1024]{1,0:T(8,128)(2,1)S(1)} collective-permute-done((bf16[128,1024]{1,0:T(8,128)(2,1)}, bf16[128,1024]{1,0:T(8,128)(2,1)S(1)}, u32[]{:S(2)}, u32[]{:S(2)}) %collective-permute-start.23) | collective-permute-done | bytes 262176 | tf_op jit(solution)/shard_map/ppermute | solution.py:370
  204.6 3.3 %outer_update.9 = (bf16[1792,1024]{1,0:T(8,128)(2,1)}, f32[1792,1024]{1,0:T(8,128)}, f32[8,128]{1,0:T(8,128)}) custom-call(s32[1]{0:T(128)} %bitcast.1.me_ref, bf16[1792,1024]{1,0:T(8,128)(2,1)} %outer_ref.9, f32[1792,1024]{1,0:T(8,128)} %moment_ref.9, bf16[1,1792,4096]{2,1,0:T(8,128)(2,1)} %refs_0_.25, ...), custom_call_target="tpu_custom_call", output_to_operand_aliasing={{0}: (7, {}), {1}: (8, {})} | custom-call | flops 1 | bytes 1 | tf_op jit(solution)/shard_map/outer_update/pallas_call | solution.py:342
  (108 shorter events, 31.9 us)
Async XLA Ops:
  7.2 68.3 %all-gather.3.cloned.1.call-start = ((), (), s32[]{:S(2)}) async-start(), calls=%async_computation | async-start | bytes 2359296 | tf_op jit(solution)/shard_map/all_gather | solution.py:406
  12.0 3.1 %collective-permute-start = (bf16[16,1024]{1,0:T(8,128)(2,1)}, bf16[16,1024]{1,0:T(8,128)(2,1)S(1)}, u32[]{:S(2)}, u32[]{:S(2)}) collective-permute-start(bf16[16,1024]{1,0:T(8,128)(2,1)} %get-tuple-element.69), channel_id=1, source_target_pairs={{0,8},{8,0},{16,24},{24,16},{1,9},{9,1},{17,25},{25,17},{2,10},{10... | collective-permute-start | bytes 98312 | tf_op jit(solution)/shard_map/ppermute | solution.py:370
  12.5 4.8 %collective-permute-start.1 = (bf16[16,1024]{1,0:T(8,128)(2,1)}, bf16[16,1024]{1,0:T(8,128)(2,1)S(1)}, u32[]{:S(2)}, u32[]{:S(2)}) collective-permute-start(bf16[16,1024]{1,0:T(8,128)(2,1)} %get-tuple-element.70), channel_id=1, source_target_pairs={{0,16},{8,24},{16,0},{24,8},{1,17},{9,25},{17,1},{25,9},{2,18},{10... | collective-permute-start | bytes 98312 | tf_op jit(solution)/shard_map/ppermute | solution.py:370
  15.0 3.6 %collective-permute-start.2 = (bf16[16,1024]{1,0:T(8,128)(2,1)}, bf16[16,1024]{1,0:T(8,128)(2,1)S(1)}, u32[]{:S(2)}, u32[]{:S(2)}) collective-permute-start(bf16[16,1024]{1,0:T(8,128)(2,1)} %get-tuple-element.71), channel_id=1, source_target_pairs={{0,24},{8,16},{16,8},{24,0},{1,25},{9,17},{17,9},{25,1},{2,26},{10... | collective-permute-start | bytes 98312 | tf_op jit(solution)/shard_map/ppermute | solution.py:370
  20.8 26.3 %collective-permute-start.3 = (bf16[512,1024]{1,0:T(8,128)(2,1)}, bf16[512,1024]{1,0:T(8,128)(2,1)S(1)}, u32[]{:S(2)}, u32[]{:S(2)}) collective-permute-start(bf16[512,1024]{1,0:T(8,128)(2,1)} %get-tuple-element.74), channel_id=1, source_target_pairs={{0,16},{8,24},{16,0},{24,8},{1,17},{9,25},{17,1},{25,9},{2,18},{10... | collective-permute-start | bytes 3145736 | tf_op jit(solution)/shard_map/ppermute | solution.py:370
  25.5 27.4 %collective-permute-start.4 = (bf16[512,1024]{1,0:T(8,128)(2,1)}, bf16[512,1024]{1,0:T(8,128)(2,1)S(1)}, u32[]{:S(2)}, u32[]{:S(2)}) collective-permute-start(bf16[512,1024]{1,0:T(8,128)(2,1)} %get-tuple-element.76), channel_id=1, source_target_pairs={{0,8},{8,0},{16,24},{24,16},{1,9},{9,1},{17,25},{25,17},{2,10},{10... | collective-permute-start | bytes 3145736 | tf_op jit(solution)/shard_map/ppermute | solution.py:370
  25.5 42.8 %collective-permute-start.5 = (bf16[512,1024]{1,0:T(8,128)(2,1)}, bf16[512,1024]{1,0:T(8,128)(2,1)}, u32[]{:S(2)}, u32[]{:S(2)}) collective-permute-start(bf16[512,1024]{1,0:T(8,128)(2,1)} %get-tuple-element.77), channel_id=1, source_target_pairs={{0,24},{8,16},{16,8},{24,0},{1,25},{9,17},{17,9},{25,1},{2,26},{10... | collective-permute-start | bytes 3145736 | tf_op jit(solution)/shard_map/ppermute | solution.py:370
  52.0 52.5 %collective-permute-start.10 = (bf16[640,1024]{1,0:T(8,128)(2,1)}, bf16[640,1024]{1,0:T(8,128)(2,1)S(1)}, u32[]{:S(2)}, u32[]{:S(2)}) collective-permute-start(bf16[640,1024]{1,0:T(8,128)(2,1)} %get-tuple-element.91), channel_id=1, source_target_pairs={{0,16},{8,24},{16,0},{24,8},{1,17},{9,25},{17,1},{25,9},{2,18},{10... | collective-permute-start | bytes 3932168 | tf_op jit(solution)/shard_map/ppermute | solution.py:370
  52.9 15.4 %copy-start.5 = (bf16[512,1024]{1,0:T(8,128)(2,1)}, bf16[512,1024]{1,0:T(8,128)(2,1)S(1)}, u32[]{:S(2)}) copy-start(bf16[512,1024]{1,0:T(8,128)(2,1)S(1)} %collective-permute-done.4.refs_2_) | copy-start | bytes 3145732
  85.4 14.3 %copy-start.22 = (s32[1,8]{1,0:T(1,128)S(1)}, s32[1,8]{1,0:T(1,128)}, u32[]{:S(2)}) copy-start(s32[1,8]{1,0:T(1,128)} %param.12) | copy-start | bytes 100
  85.4 3.2 %collective-permute-start.6 = (bf16[128,1792]{1,0:T(8,128)(2,1)}, bf16[128,1792]{1,0:T(8,128)(2,1)S(1)}, u32[]{:S(2)}, u32[]{:S(2)}) collective-permute-start(bf16[128,1792]{1,0:T(8,128)(2,1)} %get-tuple-element.82), channel_id=1, source_target_pairs={{0,8},{8,0},{16,24},{24,16},{1,9},{9,1},{17,25},{25,17},{2,10},{10... | collective-permute-start | bytes 1376264 | tf_op jit(solution)/shard_map/ppermute | solution.py:370
  87.0 2.3 %collective-permute-start.7 = (bf16[128,1792]{1,0:T(8,128)(2,1)}, bf16[128,1792]{1,0:T(8,128)(2,1)S(1)}, u32[]{:S(2)}, u32[]{:S(2)}) collective-permute-start(bf16[128,1792]{1,0:T(8,128)(2,1)} %get-tuple-element.84), channel_id=1, source_target_pairs={{0,8},{8,0},{16,24},{24,16},{1,9},{9,1},{17,25},{25,17},{2,10},{10... | collective-permute-start | bytes 1376264 | tf_op jit(solution)/shard_map/ppermute | solution.py:370
  87.0 2.9 %collective-permute-start.8 = (bf16[128,1792]{1,0:T(8,128)(2,1)}, bf16[128,1792]{1,0:T(8,128)(2,1)S(1)}, u32[]{:S(2)}, u32[]{:S(2)}) collective-permute-start(bf16[128,1792]{1,0:T(8,128)(2,1)} %get-tuple-element.86), channel_id=1, source_target_pairs={{0,8},{8,0},{16,24},{24,16},{1,9},{9,1},{17,25},{25,17},{2,10},{10... | collective-permute-start | bytes 1376264 | tf_op jit(solution)/shard_map/ppermute | solution.py:370
  87.5 3.1 %collective-permute-start.9 = (bf16[128,1792]{1,0:T(8,128)(2,1)}, bf16[128,1792]{1,0:T(8,128)(2,1)S(1)}, u32[]{:S(2)}, u32[]{:S(2)}) collective-permute-start(bf16[128,1792]{1,0:T(8,128)(2,1)} %get-tuple-element.88), channel_id=1, source_target_pairs={{0,8},{8,0},{16,24},{24,16},{1,9},{9,1},{17,25},{25,17},{2,10},{10... | collective-permute-start | bytes 1376264 | tf_op jit(solution)/shard_map/ppermute | solution.py:370
  97.6 29.7 %collective-permute-start.12 = (bf16[128,1792]{1,0:T(8,128)(2,1)}, bf16[128,1792]{1,0:T(8,128)(2,1)}, u32[]{:S(2)}, u32[]{:S(2)}) collective-permute-start(bf16[128,1792]{1,0:T(8,128)(2,1)} %get-tuple-element.98), channel_id=1, source_target_pairs={{0,16},{8,24},{16,0},{24,8},{1,17},{9,25},{17,1},{25,9},{2,18},{10... | collective-permute-start | bytes 1376264 | tf_op jit(solution)/shard_map/ppermute | solution.py:370
  98.5 28.7 %collective-permute-start.11 = (bf16[128,1792]{1,0:T(8,128)(2,1)}, bf16[128,1792]{1,0:T(8,128)(2,1)}, u32[]{:S(2)}, u32[]{:S(2)}) collective-permute-start(bf16[128,1792]{1,0:T(8,128)(2,1)} %get-tuple-element.96), channel_id=1, source_target_pairs={{0,16},{8,24},{16,0},{24,8},{1,17},{9,25},{17,1},{25,9},{2,18},{10... | collective-permute-start | bytes 1376264 | tf_op jit(solution)/shard_map/ppermute | solution.py:370
  108.5 70.5 %collective-permute-start.16 = (bf16[384,1024]{1,0:T(8,128)(2,1)}, bf16[384,1024]{1,0:T(8,128)(2,1)}, u32[]{:S(2)}, u32[]{:S(2)}) collective-permute-start(bf16[384,1024]{1,0:T(8,128)(2,1)} %get-tuple-element.103), channel_id=1, source_target_pairs={{0,16},{8,24},{16,0},{24,8},{1,17},{9,25},{17,1},{25,9},{2,18},{10... | collective-permute-start | bytes 2359304 | tf_op jit(solution)/shard_map/ppermute | solution.py:370
  109.3 51.9 %collective-permute-start.19 = (bf16[640,1024]{1,0:T(8,128)(2,1)}, bf16[640,1024]{1,0:T(8,128)(2,1)S(1)}, u32[]{:S(2)}, u32[]{:S(2)}) collective-permute-start(bf16[640,1024]{1,0:T(8,128)(2,1)} %get-tuple-element.107), channel_id=1, source_target_pairs={{0,8},{8,0},{16,24},{24,16},{1,9},{9,1},{17,25},{25,17},{2,10},{10... | collective-permute-start | bytes 3932168 | tf_op jit(solution)/shard_map/ppermute | solution.py:370
  109.3 55.5 %collective-permute-start.20 = (bf16[640,1024]{1,0:T(8,128)(2,1)}, bf16[640,1024]{1,0:T(8,128)(2,1)S(1)}, u32[]{:S(2)}, u32[]{:S(2)}) collective-permute-start(bf16[640,1024]{1,0:T(8,128)(2,1)} %get-tuple-element.108), channel_id=1, source_target_pairs={{0,24},{8,16},{16,8},{24,0},{1,25},{9,17},{17,9},{25,1},{2,26},{10... | collective-permute-start | bytes 3932168 | tf_op jit(solution)/shard_map/ppermute | solution.py:370
  110.6 16.6 %copy-start.2 = (bf16[128,1792]{1,0:T(8,128)(2,1)S(1)}, bf16[128,1792]{1,0:T(8,128)(2,1)}, u32[]{:S(2)}) copy-start(bf16[128,1792]{1,0:T(8,128)(2,1)} %readout_ref.1) | copy-start | bytes 1376260
  110.6 16.6 %copy-start.6 = (f32[128,1792]{1,0:T(8,128)S(1)}, f32[128,1792]{1,0:T(8,128)}, u32[]{:S(2)}) copy-start(f32[128,1792]{1,0:T(8,128)} %get-tuple-element.95) | copy-start | bytes 2752516
  130.4 3.6 %collective-permute-start.13 = (f32[8]{0:T(128)S(1)}, f32[8]{0:T(128)S(1)}, u32[]{:S(2)}, u32[]{:S(2)}) collective-permute-start(f32[8]{0:T(128)S(1)} %sub.9), channel_id=1, source_target_pairs={{0,1},{1,0},{2,3},{3,2},{4,5},{5,4},{6,7},{7,6},{8,9},{9,8},{10,11... | collective-permute-start | bytes 104 | tf_op jit(solution)/shard_map/ppermute | solution.py:431
  134.1 3.5 %collective-permute-start.14 = (f32[8]{0:T(128)S(1)}, f32[8]{0:T(128)S(1)}, u32[]{:S(2)}, u32[]{:S(2)}) collective-permute-start(f32[8]{0:T(128)S(1)} %add.33), channel_id=1, source_target_pairs={{0,2},{1,3},{2,0},{3,1},{4,6},{5,7},{6,4},{7,5},{8,10},{9,11},{10,... | collective-permute-start | bytes 104 | tf_op jit(solution)/shard_map/ppermute | solution.py:431
  137.6 4.4 %collective-permute-start.15 = (f32[8]{0:T(128)S(1)}, f32[8]{0:T(128)S(1)}, u32[]{:S(2)}, u32[]{:S(2)}) collective-permute-start(f32[8]{0:T(128)S(1)} %add.34), channel_id=1, source_target_pairs={{0,4},{1,5},{2,6},{3,7},{4,0},{5,1},{6,2},{7,3},{8,12},{9,13},{10,... | collective-permute-start | bytes 104 | tf_op jit(solution)/shard_map/ppermute | solution.py:431
  160.2 19.2 %collective-permute-start.17 = (bf16[384,1024]{1,0:T(8,128)(2,1)}, bf16[384,1024]{1,0:T(8,128)(2,1)S(1)}, u32[]{:S(2)}, u32[]{:S(2)}) collective-permute-start(bf16[384,1024]{1,0:T(8,128)(2,1)} %get-tuple-element.105), channel_id=1, source_target_pairs={{0,8},{8,0},{16,24},{24,16},{1,9},{9,1},{17,25},{25,17},{2,10},{10... | collective-permute-start | bytes 2359304 | tf_op jit(solution)/shard_map/ppermute | solution.py:370
  160.3 21.6 %collective-permute-start.18 = (bf16[384,1024]{1,0:T(8,128)(2,1)}, bf16[384,1024]{1,0:T(8,128)(2,1)}, u32[]{:S(2)}, u32[]{:S(2)}) collective-permute-start(bf16[384,1024]{1,0:T(8,128)(2,1)} %get-tuple-element.106), channel_id=1, source_target_pairs={{0,24},{8,16},{16,8},{24,0},{1,25},{9,17},{17,9},{25,1},{2,26},{10... | collective-permute-start | bytes 2359304 | tf_op jit(solution)/shard_map/ppermute | solution.py:370
  176.8 14.9 %collective-permute-start.24 = (bf16[128,1024]{1,0:T(8,128)(2,1)}, bf16[128,1024]{1,0:T(8,128)(2,1)S(1)}, u32[]{:S(2)}, u32[]{:S(2)}) collective-permute-start(bf16[128,1024]{1,0:T(8,128)(2,1)} %get-tuple-element.120), channel_id=1, source_target_pairs={{0,8},{8,0},{16,24},{24,16},{1,9},{9,1},{17,25},{25,17},{2,10},{10... | collective-permute-start | bytes 786440 | tf_op jit(solution)/shard_map/ppermute | solution.py:370
  178.1 14.7 %collective-permute-start.25 = (bf16[128,1024]{1,0:T(8,128)(2,1)}, bf16[128,1024]{1,0:T(8,128)(2,1)S(1)}, u32[]{:S(2)}, u32[]{:S(2)}) collective-permute-start(bf16[128,1024]{1,0:T(8,128)(2,1)} %get-tuple-element.121), channel_id=1, source_target_pairs={{0,16},{8,24},{16,0},{24,8},{1,17},{9,25},{17,1},{25,9},{2,18},{10... | collective-permute-start | bytes 786440 | tf_op jit(solution)/shard_map/ppermute | solution.py:370
  178.9 14.0 %collective-permute-start.26 = (bf16[128,1024]{1,0:T(8,128)(2,1)}, bf16[128,1024]{1,0:T(8,128)(2,1)S(1)}, u32[]{:S(2)}, u32[]{:S(2)}) collective-permute-start(bf16[128,1024]{1,0:T(8,128)(2,1)} %get-tuple-element.122), channel_id=1, source_target_pairs={{0,24},{8,16},{16,8},{24,0},{1,25},{9,17},{17,9},{25,1},{2,26},{10... | collective-permute-start | bytes 786440 | tf_op jit(solution)/shard_map/ppermute | solution.py:370
  189.8 7.1 %collective-permute-start.21 = (bf16[128,1024]{1,0:T(8,128)(2,1)}, bf16[128,1024]{1,0:T(8,128)(2,1)S(1)}, u32[]{:S(2)}, u32[]{:S(2)}) collective-permute-start(bf16[128,1024]{1,0:T(8,128)(2,1)} %get-tuple-element.117), channel_id=1, source_target_pairs={{0,8},{8,0},{16,24},{24,16},{1,9},{9,1},{17,25},{25,17},{2,10},{10... | collective-permute-start | bytes 786440 | tf_op jit(solution)/shard_map/ppermute | solution.py:370
  190.8 9.4 %collective-permute-start.22 = (bf16[128,1024]{1,0:T(8,128)(2,1)}, bf16[128,1024]{1,0:T(8,128)(2,1)S(1)}, u32[]{:S(2)}, u32[]{:S(2)}) collective-permute-start(bf16[128,1024]{1,0:T(8,128)(2,1)} %get-tuple-element.118), channel_id=1, source_target_pairs={{0,16},{8,24},{16,0},{24,8},{1,17},{9,25},{17,1},{25,9},{2,18},{10... | collective-permute-start | bytes 786440 | tf_op jit(solution)/shard_map/ppermute | solution.py:370
  191.6 12.2 %collective-permute-start.23 = (bf16[128,1024]{1,0:T(8,128)(2,1)}, bf16[128,1024]{1,0:T(8,128)(2,1)S(1)}, u32[]{:S(2)}, u32[]{:S(2)}) collective-permute-start(bf16[128,1024]{1,0:T(8,128)(2,1)} %get-tuple-element.119), channel_id=1, source_target_pairs={{0,24},{8,16},{16,8},{24,0},{1,25},{9,17},{17,9},{25,1},{2,26},{10... | collective-permute-start | bytes 786440 | tf_op jit(solution)/shard_map/ppermute | solution.py:370
  (19 other events, 36.2 us)
Sparse Core Ops, SparseCore 0:
  20.9 49.9 all-gather.2

commit v5 on v4

--- a/solution.py
+++ b/solution.py
@@ -9,7 +9,7 @@
 
 BLOCK = 128
 LEN = 16
-CHUNKS = (4, 5, 3, 1, 1)
+TILES = 14
 VMEM_LIMIT = 60 * 1024 * 1024
 BRIEF = pl.CostEstimate(flops=1, bytes_accessed=1, transcendentals=0)
 
@@ -161,51 +161,52 @@
     )(gathered, outer_gate, outer_up, *after)
 
 
-def join_kernel(*refs):
-    *parts, leave_gate_ref, leave_up_ref, stay_gate_ref, stay_up_ref, token_ref = refs
-    mark(token_ref)
-    targets = ((leave_gate_ref, stay_gate_ref), (leave_up_ref, stay_up_ref))
-    for which, (leave_ref, target_ref) in enumerate(targets):
-        stay_ref, mate_ref, far_ref, both_ref = parts[4 * which : 4 * which + 4]
-        target_ref[...] = stay_ref[...] + mate_ref[...].astype(jnp.float32)
+def join_kernel(far_gate_ref, both_gate_ref, far_up_ref, both_up_ref, *refs):
+    leave_gate_ref, leave_up_ref, token_ref = refs[-3:]
+    mark(token_ref)
+    for far_ref, both_ref, leave_ref in (
+        (far_gate_ref, both_gate_ref, leave_gate_ref),
+        (far_up_ref, both_up_ref, leave_up_ref),
+    ):
         leave_ref[...] = (far_ref[...] + both_ref[...].astype(jnp.float32)).astype(
             leave_ref.dtype
         )
 
 
-def join(parts):
+def join(parts, *after):
     group_tok, unit_rows = parts[0].shape
-    tile = tile_of(unit_rows)
+    tile = unit_rows // 2 if unit_rows % 256 == 0 else unit_rows
     block = pl.BlockSpec((group_tok, tile), lambda i: (0, i))
     leave = jax.ShapeDtypeStruct((group_tok, unit_rows), jnp.bfloat16)
-    stay = jax.ShapeDtypeStruct((group_tok, unit_rows), jnp.float32)
     return pl.pallas_call(
         join_kernel,
         grid=(unit_rows // tile,),
-        in_specs=[block] * len(parts),
-        out_specs=[block] * 4 + [TOKEN_SPEC],
-        out_shape=[leave, leave, stay, stay, TOKEN],
+        in_specs=[block] * len(parts) + [STAY] * len(after),
+        out_specs=[block] * 2 + [TOKEN_SPEC],
+        out_shape=[leave, leave, TOKEN],
         compiler_params=pltpu.CompilerParams(vmem_limit_bytes=VMEM_LIMIT),
         cost_estimate=BRIEF,
         name="join",
-    )(*parts)
+    )(*parts, *after)
 
 
 def policy_kernel(blocks_ref, w_gate_ref, w_up_ref, *refs):
-    gate_ref, up_ref, inputs_ref, token_ref = refs[-4:]
+    gate_ref, up_ref, inputs_ref, token_ref, turned_ref = refs[-5:]
     ranks, groups, rows, width = blocks_ref.shape
 
     @pl.when(pl.program_id(0) == 0)
     def _():
         mark(token_ref)
         for block in range(groups):
-            inputs_ref[:, block * width : (block + 1) * width] = blocks_ref[:, block].reshape(
-                ranks * rows, width
-            )
-
-    inputs = inputs_ref[...]
-    gate_ref[...] = project(inputs, w_gate_ref[0])
-    up_ref[...] = project(inputs, w_up_ref[0])
+            part = blocks_ref[:, block].reshape(ranks * rows, width)
+            inputs_ref[:, block * width : (block + 1) * width] = part
+            turned_ref[block * width : (block + 1) * width] = part.T
+
+    turned = turned_ref[...]
+    for weight_ref, result_ref in ((w_gate_ref, gate_ref), (w_up_ref, up_ref)):
+        result_ref[...] = jnp.dot(
+            weight_ref[0], turned, preferred_element_type=jnp.float32
+        ).T
 
 
 def policy_products(gathered, w_gate, w_up, *after):
@@ -236,6 +237,7 @@
             jax.ShapeDtypeStruct((group_tok, depth), gathered.dtype),
             TOKEN,
         ],
+        scratch_shapes=[pltpu.VMEM((depth, group_tok), gathered.dtype)],
         compiler_params=pltpu.CompilerParams(vmem_limit_bytes=VMEM_LIMIT),
         cost_estimate=BRIEF,
         name="policy_products",
@@ -369,54 +371,58 @@
     def swap(value, bits):
         return lax.ppermute(value, "rep", [(i, i ^ bits) for i in range(groups)])
 
-    tile = outer_gate.shape[0] // sum(CHUNKS)
-    starts = [sum(CHUNKS[:chunk]) for chunk in range(len(CHUNKS))]
-    pieces = [[] for _ in CHUNKS]
+    tile = outer_gate.shape[0] // TILES
+    pieces = []
     updated = None
 
-    def send(chunks, masks, *after):
-        steps = sum(CHUNKS[chunk] for chunk in chunks)
-        begin = starts[chunks[0]]
+    def send(begin, steps, masks, *after):
         parts, token = pick(begin, steps, tile, place, w_gate, masks, width, *after)
-        came = [swap(part, bits) for part, bits in zip(parts, masks)]
-        for chunk in chunks:
-            pieces[chunk] += [(piece, begin) for piece in came]
+        came = [swap(part, mask) for part, mask in zip(parts, masks)]
+        pieces.extend((mask, begin, steps, piece) for mask, piece in zip(masks, came))
         return came, token
 
-    def update(chunk, *after):
+    def update(first, steps, *after):
+        there = [
+            (piece, begin)
+            for mask, begin, count, piece in pieces
+            if begin <= first and first + steps <= begin + count
+        ]
+        assert len(there) == groups - 1
         return outer_update(
-            starts[chunk],
-            CHUNKS[chunk],
-            tile,
-            place,
-            outer_gate,
-            moment,
-            w_gate,
-            pieces[chunk],
-            updated,
-            *after,
+            first, steps, tile, place, outer_gate, moment, w_gate, there, updated, *after
         )
 
-    first, token = send((0,), (2,))
+    early, token = send(0, 6, (2,))
     shares, token = pick(
         0, 1, tokens.shape[0], place, tokens[None], tuple(range(1, groups)), width, token
     )
     others = [swap(share, bits) for bits, share in enumerate(shares, 1)]
     assembled, token = assemble(place, tokens, others, token)
     gathered = lax.all_gather(assembled, "fsdp", axis=0, tiled=False)
-    _, token = send((0,), (1, 3), token)
-    second, token = send((1,), (2,), token, *first)
-    updated, token = update(0, token)
-
-    *parts, token = partial_products(gathered, outer_gate, outer_up, token)
+    _, token = send(0, 3, (1, 3), token)
+    late, token = send(3, 3, (1, 3), token, *early)
+    updated, token = update(0, 3, token)
+    second, token = send(6, 4, (2,), token)
+
+    *parts, token = partial_products(gathered, outer_gate, outer_up, token, *late)
     for at in (1, 3, 5, 7):
         parts[at] = swap(parts[at], 1)
-    leave_gate, leave_up, stay_gate, stay_up, token = join(parts)
-    gate_ref = stay_gate + swap(leave_gate, 2).astype(jnp.float32)
-    upper_ref = stay_up + swap(leave_up, 2).astype(jnp.float32)
-    _, token = send((1,), (1, 3), token)
-    third, token = send((2,), (2,), token, *second)
+    stay_gate, near_gate, far_gate, both_gate, stay_up, near_up, far_up, both_up = parts
+    leave_gate, leave_up, token = join(
+        (far_gate, both_gate, far_up, both_up), near_gate, near_up
+    )
+    gate_ref, upper_ref = (
+        stay + near.astype(jnp.float32) + swap(leave, 2).astype(jnp.float32)
+        for stay, near, leave in (
+            (stay_gate, near_gate, leave_gate),
+            (stay_up, near_up, leave_up),
+        )
+    )
+    _, token = send(6, 4, (1, 3), token)
+    _, token = send(10, 2, (2,), token, *second)
     gate, upper, inputs, token = policy_products(gathered, w_gate, w_up, token)
+    _, token = send(10, 2, (1, 3), token)
+    updated, token = update(3, 3, token)
 
     group_tok = inputs.shape[0]
     seqs = group_tok // LEN
@@ -445,13 +451,12 @@
     coef = jnp.dot(weight, pick_rejected - pick_chosen, precision=highest)
     token_grad = jnp.broadcast_to(coef[:, None], (seqs, LEN)).reshape(-1) * mask_f
     grad_gate, grad_up, token = weight_grads(gate, upper, readout, token_grad, inputs, token)
-    _, token = send((2,), (1, 3), token)
-    updated, token = update(1, token)
-    _, token = send((3,), (1, 2, 3), token)
-    updated, token = update(2, token)
-    _, token = send((4,), (1, 2, 3), token)
-    updated, token = update(3, token)
-    updated, token = update(4, token)
+    _, token = send(12, 1, (1, 2, 3), token)
+    updated, token = update(6, 4, token)
+    _, token = send(13, 1, (1, 2, 3), token)
+    updated, token = update(10, 2, token)
+    updated, token = update(12, 1, token)
+    updated, token = update(13, 1, token)
     new_outer, new_moment = updated
     return (loss, grad_gate, grad_up, new_outer, new_moment)
 

time: 218 us -> 226 us (1.037)
  waiting for transfers between devices: 61.3 us -> 69.2 us
    ppermute x24 -> x26, waiting for transfers between devices: 55.1 us -> 63.4 us  [swap(): return lax.ppermute(value, 'rep', [(i, i ^ bits) for i in range(groups)])]
    pallas_call x1, Pallas kernels: 6.19 us -> 2.63 us  [join(): pl.pallas_call(join_kernel, grid=(unit_rows // tile,), in_specs=[block] *...]
    pallas_call x5 -> x6, Pallas kernels: 28.5 us -> 30.3 us  [outer_update(): pl.pallas_call(functools.partial(outer_kernel, groups, strip), grid_spec=...]
    ppermute x24 -> x26, starting transfers between devices: 18.5 us -> 17.9 us  [swap(): return lax.ppermute(value, 'rep', [(i, i ^ bits) for i in range(groups)])]
    unnamed x46 -> x54, local copies, waits for them, and re-layouts: 6 us -> 5.85 us
    pallas_call x9 -> x10, Pallas kernels: 27.6 us -> 27.7 us  [pick(): pl.pallas_call(functools.partial(pick_kernel, count), grid_spec=pltpu.Pre...]
  transfers between devices with their start and end apart: 28 -> 30, of which waited for: 16 -> 15; matrix products, arithmetic and copies ran while one was open for 3% -> 4% of each run, Pallas kernels for 43% -> 40%
where the time goes in v5:
time: 226 us; the launch traced here: 225 us
  Pallas kernels  101 us (45%)
  waiting for transfers between devices  69.2 us (31%)
  starting transfers between devices  23.7 us (10%)
  between operations  16 us (7%)
  local copies, waits for them, and re-layouts  8.15 us (4%)
  other arithmetic  3.86 us (2%)
  matrix products  3.23 us (1%)
    ppermute x26, waiting for transfers between devices, swap(): return lax.ppermute(value, 'rep', [(i, i ^ bits) for i in range(groups)])  63.4 us
    pallas_call x6, Pallas kernels, outer_update(): pl.pallas_call(functools.partial(outer_kernel, groups, strip), grid_spec=...  30.3 us
    pallas_call x10, Pallas kernels, pick(): pl.pallas_call(functools.partial(pick_kernel, count), grid_spec=pltpu.Pre...  27.7 us
    ppermute x26, starting transfers between devices, swap(): return lax.ppermute(value, 'rep', [(i, i ^ bits) for i in range(groups)])  17.9 us
    pallas_call x1, Pallas kernels, policy_products(): pl.pallas_call(policy_kernel, grid=(unit_rows // tile,), in_specs=[pl.Blo...  15.8 us
    pallas_call x1, Pallas kernels, weight_grads(): pl.pallas_call(grads_kernel, grid=(unit_rows // tile,), in_specs=[units,...  12.7 us
    pallas_call x1, Pallas kernels, partial_products(): pl.pallas_call(partial_kernel, grid=(unit_rows // tile,), in_specs=[pl.Bl...  10 us
    unnamed x54, local copies, waits for them, and re-layouts  5.85 us
  transfers between devices with their start and end apart: 30, of which 15 were waited for; matrix products, arithmetic and copies ran while one was open for 4% of the time, Pallas kernels for 40%

profile of v5, /device:TPU:0, one launch (start us, length us, event | category | flops | bytes accessed | tf_op | source)
XLA Modules:
  0.0 224.9 jit_solution(5758135707200940651)
XLA Ops:
  7.2 4.6 %pick.10 = (bf16[768,1024]{1,0:T(8,128)(2,1)}, f32[8,128]{1,0:T(8,128)}) custom-call(s32[1]{0:T(128)} %bitcast.1.me_ref, bf16[1,1792,4096]{2,1,0:T(8,128)(2,1)} %refs_0_.29), custom_call_target="tpu_custom_call" | custom-call | flops 1 | bytes 1 | tf_op jit(solution)/shard_map/pick/pallas_call | solution.py:57
  13.7 2.5 %collective-permute-start.1 = (bf16[16,1024]{1,0:T(8,128)(2,1)}, bf16[16,1024]{1,0:T(8,128)(2,1)S(1)}, u32[]{:S(2)}, u32[]{:S(2)}) collective-permute-start(bf16[16,1024]{1,0:T(8,128)(2,1)} %get-tuple-element.74), channel_id=1, source_target_pairs={{0,16},{8,24},{16,0},{24,8},{1,17},{9,25},{17,1},{25,9},{2,18},{10... | collective-permute-start | bytes 98312 | tf_op jit(solution)/shard_map/ppermute | solution.py:372
  16.3 2.1 collective-permute-done.1.refs_1_
  20.3 1.6 assemble.1
  22.9 3.3 %pick.12 = (bf16[384,1024]{1,0:T(8,128)(2,1)}, bf16[384,1024]{1,0:T(8,128)(2,1)}, f32[8,128]{1,0:T(8,128)}) custom-call(s32[1]{0:T(128)} %bitcast.1.me_ref, bf16[1,1792,4096]{2,1,0:T(8,128)(2,1)} %refs_0_.29, bf16[1,1792,4096]{2,1,0:T(8,128)(2,1)} %refs_0_.29, f32[8,128]{1,0:T(8,128)} %get-tuple-element.79.refs_2_), custom_call_target="tpu_custom_call" | custom-call | flops 1 | bytes 1 | tf_op jit(solution)/shard_map/pick/pallas_call | solution.py:57
  27.5 32.0 %collective-permute-done.3.refs_3_.refs_1_ = bf16[768,1024]{1,0:T(8,128)(2,1)S(1)} collective-permute-done((bf16[768,1024]{1,0:T(8,128)(2,1)}, bf16[768,1024]{1,0:T(8,128)(2,1)S(1)}, u32[]{:S(2)}, u32[]{:S(2)}) %collective-permute-start.3) | collective-permute-done | bytes 1572896 | tf_op jit(solution)/shard_map/ppermute | solution.py:372
  60.6 3.4 %pick.13 = (bf16[384,1024]{1,0:T(8,128)(2,1)}, bf16[384,1024]{1,0:T(8,128)(2,1)}, f32[8,128]{1,0:T(8,128)}) custom-call(s32[1]{0:T(128)} %bitcast.1.me_ref, bf16[1,1792,4096]{2,1,0:T(8,128)(2,1)} %refs_0_.29, bf16[1,1792,4096]{2,1,0:T(8,128)(2,1)} %refs_0_.29, f32[8,128]{1,0:T(8,128)} %get-tuple-element.82.refs_2_, bf16[768,1024]{1,0:T(8,128)(2,1)} %copy-done), custom_call_target="tpu_custom_call" | custom-call | flops 1 | bytes 1 | tf_op jit(solution)/shard_map/pick/pallas_call | solution.py:57
  64.9 10.1 %collective-permute-done.5.refs_3_ = bf16[384,1024]{1,0:T(8,128)(2,1)} collective-permute-done((bf16[384,1024]{1,0:T(8,128)(2,1)}, bf16[384,1024]{1,0:T(8,128)(2,1)}, u32[]{:S(2)}, u32[]{:S(2)}) %collective-permute-start.5) | collective-permute-done | bytes 786464 | tf_op jit(solution)/shard_map/ppermute | solution.py:372
  75.1 6.0 %outer_update.6 = (bf16[1792,1024]{1,0:T(8,128)(2,1)}, f32[1792,1024]{1,0:T(8,128)}, f32[8,128]{1,0:T(8,128)}) custom-call(s32[1]{0:T(128)} %bitcast.1.me_ref, bf16[1792,1024]{1,0:T(8,128)(2,1)} %outer_ref.11, f32[1792,1024]{1,0:T(8,128)} %moment_ref.11, bf16[1,1792,4096]{2,1,0:T(8,128)(2,1)} %refs_0_.29, bf16[768,1024]{1,0:T(8,128)(2,1)} %copy-done, ...), custom_call_target="tpu_custom_call" | custom-call | flops 1 | bytes 1 | tf_op jit(solution)/shard_map/outer_update/pallas_call | solution.py:344
  81.1 3.4 %pick.14 = (bf16[512,1024]{1,0:T(8,128)(2,1)}, f32[8,128]{1,0:T(8,128)}) custom-call(s32[1]{0:T(128)} %bitcast.1.me_ref, bf16[1,1792,4096]{2,1,0:T(8,128)(2,1)} %refs_0_.29, f32[8,128]{1,0:T(8,128)} %get-tuple-element.84.refs_1_), custom_call_target="tpu_custom_call" | custom-call | flops 1 | bytes 1 | tf_op jit(solution)/shard_map/pick/pallas_call | solution.py:57
  85.4 6.4 %collective-permute-done.7.refs_2_.refs_3_ = bf16[384,1024]{1,0:T(8,128)(2,1)S(1)} collective-permute-done((bf16[384,1024]{1,0:T(8,128)(2,1)}, bf16[384,1024]{1,0:T(8,128)(2,1)S(1)}, u32[]{:S(2)}, u32[]{:S(2)}) %collective-permute-start.7) | collective-permute-done | bytes 786464 | tf_op jit(solution)/shard_map/ppermute | solution.py:372
  92.7 10.0 %partial_products.1 = (f32[128,1792]{1,0:T(8,128)}, bf16[128,1792]{1,0:T(8,128)(2,1)}, f32[128,1792]{1,0:T(8,128)}, bf16[128,1792]{1,0:T(8,128)(2,1)}, f32[128,1...) custom-call(bf16[8,8,16,1024]{3,2,1,0:T(8,128)(2,1)} %bitcast.28, ...), custom_call_target="tpu_custom_call" | custom-call | flops 1 | bytes 1 | tf_op jit(solution)/shard_map/partial_products/pallas_call | solution.py:136
  108.4 2.6 %join.1 = (bf16[128,1792]{1,0:T(8,128)(2,1)}, bf16[128,1792]{1,0:T(8,128)(2,1)}, f32[8,128]{1,0:T(8,128)}) custom-call(f32[128,1792]{1,0:T(8,128)} %get-tuple-element.88.far_gate_ref, bf16[128,1792]{1,0:T(8,128)(2,1)} %copy-done.14, f32[128,1792]{1,0:T(8,128)} %get-tuple-element.90.far_up_ref, bf16[128,1792]{1,0:T(8,128)(2,1)} %copy-done.15, ...), custom_call_target="tpu_custom_call" | custom-call | flops 1 | bytes 1 | tf_op jit(solution)/shard_map/join/pallas_call | solution.py:181
  114.3 3.8 %pick.15 = (bf16[512,1024]{1,0:T(8,128)(2,1)}, bf16[512,1024]{1,0:T(8,128)(2,1)}, f32[8,128]{1,0:T(8,128)}) custom-call(s32[1]{0:T(128)} %bitcast.1.me_ref, bf16[1,1792,4096]{2,1,0:T(8,128)(2,1)} %refs_0_.29, bf16[1,1792,4096]{2,1,0:T(8,128)(2,1)} %refs_0_.29, f32[8,128]{1,0:T(8,128)} %get-tuple-element.94.refs_2_), custom_call_target="tpu_custom_call" | custom-call | flops 1 | bytes 1 | tf_op jit(solution)/shard_map/pick/pallas_call | solution.py:57
  119.0 1.8 pick.16
  121.6 15.8 %policy_products.1 = (f32[128,1792]{1,0:T(8,128)}, f32[128,1792]{1,0:T(8,128)}, bf16[128,4096]{1,0:T(8,128)(2,1)}, f32[8,128]{1,0:T(8,128)}) custom-call(bf16[8,8,16,1024]{3,2,1,0:T(8,128)(2,1)} %bitcast.29, bf16[1,1792,4096]{2,1,0:T(8,128)(2,1)} %refs_0_.29, bf16[1,1792,4096]{2,1,0:T(8,128)(2,1)} %w_up_ref.1, f32[8,128]{1,0:T(8,128)} %get-tuple-element.97.refs_0_), custom_call_target="tpu_custom_call" | custom-call | flops 1 | bytes 1 | tf_op jit(solution)/shard_map/policy_products/pallas_call | solution.py:220
  137.4 2.0 pick.17
  140.0 6.2 %outer_update.7 = (bf16[1792,1024]{1,0:T(8,128)(2,1)}, f32[1792,1024]{1,0:T(8,128)}, f32[8,128]{1,0:T(8,128)}) custom-call(s32[1]{0:T(128)} %bitcast.1.me_ref, bf16[1792,1024]{1,0:T(8,128)(2,1)} %outer_ref.11, f32[1792,1024]{1,0:T(8,128)} %moment_ref.11, bf16[1,1792,4096]{2,1,0:T(8,128)(2,1)} %refs_0_.29, ...), custom_call_target="tpu_custom_call", output_to_operand_aliasing={{0}: (7, {}), {1}: (8, {})} | custom-call | flops 1 | bytes 1 | tf_op jit(solution)/shard_map/outer_update/pallas_call | solution.py:344
  147.2 2.3 %fusion.3 = (f32[128]{0:T(128)S(1)}, f32[128]{0:T(128)S(1)}) fusion(bf16[128,1792]{1,0:T(8,128)(2,1)S(1)} %copy-done.10, bf16[128,1792]{1,0:T(8,128)(2,1)} %collective-permute-done.14, f32[128,1792]{1,0:T(8,128)} %get-tuple-element.102, bf16[128,1792]{1,0:T(8,128)(2,1)S(1)} %copy-done.9, bf16[128,1792]{1,0:T(8,128)(2,1)} %collective-permute-done.13, ...), kind=kLoop, calls=%fused_computation.8 | loop fusion | flops 6192896 | bytes 5964800 | tf_op jit(solution)/shard_map/reduce_sum | solution.py:29
  150.5 1.6 collective-permute-start.15
  152.1 2.0 collective-permute-done.15
  155.7 2.0 collective-permute-done.16
  157.7 2.6 %collective-permute-start.17 = (f32[8]{0:T(128)S(1)}, f32[8]{0:T(128)S(1)}, u32[]{:S(2)}, u32[]{:S(2)}) collective-permute-start(f32[8]{0:T(128)S(1)} %add.42), channel_id=1, source_target_pairs={{0,4},{1,5},{2,6},{3,7},{4,0},{5,1},{6,2},{7,3},{8,12},{9,13},{10,... | collective-permute-start | bytes 104 | tf_op jit(solution)/shard_map/ppermute | solution.py:437
  160.3 1.8 collective-permute-done.17
  166.9 12.7 %weight_grads.1 = (bf16[1,1792,4096]{2,1,0:T(8,128)(2,1)}, bf16[1,1792,4096]{2,1,0:T(8,128)(2,1)}, f32[8,128]{1,0:T(8,128)}) custom-call(f32[128,1792]{1,0:T(8,128)} %get-tuple-element.98.gate_ref, f32[128,1792]{1,0:T(8,128)} %get-tuple-element.99.up_ref, bf16[128,1792]{1,0:T(8,128)(2,1)} %readout_ref.1, f32[128,1]{1,0:T(8,128)} %copy.25.token_grad_ref, ...), custom_call_target="tpu_custom_call" | custom-call | flops 1 | bytes 1 | tf_op jit(solution)/shard_map/weight_grads/pallas_call | solution.py:272
  179.6 2.0 pick.18
  183.8 7.2 %outer_update.8 = (bf16[1792,1024]{1,0:T(8,128)(2,1)}, f32[1792,1024]{1,0:T(8,128)}, f32[8,128]{1,0:T(8,128)}) custom-call(s32[1]{0:T(128)} %bitcast.1.me_ref, bf16[1792,1024]{1,0:T(8,128)(2,1)} %outer_ref.11, f32[1792,1024]{1,0:T(8,128)} %moment_ref.11, bf16[1,1792,4096]{2,1,0:T(8,128)(2,1)} %refs_0_.29, ...), custom_call_target="tpu_custom_call", output_to_operand_aliasing={{0}: (7, {}), {1}: (8, {})} | custom-call | flops 1 | bytes 1 | tf_op jit(solution)/shard_map/outer_update/pallas_call | solution.py:344
  191.0 2.0 pick.19
  196.1 4.4 %outer_update.9 = (bf16[1792,1024]{1,0:T(8,128)(2,1)}, f32[1792,1024]{1,0:T(8,128)}, f32[8,128]{1,0:T(8,128)}) custom-call(s32[1]{0:T(128)} %bitcast.1.me_ref, bf16[1792,1024]{1,0:T(8,128)(2,1)} %outer_ref.11, f32[1792,1024]{1,0:T(8,128)} %moment_ref.11, bf16[1,1792,4096]{2,1,0:T(8,128)(2,1)} %refs_0_.29, ...), custom_call_target="tpu_custom_call", output_to_operand_aliasing={{0}: (7, {}), {1}: (8, {})} | custom-call | flops 1 | bytes 1 | tf_op jit(solution)/shard_map/outer_update/pallas_call | solution.py:344
  202.4 3.3 %outer_update.10 = (bf16[1792,1024]{1,0:T(8,128)(2,1)}, f32[1792,1024]{1,0:T(8,128)}, f32[8,128]{1,0:T(8,128)}) custom-call(s32[1]{0:T(128)} %bitcast.1.me_ref, bf16[1792,1024]{1,0:T(8,128)(2,1)} %outer_ref.11, f32[1792,1024]{1,0:T(8,128)} %moment_ref.11, bf16[1,1792,4096]{2,1,0:T(8,128)(2,1)} %refs_0_.29, ...), custom_call_target="tpu_custom_call", output_to_operand_aliasing={{0}: (7, {}), {1}: (8, {})} | custom-call | flops 1 | bytes 1 | tf_op jit(solution)/shard_map/outer_update/pallas_call | solution.py:344
  207.3 5.6 %collective-permute-done.22.refs_3_ = bf16[128,1024]{1,0:T(8,128)(2,1)S(1)} collective-permute-done((bf16[128,1024]{1,0:T(8,128)(2,1)}, bf16[128,1024]{1,0:T(8,128)(2,1)S(1)}, u32[]{:S(2)}, u32[]{:S(2)}) %collective-permute-start.22) | collective-permute-done | bytes 262176 | tf_op jit(solution)/shard_map/ppermute | solution.py:372
  213.6 3.3 %outer_update.11 = (bf16[1792,1024]{1,0:T(8,128)(2,1)}, f32[1792,1024]{1,0:T(8,128)}, f32[8,128]{1,0:T(8,128)}) custom-call(s32[1]{0:T(128)} %bitcast.1.me_ref, bf16[1792,1024]{1,0:T(8,128)(2,1)} %outer_ref.11, f32[1792,1024]{1,0:T(8,128)} %moment_ref.11, bf16[1,1792,4096]{2,1,0:T(8,128)(2,1)} %refs_0_.29, ...), custom_call_target="tpu_custom_call", output_to_operand_aliasing={{0}: (7, {}), {1}: (8, {})} | custom-call | flops 1 | bytes 1 | tf_op jit(solution)/shard_map/outer_update/pallas_call | solution.py:344
  (122 shorter events, 38.5 us)
Async XLA Ops:
  7.2 84.7 %all-gather.3.cloned.1.call-start = ((), (), s32[]{:S(2)}) async-start(), calls=%async_computation | async-start | bytes 2359296 | tf_op jit(solution)/shard_map/all_gather | solution.py:401
  13.2 3.1 %collective-permute-start = (bf16[16,1024]{1,0:T(8,128)(2,1)}, bf16[16,1024]{1,0:T(8,128)(2,1)S(1)}, u32[]{:S(2)}, u32[]{:S(2)}) collective-permute-start(bf16[16,1024]{1,0:T(8,128)(2,1)} %get-tuple-element.73), channel_id=1, source_target_pairs={{0,8},{8,0},{16,24},{24,16},{1,9},{9,1},{17,25},{25,17},{2,10},{10... | collective-permute-start | bytes 98312 | tf_op jit(solution)/shard_map/ppermute | solution.py:372
  13.7 4.8 %collective-permute-start.1 = (bf16[16,1024]{1,0:T(8,128)(2,1)}, bf16[16,1024]{1,0:T(8,128)(2,1)S(1)}, u32[]{:S(2)}, u32[]{:S(2)}) collective-permute-start(bf16[16,1024]{1,0:T(8,128)(2,1)} %get-tuple-element.74), channel_id=1, source_target_pairs={{0,16},{8,24},{16,0},{24,8},{1,17},{9,25},{17,1},{25,9},{2,18},{10... | collective-permute-start | bytes 98312 | tf_op jit(solution)/shard_map/ppermute | solution.py:372
  16.1 3.6 %collective-permute-start.2 = (bf16[16,1024]{1,0:T(8,128)(2,1)}, bf16[16,1024]{1,0:T(8,128)(2,1)S(1)}, u32[]{:S(2)}, u32[]{:S(2)}) collective-permute-start(bf16[16,1024]{1,0:T(8,128)(2,1)} %get-tuple-element.75), channel_id=1, source_target_pairs={{0,24},{8,16},{16,8},{24,0},{1,25},{9,17},{17,9},{25,1},{2,26},{10... | collective-permute-start | bytes 98312 | tf_op jit(solution)/shard_map/ppermute | solution.py:372
  22.0 37.5 %collective-permute-start.3 = (bf16[768,1024]{1,0:T(8,128)(2,1)}, bf16[768,1024]{1,0:T(8,128)(2,1)S(1)}, u32[]{:S(2)}, u32[]{:S(2)}) collective-permute-start(bf16[768,1024]{1,0:T(8,128)(2,1)} %get-tuple-element.78), channel_id=1, source_target_pairs={{0,16},{8,24},{16,0},{24,8},{1,17},{9,25},{17,1},{25,9},{2,18},{10... | collective-permute-start | bytes 4718600 | tf_op jit(solution)/shard_map/ppermute | solution.py:372
  26.2 38.7 %collective-permute-start.4 = (bf16[384,1024]{1,0:T(8,128)(2,1)}, bf16[384,1024]{1,0:T(8,128)(2,1)S(1)}, u32[]{:S(2)}, u32[]{:S(2)}) collective-permute-start(bf16[384,1024]{1,0:T(8,128)(2,1)} %get-tuple-element.80), channel_id=1, source_target_pairs={{0,8},{8,0},{16,24},{24,16},{1,9},{9,1},{17,25},{25,17},{2,10},{10... | collective-permute-start | bytes 2359304 | tf_op jit(solution)/shard_map/ppermute | solution.py:372
  26.2 48.8 %collective-permute-start.5 = (bf16[384,1024]{1,0:T(8,128)(2,1)}, bf16[384,1024]{1,0:T(8,128)(2,1)}, u32[]{:S(2)}, u32[]{:S(2)}) collective-permute-start(bf16[384,1024]{1,0:T(8,128)(2,1)} %get-tuple-element.81), channel_id=1, source_target_pairs={{0,24},{8,16},{16,8},{24,0},{1,25},{9,17},{17,9},{25,1},{2,26},{10... | collective-permute-start | bytes 2359304 | tf_op jit(solution)/shard_map/ppermute | solution.py:372
  64.0 21.4 %collective-permute-start.6 = (bf16[384,1024]{1,0:T(8,128)(2,1)}, bf16[384,1024]{1,0:T(8,128)(2,1)S(1)}, u32[]{:S(2)}, u32[]{:S(2)}) collective-permute-start(bf16[384,1024]{1,0:T(8,128)(2,1)} %get-tuple-element.86), channel_id=1, source_target_pairs={{0,8},{8,0},{16,24},{24,16},{1,9},{9,1},{17,25},{25,17},{2,10},{10... | collective-permute-start | bytes 2359304 | tf_op jit(solution)/shard_map/ppermute | solution.py:372
  64.0 27.8 %collective-permute-start.7 = (bf16[384,1024]{1,0:T(8,128)(2,1)}, bf16[384,1024]{1,0:T(8,128)(2,1)S(1)}, u32[]{:S(2)}, u32[]{:S(2)}) collective-permute-start(bf16[384,1024]{1,0:T(8,128)(2,1)} %get-tuple-element.87), channel_id=1, source_target_pairs={{0,24},{8,16},{16,8},{24,0},{1,25},{9,17},{17,9},{25,1},{2,26},{10... | collective-permute-start | bytes 2359304 | tf_op jit(solution)/shard_map/ppermute | solution.py:372
  64.9 10.1 %copy-start.12 = (bf16[384,1024]{1,0:T(8,128)(2,1)}, bf16[384,1024]{1,0:T(8,128)(2,1)S(1)}, u32[]{:S(2)}) copy-start(bf16[384,1024]{1,0:T(8,128)(2,1)S(1)} %collective-permute-done.4.refs_2_) | copy-start | bytes 2359300
  84.4 33.6 %collective-permute-start.12 = (bf16[512,1024]{1,0:T(8,128)(2,1)}, bf16[512,1024]{1,0:T(8,128)(2,1)S(1)}, u32[]{:S(2)}, u32[]{:S(2)}) collective-permute-start(bf16[512,1024]{1,0:T(8,128)(2,1)} %get-tuple-element.96), channel_id=1, source_target_pairs={{0,16},{8,24},{16,0},{24,8},{1,17},{9,25},{17,1},{25,9},{2,18},{10... | collective-permute-start | bytes 3145736 | tf_op jit(solution)/shard_map/ppermute | solution.py:372
  92.7 20.3 %copy-start.26 = (s32[1,8]{1,0:T(1,128)S(1)}, s32[1,8]{1,0:T(1,128)}, u32[]{:S(2)}) copy-start(s32[1,8]{1,0:T(1,128)} %param.12) | copy-start | bytes 100
  102.7 2.9 %collective-permute-start.8 = (bf16[128,1792]{1,0:T(8,128)(2,1)}, bf16[128,1792]{1,0:T(8,128)(2,1)S(1)}, u32[]{:S(2)}, u32[]{:S(2)}) collective-permute-start(bf16[128,1792]{1,0:T(8,128)(2,1)} %get-tuple-element.89), channel_id=1, source_target_pairs={{0,8},{8,0},{16,24},{24,16},{1,9},{9,1},{17,25},{25,17},{2,10},{10... | collective-permute-start | bytes 1376264 | tf_op jit(solution)/shard_map/ppermute | solution.py:372
  104.0 2.3 %collective-permute-start.9 = (bf16[128,1792]{1,0:T(8,128)(2,1)}, bf16[128,1792]{1,0:T(8,128)(2,1)S(1)}, u32[]{:S(2)}, u32[]{:S(2)}) collective-permute-start(bf16[128,1792]{1,0:T(8,128)(2,1)} %get-tuple-element.91), channel_id=1, source_target_pairs={{0,8},{8,0},{16,24},{24,16},{1,9},{9,1},{17,25},{25,17},{2,10},{10... | collective-permute-start | bytes 1376264 | tf_op jit(solution)/shard_map/ppermute | solution.py:372
  104.0 2.9 %collective-permute-start.10 = (bf16[128,1792]{1,0:T(8,128)(2,1)}, bf16[128,1792]{1,0:T(8,128)(2,1)S(1)}, u32[]{:S(2)}, u32[]{:S(2)}) collective-permute-start(bf16[128,1792]{1,0:T(8,128)(2,1)} %get-tuple-element.92), channel_id=1, source_target_pairs={{0,8},{8,0},{16,24},{24,16},{1,9},{9,1},{17,25},{25,17},{2,10},{10... | collective-permute-start | bytes 1376264 | tf_op jit(solution)/shard_map/ppermute | solution.py:372
  104.5 3.1 %collective-permute-start.11 = (bf16[128,1792]{1,0:T(8,128)(2,1)}, bf16[128,1792]{1,0:T(8,128)(2,1)S(1)}, u32[]{:S(2)}, u32[]{:S(2)}) collective-permute-start(bf16[128,1792]{1,0:T(8,128)(2,1)} %get-tuple-element.93), channel_id=1, source_target_pairs={{0,8},{8,0},{16,24},{24,16},{1,9},{9,1},{17,25},{25,17},{2,10},{10... | collective-permute-start | bytes 1376264 | tf_op jit(solution)/shard_map/ppermute | solution.py:372
  111.0 35.2 %collective-permute-start.13 = (bf16[128,1792]{1,0:T(8,128)(2,1)}, bf16[128,1792]{1,0:T(8,128)(2,1)}, u32[]{:S(2)}, u32[]{:S(2)}) collective-permute-start(bf16[128,1792]{1,0:T(8,128)(2,1)} %get-tuple-element.101), channel_id=1, source_target_pairs={{0,16},{8,24},{16,0},{24,8},{1,17},{9,25},{17,1},{25,9},{2,18},{10... | collective-permute-start | bytes 1376264 | tf_op jit(solution)/shard_map/ppermute | solution.py:372
  111.8 35.3 %collective-permute-start.14 = (bf16[128,1792]{1,0:T(8,128)(2,1)}, bf16[128,1792]{1,0:T(8,128)(2,1)}, u32[]{:S(2)}, u32[]{:S(2)}) collective-permute-start(bf16[128,1792]{1,0:T(8,128)(2,1)} %get-tuple-element.103), channel_id=1, source_target_pairs={{0,16},{8,24},{16,0},{24,8},{1,17},{9,25},{17,1},{25,9},{2,18},{10... | collective-permute-start | bytes 1376264 | tf_op jit(solution)/shard_map/ppermute | solution.py:372
  120.8 72.2 %collective-permute-start.26 = (bf16[256,1024]{1,0:T(8,128)(2,1)}, bf16[256,1024]{1,0:T(8,128)(2,1)}, u32[]{:S(2)}, u32[]{:S(2)}) collective-permute-start(bf16[256,1024]{1,0:T(8,128)(2,1)} %get-tuple-element.125), channel_id=1, source_target_pairs={{0,16},{8,24},{16,0},{24,8},{1,17},{9,25},{17,1},{25,9},{2,18},{10... | collective-permute-start | bytes 1572872 | tf_op jit(solution)/shard_map/ppermute | solution.py:372
  139.5 53.8 %collective-permute-start.27 = (bf16[256,1024]{1,0:T(8,128)(2,1)}, bf16[256,1024]{1,0:T(8,128)(2,1)}, u32[]{:S(2)}, u32[]{:S(2)}) collective-permute-start(bf16[256,1024]{1,0:T(8,128)(2,1)} %get-tuple-element.126), channel_id=1, source_target_pairs={{0,8},{8,0},{16,24},{24,16},{1,9},{9,1},{17,25},{25,17},{2,10},{10... | collective-permute-start | bytes 1572872 | tf_op jit(solution)/shard_map/ppermute | solution.py:372
  139.5 42.1 %collective-permute-start.18 = (bf16[512,1024]{1,0:T(8,128)(2,1)}, bf16[512,1024]{1,0:T(8,128)(2,1)}, u32[]{:S(2)}, u32[]{:S(2)}) collective-permute-start(bf16[512,1024]{1,0:T(8,128)(2,1)} %get-tuple-element.112), channel_id=1, source_target_pairs={{0,8},{8,0},{16,24},{24,16},{1,9},{9,1},{17,25},{25,17},{2,10},{10... | collective-permute-start | bytes 3145736 | tf_op jit(solution)/shard_map/ppermute | solution.py:372
  146.2 36.4 %collective-permute-start.19 = (bf16[512,1024]{1,0:T(8,128)(2,1)}, bf16[512,1024]{1,0:T(8,128)(2,1)}, u32[]{:S(2)}, u32[]{:S(2)}) collective-permute-start(bf16[512,1024]{1,0:T(8,128)(2,1)} %get-tuple-element.113), channel_id=1, source_target_pairs={{0,24},{8,16},{16,8},{24,0},{1,25},{9,17},{17,9},{25,1},{2,26},{10... | collective-permute-start | bytes 3145736 | tf_op jit(solution)/shard_map/ppermute | solution.py:372
  150.5 3.6 %collective-permute-start.15 = (f32[8]{0:T(128)S(1)}, f32[8]{0:T(128)S(1)}, u32[]{:S(2)}, u32[]{:S(2)}) collective-permute-start(f32[8]{0:T(128)S(1)} %sub.9), channel_id=1, source_target_pairs={{0,1},{1,0},{2,3},{3,2},{4,5},{5,4},{6,7},{7,6},{8,9},{9,8},{10,11... | collective-permute-start | bytes 104 | tf_op jit(solution)/shard_map/ppermute | solution.py:437
  154.1 3.5 %collective-permute-start.16 = (f32[8]{0:T(128)S(1)}, f32[8]{0:T(128)S(1)}, u32[]{:S(2)}, u32[]{:S(2)}) collective-permute-start(f32[8]{0:T(128)S(1)} %add.41), channel_id=1, source_target_pairs={{0,2},{1,3},{2,0},{3,1},{4,6},{5,7},{6,4},{7,5},{8,10},{9,11},{10,... | collective-permute-start | bytes 104 | tf_op jit(solution)/shard_map/ppermute | solution.py:437
  157.7 4.4 %collective-permute-start.17 = (f32[8]{0:T(128)S(1)}, f32[8]{0:T(128)S(1)}, u32[]{:S(2)}, u32[]{:S(2)}) collective-permute-start(f32[8]{0:T(128)S(1)} %add.42), channel_id=1, source_target_pairs={{0,4},{1,5},{2,6},{3,7},{4,0},{5,1},{6,2},{7,3},{8,12},{9,13},{10,... | collective-permute-start | bytes 104 | tf_op jit(solution)/shard_map/ppermute | solution.py:437
  162.1 31.9 %collective-permute-start.28 = (bf16[256,1024]{1,0:T(8,128)(2,1)}, bf16[256,1024]{1,0:T(8,128)(2,1)S(1)}, u32[]{:S(2)}, u32[]{:S(2)}) collective-permute-start(bf16[256,1024]{1,0:T(8,128)(2,1)} %get-tuple-element.127), channel_id=1, source_target_pairs={{0,24},{8,16},{16,8},{24,0},{1,25},{9,17},{17,9},{25,1},{2,26},{10... | collective-permute-start | bytes 1572872 | tf_op jit(solution)/shard_map/ppermute | solution.py:372
  181.6 13.6 %collective-permute-start.23 = (bf16[128,1024]{1,0:T(8,128)(2,1)}, bf16[128,1024]{1,0:T(8,128)(2,1)S(1)}, u32[]{:S(2)}, u32[]{:S(2)}) collective-permute-start(bf16[128,1024]{1,0:T(8,128)(2,1)} %get-tuple-element.122), channel_id=1, source_target_pairs={{0,8},{8,0},{16,24},{24,16},{1,9},{9,1},{17,25},{25,17},{2,10},{10... | collective-permute-start | bytes 786440 | tf_op jit(solution)/shard_map/ppermute | solution.py:372
  182.6 17.9 %collective-permute-start.24 = (bf16[128,1024]{1,0:T(8,128)(2,1)}, bf16[128,1024]{1,0:T(8,128)(2,1)S(1)}, u32[]{:S(2)}, u32[]{:S(2)}) collective-permute-start(bf16[128,1024]{1,0:T(8,128)(2,1)} %get-tuple-element.123), channel_id=1, source_target_pairs={{0,16},{8,24},{16,0},{24,8},{1,17},{9,25},{17,1},{25,9},{2,18},{10... | collective-permute-start | bytes 786440 | tf_op jit(solution)/shard_map/ppermute | solution.py:372
  193.0 8.7 %collective-permute-start.25 = (bf16[128,1024]{1,0:T(8,128)(2,1)S(1)}, bf16[128,1024]{1,0:T(8,128)(2,1)S(1)}, u32[]{:S(2)}, u32[]{:S(2)}) collective-permute-start(bf16[128,1024]{1,0:T(8,128)(2,1)S(1)} %copy-done.25), channel_id=1, source_target_pairs={{0,24},{8,16},{16,8},{24,0},{1,25},{9,17},{17,9},{25,1},{2,26},{10... | collective-permute-start | bytes 786440 | tf_op jit(solution)/shard_map/ppermute | solution.py:372
  193.3 12.4 %collective-permute-start.20 = (bf16[128,1024]{1,0:T(8,128)(2,1)}, bf16[128,1024]{1,0:T(8,128)(2,1)S(1)}, u32[]{:S(2)}, u32[]{:S(2)}) collective-permute-start(bf16[128,1024]{1,0:T(8,128)(2,1)} %get-tuple-element.119), channel_id=1, source_target_pairs={{0,8},{8,0},{16,24},{24,16},{1,9},{9,1},{17,25},{25,17},{2,10},{10... | collective-permute-start | bytes 786440 | tf_op jit(solution)/shard_map/ppermute | solution.py:372
  194.0 13.2 %collective-permute-start.21 = (bf16[128,1024]{1,0:T(8,128)(2,1)}, bf16[128,1024]{1,0:T(8,128)(2,1)S(1)}, u32[]{:S(2)}, u32[]{:S(2)}) collective-permute-start(bf16[128,1024]{1,0:T(8,128)(2,1)} %get-tuple-element.120), channel_id=1, source_target_pairs={{0,16},{8,24},{16,0},{24,8},{1,17},{9,25},{17,1},{25,9},{2,18},{10... | collective-permute-start | bytes 786440 | tf_op jit(solution)/shard_map/ppermute | solution.py:372
  195.2 17.7 %collective-permute-start.22 = (bf16[128,1024]{1,0:T(8,128)(2,1)}, bf16[128,1024]{1,0:T(8,128)(2,1)S(1)}, u32[]{:S(2)}, u32[]{:S(2)}) collective-permute-start(bf16[128,1024]{1,0:T(8,128)(2,1)} %get-tuple-element.121), channel_id=1, source_target_pairs={{0,24},{8,16},{16,8},{24,0},{1,25},{9,17},{17,9},{25,1},{2,26},{10... | collective-permute-start | bytes 786440 | tf_op jit(solution)/shard_map/ppermute | solution.py:372
  (25 other events, 87.2 us)
Sparse Core Ops, SparseCore 0:
  22.1 49.9 all-gather.2

commit v6 on v5

--- a/solution.py
+++ b/solution.py
@@ -53,6 +53,12 @@
 
 def pick(first, steps, tile, me, weight, masks, width, *after):
     rows = steps * tile
+    block = max(
+        size
+        for size in range(1, max(1, steps // 2) + 1)
+        if steps % size == 0 and first % size == 0
+    )
+    first, steps, tile = first // block, steps // block, tile * block
     count = len(masks)
     *parts, token = pl.pallas_call(
         functools.partial(pick_kernel, count),
@@ -392,19 +398,16 @@
             first, steps, tile, place, outer_gate, moment, w_gate, there, updated, *after
         )
 
-    early, token = send(0, 6, (2,))
+    early, token = send(0, 10, (2,))
     shares, token = pick(
         0, 1, tokens.shape[0], place, tokens[None], tuple(range(1, groups)), width, token
     )
     others = [swap(share, bits) for bits, share in enumerate(shares, 1)]
     assembled, token = assemble(place, tokens, others, token)
     gathered = lax.all_gather(assembled, "fsdp", axis=0, tiled=False)
-    _, token = send(0, 3, (1, 3), token)
-    late, token = send(3, 3, (1, 3), token, *early)
-    updated, token = update(0, 3, token)
-    second, token = send(6, 4, (2,), token)
-
-    *parts, token = partial_products(gathered, outer_gate, outer_up, token, *late)
+    (near, _), token = send(0, 6, (1, 3), token)
+
+    *parts, token = partial_products(gathered, outer_gate, outer_up, token, near, *early)
     for at in (1, 3, 5, 7):
         parts[at] = swap(parts[at], 1)
     stay_gate, near_gate, far_gate, both_gate, stay_up, near_up, far_up, both_up = parts
@@ -419,10 +422,8 @@
         )
     )
     _, token = send(6, 4, (1, 3), token)
-    _, token = send(10, 2, (2,), token, *second)
     gate, upper, inputs, token = policy_products(gathered, w_gate, w_up, token)
-    _, token = send(10, 2, (1, 3), token)
-    updated, token = update(3, 3, token)
+    updated, token = update(0, 6, token)
 
     group_tok = inputs.shape[0]
     seqs = group_tok // LEN
@@ -432,6 +433,7 @@
     relative = local_scores(hidden, readout, mask_f, seqs) - local_scores(
         hidden_ref, readout, mask_f, seqs
     )
+    _, token = send(10, 2, (1, 2, 3), token, relative[None])
     hop = 1
     while hop < ranks:
         relative = relative + lax.ppermute(

time: 226 us -> 213 us (0.942)
  Pallas kernels: 101 us -> 87.6 us
  waiting for transfers between devices: 69.2 us -> 76.1 us
  starting transfers between devices: 23.7 us -> 21 us
    pallas_call x10 -> x7, Pallas kernels: 27.7 us -> 16.6 us  [pick(): pl.pallas_call(functools.partial(pick_kernel, count), grid_spec=pltpu.Pre...]
    ppermute x26 -> x23, waiting for transfers between devices: 63.4 us -> 72.2 us  [swap(): return lax.ppermute(value, 'rep', [(i, i ^ bits) for i in range(groups)])]
    ppermute x26 -> x23, starting transfers between devices: 17.9 us -> 15.2 us  [swap(): return lax.ppermute(value, 'rep', [(i, i ^ bits) for i in range(groups)])]
    pallas_call x6 -> x5, Pallas kernels: 30.3 us -> 28.3 us  [outer_update(): pl.pallas_call(functools.partial(outer_kernel, groups, strip), grid_spec=...]
    unnamed x54 -> x60, local copies, waits for them, and re-layouts: 5.85 us -> 4.37 us
  transfers between devices with their start and end apart: 30 -> 27, of which waited for: 15 -> 14; matrix products, arithmetic and copies ran while one was open for 4% -> 3% of each run, Pallas kernels for 40% -> 37%
where the time goes in v6:
time: 213 us; the launch traced here: 212 us
  Pallas kernels  87.6 us (41%)
  waiting for transfers between devices  76.1 us (36%)
  starting transfers between devices  21 us (10%)
  between operations  16.1 us (8%)
  local copies, waits for them, and re-layouts  6.66 us (3%)
  other arithmetic  3.19 us (1%)
    ppermute x23, waiting for transfers between devices, swap(): return lax.ppermute(value, 'rep', [(i, i ^ bits) for i in range(groups)])  72.2 us
    pallas_call x5, Pallas kernels, outer_update(): pl.pallas_call(functools.partial(outer_kernel, groups, strip), grid_spec=...  28.3 us
    pallas_call x7, Pallas kernels, pick(): pl.pallas_call(functools.partial(pick_kernel, count), grid_spec=pltpu.Pre...  16.6 us
    pallas_call x1, Pallas kernels, policy_products(): pl.pallas_call(policy_kernel, grid=(unit_rows // tile,), in_specs=[pl.Blo...  15.8 us
    ppermute x23, starting transfers between devices, swap(): return lax.ppermute(value, 'rep', [(i, i ^ bits) for i in range(groups)])  15.2 us
    pallas_call x1, Pallas kernels, weight_grads(): pl.pallas_call(grads_kernel, grid=(unit_rows // tile,), in_specs=[units,...  12.7 us
    pallas_call x1, Pallas kernels, partial_products(): pl.pallas_call(partial_kernel, grid=(unit_rows // tile,), in_specs=[pl.Bl...  9.91 us
    ppermute x3, starting transfers between devices, per_device(): lax.ppermute(relative, 'fsdp', [(i, i ^ hop) for i in range(ranks)])  5.75 us
  transfers between devices with their start and end apart: 27, of which 14 were waited for; matrix products, arithmetic and copies ran while one was open for 3% of the time, Pallas kernels for 37%

profile of v6, /device:TPU:0, one launch (start us, length us, event | category | flops | bytes accessed | tf_op | source)
XLA Modules:
  0.0 211.7 jit_solution(12252513423792479833)
XLA Ops:
  7.2 2.9 %pick.7 = (bf16[1280,1024]{1,0:T(8,128)(2,1)}, f32[8,128]{1,0:T(8,128)}) custom-call(s32[1]{0:T(128)} %bitcast.1.me_ref, bf16[1,1792,4096]{2,1,0:T(8,128)(2,1)} %refs_0_.21), custom_call_target="tpu_custom_call" | custom-call | flops 1 | bytes 1 | tf_op jit(solution)/shard_map/pick/pallas_call | solution.py:63
  10.1 1.4 pick.8
  12.0 2.5 %collective-permute-start.1 = (bf16[16,1024]{1,0:T(8,128)(2,1)}, bf16[16,1024]{1,0:T(8,128)(2,1)S(1)}, u32[]{:S(2)}, u32[]{:S(2)}) collective-permute-start(bf16[16,1024]{1,0:T(8,128)(2,1)} %get-tuple-element.65), channel_id=1, source_target_pairs={{0,16},{8,24},{16,0},{24,8},{1,17},{9,25},{17,1},{25,9},{2,18},{10... | collective-permute-start | bytes 98312 | tf_op jit(solution)/shard_map/ppermute | solution.py:378
  14.7 2.1 %collective-permute-done.1.refs_1_ = bf16[16,1024]{1,0:T(8,128)(2,1)S(1)} collective-permute-done((bf16[16,1024]{1,0:T(8,128)(2,1)}, bf16[16,1024]{1,0:T(8,128)(2,1)S(1)}, u32[]{:S(2)}, u32[]{:S(2)}) %collective-permute-start.1) | collective-permute-done | bytes 32800 | tf_op jit(solution)/shard_map/ppermute | solution.py:378
  18.7 1.6 assemble.1
  21.3 3.1 %pick.9 = (bf16[768,1024]{1,0:T(8,128)(2,1)}, bf16[768,1024]{1,0:T(8,128)(2,1)}, f32[8,128]{1,0:T(8,128)}) custom-call(s32[1]{0:T(128)} %bitcast.1.me_ref, bf16[1,1792,4096]{2,1,0:T(8,128)(2,1)} %refs_0_.21, bf16[1,1792,4096]{2,1,0:T(8,128)(2,1)} %refs_0_.21, f32[8,128]{1,0:T(8,128)} %get-tuple-element.69.refs_2_), custom_call_target="tpu_custom_call" | custom-call | flops 1 | bytes 1 | tf_op jit(solution)/shard_map/pick/pallas_call | solution.py:63
  25.7 2.4 %collective-permute-done.3.refs_1_.refs_2_ = bf16[768,1024]{1,0:T(8,128)(2,1)} collective-permute-done((bf16[768,1024]{1,0:T(8,128)(2,1)}, bf16[768,1024]{1,0:T(8,128)(2,1)}, u32[]{:S(2)}, u32[]{:S(2)}) %collective-permute-start.3) | collective-permute-done | bytes 1572896 | tf_op jit(solution)/shard_map/ppermute | solution.py:378
  28.1 52.2 %collective-permute-done.4.refs_2_.refs_1_ = bf16[1280,1024]{1,0:T(8,128)(2,1)S(1)} collective-permute-done((bf16[1280,1024]{1,0:T(8,128)(2,1)}, bf16[1280,1024]{1,0:T(8,128)(2,1)S(1)}, u32[]{:S(2)}, u32[]{:S(2)}) %collective-permute-start.4) | collective-permute-done | bytes 2621472 | tf_op jit(solution)/shard_map/ppermute | solution.py:378
  80.3 1.5 copy-done
  81.8 9.9 %partial_products.1 = (f32[128,1792]{1,0:T(8,128)}, bf16[128,1792]{1,0:T(8,128)(2,1)}, f32[128,1792]{1,0:T(8,128)}, bf16[128,1792]{1,0:T(8,128)(2,1)}, f32[128,1...) custom-call(bf16[8,8,16,1024]{3,2,1,0:T(8,128)(2,1)} %bitcast.29, ...), custom_call_target="tpu_custom_call" | custom-call | flops 1 | bytes 1 | tf_op jit(solution)/shard_map/partial_products/pallas_call | solution.py:142
  96.6 2.6 %join.1 = (bf16[128,1792]{1,0:T(8,128)(2,1)}, bf16[128,1792]{1,0:T(8,128)(2,1)}, f32[8,128]{1,0:T(8,128)}) custom-call(f32[128,1792]{1,0:T(8,128)} %get-tuple-element.73.far_gate_ref, bf16[128,1792]{1,0:T(8,128)(2,1)} %copy-done.12, f32[128,1792]{1,0:T(8,128)} %get-tuple-element.75.far_up_ref, bf16[128,1792]{1,0:T(8,128)(2,1)} %copy-done.13, ...), custom_call_target="tpu_custom_call" | custom-call | flops 1 | bytes 1 | tf_op jit(solution)/shard_map/join/pallas_call | solution.py:187
  102.4 2.6 %pick.10 = (bf16[512,1024]{1,0:T(8,128)(2,1)}, bf16[512,1024]{1,0:T(8,128)(2,1)}, f32[8,128]{1,0:T(8,128)}) custom-call(s32[1]{0:T(128)} %bitcast.1.me_ref, bf16[1,1792,4096]{2,1,0:T(8,128)(2,1)} %refs_0_.21, bf16[1,1792,4096]{2,1,0:T(8,128)(2,1)} %refs_0_.21, f32[8,128]{1,0:T(8,128)} %get-tuple-element.79.refs_2_), custom_call_target="tpu_custom_call" | custom-call | flops 1 | bytes 1 | tf_op jit(solution)/shard_map/pick/pallas_call | solution.py:63
  106.0 15.8 %policy_products.1 = (f32[128,1792]{1,0:T(8,128)}, f32[128,1792]{1,0:T(8,128)}, bf16[128,4096]{1,0:T(8,128)(2,1)}, f32[8,128]{1,0:T(8,128)}) custom-call(bf16[8,8,16,1024]{3,2,1,0:T(8,128)(2,1)} %bitcast.30, bf16[1,1792,4096]{2,1,0:T(8,128)(2,1)} %refs_0_.21, bf16[1,1792,4096]{2,1,0:T(8,128)(2,1)} %w_up_ref.1, f32[8,128]{1,0:T(8,128)} %get-tuple-element.80.refs_0_), custom_call_target="tpu_custom_call" | custom-call | flops 1 | bytes 1 | tf_op jit(solution)/shard_map/policy_products/pallas_call | solution.py:226
  121.9 10.2 %outer_update.5 = (bf16[1792,1024]{1,0:T(8,128)(2,1)}, f32[1792,1024]{1,0:T(8,128)}, f32[8,128]{1,0:T(8,128)}) custom-call(s32[1]{0:T(128)} %bitcast.1.me_ref, bf16[1792,1024]{1,0:T(8,128)(2,1)} %outer_ref.9, f32[1792,1024]{1,0:T(8,128)} %moment_ref.9, bf16[1,1792,4096]{2,1,0:T(8,128)(2,1)} %refs_0_.21, bf16[1280,1024]{1,0:T(8,128)(2,1)} %copy-done, ...), custom_call_target="tpu_custom_call" | custom-call | flops 1 | bytes 1 | tf_op jit(solution)/shard_map/outer_update/pallas_call | solution.py:350
  132.1 1.7 collective-permute-done.10
  133.8 2.3 %fusion.3 = (f32[128]{0:T(128)S(1)}, f32[128]{0:T(128)S(1)}) fusion(bf16[128,1792]{1,0:T(8,128)(2,1)S(1)} %copy-done.7, bf16[128,1792]{1,0:T(8,128)(2,1)} %collective-permute-done.10, f32[128,1792]{1,0:T(8,128)} %get-tuple-element.85, bf16[128,1792]{1,0:T(8,128)(2,1)S(1)} %copy-done.6, bf16[128,1792]{1,0:T(8,128)(2,1)} %collective-permute-done.9, ...), kind=kLoop, calls=%fused_computation.8 | loop fusion | flops 6192896 | bytes 5964800 | tf_op jit(solution)/shard_map/reduce_sum | solution.py:29
  136.5 1.6 collective-permute-start.11
  138.1 2.4 %pick.11 = (bf16[256,1024]{1,0:T(8,128)(2,1)}, bf16[256,1024]{1,0:T(8,128)(2,1)}, bf16[256,1024]{1,0:T(8,128)(2,1)}, f32[8,128]{1,0:T(8,128)}) custom-call(s32[1]{0:T(128)} %bitcast.1.me_ref, bf16[1,1792,4096]{2,1,0:T(8,128)(2,1)} %refs_0_.21, bf16[1,1792,4096]{2,1,0:T(8,128)(2,1)} %refs_0_.21, bf16[1,1792,4096]{2,1,0:T(8,128)(2,1)} %refs_0_.21, ...), custom_call_target="tpu_custom_call" | custom-call | flops 1 | bytes 1 | tf_op jit(solution)/shard_map/pick/pallas_call | solution.py:63
  142.1 1.6 collective-permute-start.12
  143.7 2.0 collective-permute-done.12
  145.7 2.6 %collective-permute-start.13 = (f32[8]{0:T(128)S(1)}, f32[8]{0:T(128)S(1)}, u32[]{:S(2)}, u32[]{:S(2)}) collective-permute-start(f32[8]{0:T(128)S(1)} %add.42), channel_id=1, source_target_pairs={{0,4},{1,5},{2,6},{3,7},{4,0},{5,1},{6,2},{7,3},{8,12},{9,13},{10,... | collective-permute-start | bytes 104 | tf_op jit(solution)/shard_map/ppermute | solution.py:439
  148.3 1.9 collective-permute-done.13
  152.2 12.7 %weight_grads.1 = (bf16[1,1792,4096]{2,1,0:T(8,128)(2,1)}, bf16[1,1792,4096]{2,1,0:T(8,128)(2,1)}, f32[8,128]{1,0:T(8,128)}) custom-call(f32[128,1792]{1,0:T(8,128)} %get-tuple-element.81.gate_ref, f32[128,1792]{1,0:T(8,128)} %get-tuple-element.82.up_ref, bf16[128,1792]{1,0:T(8,128)(2,1)} %readout_ref.1, f32[128,1]{1,0:T(8,128)} %copy.23.token_grad_ref, ...), custom_call_target="tpu_custom_call" | custom-call | flops 1 | bytes 1 | tf_op jit(solution)/shard_map/weight_grads/pallas_call | solution.py:278
  164.9 2.0 pick.12
  169.1 7.2 %outer_update.6 = (bf16[1792,1024]{1,0:T(8,128)(2,1)}, f32[1792,1024]{1,0:T(8,128)}, f32[8,128]{1,0:T(8,128)}) custom-call(s32[1]{0:T(128)} %bitcast.1.me_ref, bf16[1792,1024]{1,0:T(8,128)(2,1)} %outer_ref.9, f32[1792,1024]{1,0:T(8,128)} %moment_ref.9, bf16[1,1792,4096]{2,1,0:T(8,128)(2,1)} %refs_0_.21, ...), custom_call_target="tpu_custom_call", output_to_operand_aliasing={{0}: (7, {}), {1}: (8, {})} | custom-call | flops 1 | bytes 1 | tf_op jit(solution)/shard_map/outer_update/pallas_call | solution.py:350
  176.3 2.1 pick.13
  181.8 4.4 %outer_update.7 = (bf16[1792,1024]{1,0:T(8,128)(2,1)}, f32[1792,1024]{1,0:T(8,128)}, f32[8,128]{1,0:T(8,128)}) custom-call(s32[1]{0:T(128)} %bitcast.1.me_ref, bf16[1792,1024]{1,0:T(8,128)(2,1)} %outer_ref.9, f32[1792,1024]{1,0:T(8,128)} %moment_ref.9, bf16[1,1792,4096]{2,1,0:T(8,128)(2,1)} %refs_0_.21, ...), custom_call_target="tpu_custom_call", output_to_operand_aliasing={{0}: (7, {}), {1}: (8, {})} | custom-call | flops 1 | bytes 1 | tf_op jit(solution)/shard_map/outer_update/pallas_call | solution.py:350
  186.2 2.3 %collective-permute-done.22.refs_3_ = bf16[128,1024]{1,0:T(8,128)(2,1)S(1)} collective-permute-done((bf16[128,1024]{1,0:T(8,128)(2,1)S(1)}, bf16[128,1024]{1,0:T(8,128)(2,1)S(1)}, u32[]{:S(2)}, u32[]{:S(2)}) %collective-permute-start.22) | collective-permute-done | bytes 262176 | tf_op jit(solution)/shard_map/ppermute | solution.py:378
  189.2 3.3 %outer_update.8 = (bf16[1792,1024]{1,0:T(8,128)(2,1)}, f32[1792,1024]{1,0:T(8,128)}, f32[8,128]{1,0:T(8,128)}) custom-call(s32[1]{0:T(128)} %bitcast.1.me_ref, bf16[1792,1024]{1,0:T(8,128)(2,1)} %outer_ref.9, f32[1792,1024]{1,0:T(8,128)} %moment_ref.9, bf16[1,1792,4096]{2,1,0:T(8,128)(2,1)} %refs_0_.21, ...), custom_call_target="tpu_custom_call", output_to_operand_aliasing={{0}: (7, {}), {1}: (8, {})} | custom-call | flops 1 | bytes 1 | tf_op jit(solution)/shard_map/outer_update/pallas_call | solution.py:350
  192.5 3.0 %collective-permute-done.18.refs_2_ = bf16[128,1024]{1,0:T(8,128)(2,1)S(1)} collective-permute-done((bf16[128,1024]{1,0:T(8,128)(2,1)}, bf16[128,1024]{1,0:T(8,128)(2,1)S(1)}, u32[]{:S(2)}, u32[]{:S(2)}) %collective-permute-start.18) | collective-permute-done | bytes 262176 | tf_op jit(solution)/shard_map/ppermute | solution.py:378
  195.5 4.2 %collective-permute-done.19.refs_3_ = bf16[128,1024]{1,0:T(8,128)(2,1)S(1)} collective-permute-done((bf16[128,1024]{1,0:T(8,128)(2,1)}, bf16[128,1024]{1,0:T(8,128)(2,1)S(1)}, u32[]{:S(2)}, u32[]{:S(2)}) %collective-permute-start.19) | collective-permute-done | bytes 262176 | tf_op jit(solution)/shard_map/ppermute | solution.py:378
  200.4 3.3 %outer_update.9 = (bf16[1792,1024]{1,0:T(8,128)(2,1)}, f32[1792,1024]{1,0:T(8,128)}, f32[8,128]{1,0:T(8,128)}) custom-call(s32[1]{0:T(128)} %bitcast.1.me_ref, bf16[1792,1024]{1,0:T(8,128)(2,1)} %outer_ref.9, f32[1792,1024]{1,0:T(8,128)} %moment_ref.9, bf16[1,1792,4096]{2,1,0:T(8,128)(2,1)} %refs_0_.21, ...), custom_call_target="tpu_custom_call", output_to_operand_aliasing={{0}: (7, {}), {1}: (8, {})} | custom-call | flops 1 | bytes 1 | tf_op jit(solution)/shard_map/outer_update/pallas_call | solution.py:350
  (118 shorter events, 24.3 us)
Async XLA Ops:
  7.2 73.2 %all-gather.3.cloned.1.call-start = ((), (), s32[]{:S(2)}) async-start(), calls=%async_computation | async-start | bytes 2359296 | tf_op jit(solution)/shard_map/all_gather | solution.py:407
  11.6 3.1 %collective-permute-start = (bf16[16,1024]{1,0:T(8,128)(2,1)}, bf16[16,1024]{1,0:T(8,128)(2,1)S(1)}, u32[]{:S(2)}, u32[]{:S(2)}) collective-permute-start(bf16[16,1024]{1,0:T(8,128)(2,1)} %get-tuple-element.64), channel_id=1, source_target_pairs={{0,8},{8,0},{16,24},{24,16},{1,9},{9,1},{17,25},{25,17},{2,10},{10... | collective-permute-start | bytes 98312 | tf_op jit(solution)/shard_map/ppermute | solution.py:378
  12.0 4.8 %collective-permute-start.1 = (bf16[16,1024]{1,0:T(8,128)(2,1)}, bf16[16,1024]{1,0:T(8,128)(2,1)S(1)}, u32[]{:S(2)}, u32[]{:S(2)}) collective-permute-start(bf16[16,1024]{1,0:T(8,128)(2,1)} %get-tuple-element.65), channel_id=1, source_target_pairs={{0,16},{8,24},{16,0},{24,8},{1,17},{9,25},{17,1},{25,9},{2,18},{10... | collective-permute-start | bytes 98312 | tf_op jit(solution)/shard_map/ppermute | solution.py:378
  14.5 3.6 %collective-permute-start.2 = (bf16[16,1024]{1,0:T(8,128)(2,1)}, bf16[16,1024]{1,0:T(8,128)(2,1)S(1)}, u32[]{:S(2)}, u32[]{:S(2)}) collective-permute-start(bf16[16,1024]{1,0:T(8,128)(2,1)} %get-tuple-element.66), channel_id=1, source_target_pairs={{0,24},{8,16},{16,8},{24,0},{1,25},{9,17},{17,9},{25,1},{2,26},{10... | collective-permute-start | bytes 98312 | tf_op jit(solution)/shard_map/ppermute | solution.py:378
  20.3 60.0 %collective-permute-start.4 = (bf16[1280,1024]{1,0:T(8,128)(2,1)}, bf16[1280,1024]{1,0:T(8,128)(2,1)S(1)}, u32[]{:S(2)}, u32[]{:S(2)}) collective-permute-start(bf16[1280,1024]{1,0:T(8,128)(2,1)} %get-tuple-element.72), channel_id=1, source_target_pairs={{0,16},{8,24},{16,0},{24,8},{1,17},{9,25},{17,1},{25,9},{2,18},{10... | collective-permute-start | bytes 7864328 | tf_op jit(solution)/shard_map/ppermute | solution.py:378
  24.4 3.8 %collective-permute-start.3 = (bf16[768,1024]{1,0:T(8,128)(2,1)}, bf16[768,1024]{1,0:T(8,128)(2,1)}, u32[]{:S(2)}, u32[]{:S(2)}) collective-permute-start(bf16[768,1024]{1,0:T(8,128)(2,1)} %get-tuple-element.71), channel_id=1, source_target_pairs={{0,8},{8,0},{16,24},{24,16},{1,9},{9,1},{17,25},{25,17},{2,10},{10... | collective-permute-start | bytes 4718600 | tf_op jit(solution)/shard_map/ppermute | solution.py:378
  24.4 97.4 %collective-permute-start.14 = (bf16[768,1024]{1,0:T(8,128)(2,1)}, bf16[768,1024]{1,0:T(8,128)(2,1)}, u32[]{:S(2)}, u32[]{:S(2)}) collective-permute-start(bf16[768,1024]{1,0:T(8,128)(2,1)} %get-tuple-element.88), channel_id=1, source_target_pairs={{0,24},{8,16},{16,8},{24,0},{1,25},{9,17},{17,9},{25,1},{2,26},{10... | collective-permute-start | bytes 4718600 | tf_op jit(solution)/shard_map/ppermute | solution.py:378
  91.7 2.1 collective-permute-start.5
  91.8 2.7 %collective-permute-start.6 = (bf16[128,1792]{1,0:T(8,128)(2,1)}, bf16[128,1792]{1,0:T(8,128)(2,1)S(1)}, u32[]{:S(2)}, u32[]{:S(2)}) collective-permute-start(bf16[128,1792]{1,0:T(8,128)(2,1)} %get-tuple-element.76), channel_id=1, source_target_pairs={{0,8},{8,0},{16,24},{24,16},{1,9},{9,1},{17,25},{25,17},{2,10},{10... | collective-permute-start | bytes 1376264 | tf_op jit(solution)/shard_map/ppermute | solution.py:378
  92.3 2.8 %collective-permute-start.7 = (bf16[128,1792]{1,0:T(8,128)(2,1)}, bf16[128,1792]{1,0:T(8,128)(2,1)S(1)}, u32[]{:S(2)}, u32[]{:S(2)}) collective-permute-start(bf16[128,1792]{1,0:T(8,128)(2,1)} %get-tuple-element.77), channel_id=1, source_target_pairs={{0,8},{8,0},{16,24},{24,16},{1,9},{9,1},{17,25},{25,17},{2,10},{10... | collective-permute-start | bytes 1376264 | tf_op jit(solution)/shard_map/ppermute | solution.py:378
  92.4 3.4 %collective-permute-start.8 = (bf16[128,1792]{1,0:T(8,128)(2,1)}, bf16[128,1792]{1,0:T(8,128)(2,1)S(1)}, u32[]{:S(2)}, u32[]{:S(2)}) collective-permute-start(bf16[128,1792]{1,0:T(8,128)(2,1)} %get-tuple-element.78), channel_id=1, source_target_pairs={{0,8},{8,0},{16,24},{24,16},{1,9},{9,1},{17,25},{25,17},{2,10},{10... | collective-permute-start | bytes 1376264 | tf_op jit(solution)/shard_map/ppermute | solution.py:378
  99.2 32.9 %collective-permute-start.9 = (bf16[128,1792]{1,0:T(8,128)(2,1)}, bf16[128,1792]{1,0:T(8,128)(2,1)}, u32[]{:S(2)}, u32[]{:S(2)}) collective-permute-start(bf16[128,1792]{1,0:T(8,128)(2,1)} %get-tuple-element.84), channel_id=1, source_target_pairs={{0,16},{8,24},{16,0},{24,8},{1,17},{9,25},{17,1},{25,9},{2,18},{10... | collective-permute-start | bytes 1376264 | tf_op jit(solution)/shard_map/ppermute | solution.py:378
  100.0 33.8 %collective-permute-start.10 = (bf16[128,1792]{1,0:T(8,128)(2,1)}, bf16[128,1792]{1,0:T(8,128)(2,1)}, u32[]{:S(2)}, u32[]{:S(2)}) collective-permute-start(bf16[128,1792]{1,0:T(8,128)(2,1)} %get-tuple-element.86), channel_id=1, source_target_pairs={{0,16},{8,24},{16,0},{24,8},{1,17},{9,25},{17,1},{25,9},{2,18},{10... | collective-permute-start | bytes 1376264 | tf_op jit(solution)/shard_map/ppermute | solution.py:378
  105.1 61.9 %collective-permute-start.15 = (bf16[512,1024]{1,0:T(8,128)(2,1)}, bf16[512,1024]{1,0:T(8,128)(2,1)}, u32[]{:S(2)}, u32[]{:S(2)}) collective-permute-start(bf16[512,1024]{1,0:T(8,128)(2,1)} %get-tuple-element.94), channel_id=1, source_target_pairs={{0,8},{8,0},{16,24},{24,16},{1,9},{9,1},{17,25},{25,17},{2,10},{10... | collective-permute-start | bytes 3145736 | tf_op jit(solution)/shard_map/ppermute | solution.py:378
  105.1 63.1 %collective-permute-start.16 = (bf16[512,1024]{1,0:T(8,128)(2,1)}, bf16[512,1024]{1,0:T(8,128)(2,1)}, u32[]{:S(2)}, u32[]{:S(2)}) collective-permute-start(bf16[512,1024]{1,0:T(8,128)(2,1)} %get-tuple-element.95), channel_id=1, source_target_pairs={{0,24},{8,16},{16,8},{24,0},{1,25},{9,17},{17,9},{25,1},{2,26},{10... | collective-permute-start | bytes 3145736 | tf_op jit(solution)/shard_map/ppermute | solution.py:378
  121.8 12.0 %copy-start.1 = (f32[128,1792]{1,0:T(8,128)S(1)}, f32[128,1792]{1,0:T(8,128)}, u32[]{:S(2)}) copy-start(f32[128,1792]{1,0:T(8,128)} %get-tuple-element.81.gate_ref) | copy-start | bytes 2752516
  121.9 11.9 %copy-start.2 = (f32[128,1792]{1,0:T(8,128)S(1)}, f32[128,1792]{1,0:T(8,128)}, u32[]{:S(2)}) copy-start(f32[128,1792]{1,0:T(8,128)} %get-tuple-element.82.up_ref) | copy-start | bytes 2752516
  136.5 4.9 %collective-permute-start.11 = (f32[8]{0:T(128)S(1)}, f32[8]{0:T(128)S(1)}, u32[]{:S(2)}, u32[]{:S(2)}) collective-permute-start(f32[8]{0:T(128)S(1)} %sub.19), channel_id=1, source_target_pairs={{0,1},{1,0},{2,3},{3,2},{4,5},{5,4},{6,7},{7,6},{8,9},{9,8},{10,11... | collective-permute-start | bytes 104 | tf_op jit(solution)/shard_map/ppermute | solution.py:439
  138.1 12.0 %copy-start.28 = (s32[1,4]{1,0:T(1,128)S(1)}, s32[1,4]{1,0:T(1,128)}, u32[]{:S(2)}) copy-start(s32[1,4]{1,0:T(1,128)} %slice.7) | copy-start | bytes 52
  138.1 12.2 %copy-start.29 = (s32[1,4]{1,0:T(1,128)S(1)}, s32[1,4]{1,0:T(1,128)}, u32[]{:S(2)}) copy-start(s32[1,4]{1,0:T(1,128)} %slice.6) | copy-start | bytes 52
  138.1 13.3 %copy-start.25 = (s32[128]{0:T(128)S(1)}, s32[128]{0:T(128)}, u32[]{:S(2)}) copy-start(s32[128]{0:T(128)} %param.11) | copy-start | bytes 1540
  140.5 38.4 %collective-permute-start.23 = (bf16[256,1024]{1,0:T(8,128)(2,1)}, bf16[256,1024]{1,0:T(8,128)(2,1)S(1)}, u32[]{:S(2)}, u32[]{:S(2)}) collective-permute-start(bf16[256,1024]{1,0:T(8,128)(2,1)} %get-tuple-element.107), channel_id=1, source_target_pairs={{0,8},{8,0},{16,24},{24,16},{1,9},{9,1},{17,25},{25,17},{2,10},{10... | collective-permute-start | bytes 1572872 | tf_op jit(solution)/shard_map/ppermute | solution.py:378
  140.5 39.2 %collective-permute-start.24 = (bf16[256,1024]{1,0:T(8,128)(2,1)}, bf16[256,1024]{1,0:T(8,128)(2,1)S(1)}, u32[]{:S(2)}, u32[]{:S(2)}) collective-permute-start(bf16[256,1024]{1,0:T(8,128)(2,1)} %get-tuple-element.108), channel_id=1, source_target_pairs={{0,16},{8,24},{16,0},{24,8},{1,17},{9,25},{17,1},{25,9},{2,18},{10... | collective-permute-start | bytes 1572872 | tf_op jit(solution)/shard_map/ppermute | solution.py:378
  142.1 3.5 %collective-permute-start.12 = (f32[8]{0:T(128)S(1)}, f32[8]{0:T(128)S(1)}, u32[]{:S(2)}, u32[]{:S(2)}) collective-permute-start(f32[8]{0:T(128)S(1)} %add.41), channel_id=1, source_target_pairs={{0,2},{1,3},{2,0},{3,1},{4,6},{5,7},{6,4},{7,5},{8,10},{9,11},{10,... | collective-permute-start | bytes 104 | tf_op jit(solution)/shard_map/ppermute | solution.py:439
  145.7 4.4 %collective-permute-start.13 = (f32[8]{0:T(128)S(1)}, f32[8]{0:T(128)S(1)}, u32[]{:S(2)}, u32[]{:S(2)}) collective-permute-start(f32[8]{0:T(128)S(1)} %add.42), channel_id=1, source_target_pairs={{0,4},{1,5},{2,6},{3,7},{4,0},{5,1},{6,2},{7,3},{8,12},{9,13},{10,... | collective-permute-start | bytes 104 | tf_op jit(solution)/shard_map/ppermute | solution.py:439
  150.1 30.5 %collective-permute-start.25 = (bf16[256,1024]{1,0:T(8,128)(2,1)}, bf16[256,1024]{1,0:T(8,128)(2,1)S(1)}, u32[]{:S(2)}, u32[]{:S(2)}) collective-permute-start(bf16[256,1024]{1,0:T(8,128)(2,1)} %get-tuple-element.109), channel_id=1, source_target_pairs={{0,24},{8,16},{16,8},{24,0},{1,25},{9,17},{17,9},{25,1},{2,26},{10... | collective-permute-start | bytes 1572872 | tf_op jit(solution)/shard_map/ppermute | solution.py:378
  167.0 11.4 %collective-permute-start.20 = (bf16[128,1024]{1,0:T(8,128)(2,1)}, bf16[128,1024]{1,0:T(8,128)(2,1)S(1)}, u32[]{:S(2)}, u32[]{:S(2)}) collective-permute-start(bf16[128,1024]{1,0:T(8,128)(2,1)} %get-tuple-element.104), channel_id=1, source_target_pairs={{0,8},{8,0},{16,24},{24,16},{1,9},{9,1},{17,25},{25,17},{2,10},{10... | collective-permute-start | bytes 786440 | tf_op jit(solution)/shard_map/ppermute | solution.py:378
  168.2 18.0 %collective-permute-start.21 = (bf16[128,1024]{1,0:T(8,128)(2,1)}, bf16[128,1024]{1,0:T(8,128)(2,1)S(1)}, u32[]{:S(2)}, u32[]{:S(2)}) collective-permute-start(bf16[128,1024]{1,0:T(8,128)(2,1)} %get-tuple-element.105), channel_id=1, source_target_pairs={{0,16},{8,24},{16,0},{24,8},{1,17},{9,25},{17,1},{25,9},{2,18},{10... | collective-permute-start | bytes 786440 | tf_op jit(solution)/shard_map/ppermute | solution.py:378
  178.4 10.1 %collective-permute-start.22 = (bf16[128,1024]{1,0:T(8,128)(2,1)S(1)}, bf16[128,1024]{1,0:T(8,128)(2,1)S(1)}, u32[]{:S(2)}, u32[]{:S(2)}) collective-permute-start(bf16[128,1024]{1,0:T(8,128)(2,1)S(1)} %copy-done.26), channel_id=1, source_target_pairs={{0,24},{8,16},{16,8},{24,0},{1,25},{9,17},{17,9},{25,1},{2,26},{10... | collective-permute-start | bytes 786440 | tf_op jit(solution)/shard_map/ppermute | solution.py:378
  179.0 13.5 %collective-permute-start.17 = (bf16[128,1024]{1,0:T(8,128)(2,1)}, bf16[128,1024]{1,0:T(8,128)(2,1)S(1)}, u32[]{:S(2)}, u32[]{:S(2)}) collective-permute-start(bf16[128,1024]{1,0:T(8,128)(2,1)} %get-tuple-element.101), channel_id=1, source_target_pairs={{0,8},{8,0},{16,24},{24,16},{1,9},{9,1},{17,25},{25,17},{2,10},{10... | collective-permute-start | bytes 786440 | tf_op jit(solution)/shard_map/ppermute | solution.py:378
  179.7 15.8 %collective-permute-start.18 = (bf16[128,1024]{1,0:T(8,128)(2,1)}, bf16[128,1024]{1,0:T(8,128)(2,1)S(1)}, u32[]{:S(2)}, u32[]{:S(2)}) collective-permute-start(bf16[128,1024]{1,0:T(8,128)(2,1)} %get-tuple-element.102), channel_id=1, source_target_pairs={{0,16},{8,24},{16,0},{24,8},{1,17},{9,25},{17,1},{25,9},{2,18},{10... | collective-permute-start | bytes 786440 | tf_op jit(solution)/shard_map/ppermute | solution.py:378
  180.6 19.1 %collective-permute-start.19 = (bf16[128,1024]{1,0:T(8,128)(2,1)}, bf16[128,1024]{1,0:T(8,128)(2,1)S(1)}, u32[]{:S(2)}, u32[]{:S(2)}) collective-permute-start(bf16[128,1024]{1,0:T(8,128)(2,1)} %get-tuple-element.103), channel_id=1, source_target_pairs={{0,24},{8,16},{16,8},{24,0},{1,25},{9,17},{17,9},{25,1},{2,26},{10... | collective-permute-start | bytes 786440 | tf_op jit(solution)/shard_map/ppermute | solution.py:378
  (25 other events, 105.7 us)
Sparse Core Ops, SparseCore 0:
  20.5 49.9 all-gather.2

commit v7 on v6

--- a/solution.py
+++ b/solution.py
@@ -398,14 +398,15 @@
             first, steps, tile, place, outer_gate, moment, w_gate, there, updated, *after
         )
 
-    early, token = send(0, 10, (2,))
+    first, token = send(0, 2, (2,))
     shares, token = pick(
         0, 1, tokens.shape[0], place, tokens[None], tuple(range(1, groups)), width, token
     )
     others = [swap(share, bits) for bits, share in enumerate(shares, 1)]
-    assembled, token = assemble(place, tokens, others, token)
+    assembled, token = assemble(place, tokens, others, token, *first)
+    early, token = send(2, 8, (2,), token)
     gathered = lax.all_gather(assembled, "fsdp", axis=0, tiled=False)
-    (near, _), token = send(0, 6, (1, 3), token)
+    (near, _), token = send(0, 4, (1, 3), token)
 
     *parts, token = partial_products(gathered, outer_gate, outer_up, token, near, *early)
     for at in (1, 3, 5, 7):
@@ -421,9 +422,10 @@
             (stay_up, near_up, leave_up),
         )
     )
-    _, token = send(6, 4, (1, 3), token)
+    _, token = send(4, 6, (1, 3), token)
     gate, upper, inputs, token = policy_products(gathered, w_gate, w_up, token)
-    updated, token = update(0, 6, token)
+    updated, token = update(0, 2, token)
+    updated, token = update(2, 2, token)
 
     group_tok = inputs.shape[0]
     seqs = group_tok // LEN
@@ -454,7 +456,7 @@
     token_grad = jnp.broadcast_to(coef[:, None], (seqs, LEN)).reshape(-1) * mask_f
     grad_gate, grad_up, token = weight_grads(gate, upper, readout, token_grad, inputs, token)
     _, token = send(12, 1, (1, 2, 3), token)
-    updated, token = update(6, 4, token)
+    updated, token = update(4, 6, token)
     _, token = send(13, 1, (1, 2, 3), token)
     updated, token = update(10, 2, token)
     updated, token = update(12, 1, token)

time: 213 us -> 213 us (level)
  waiting for transfers between devices: 76.1 us -> 68.4 us
  Pallas kernels: 87.6 us -> 93 us
  starting transfers between devices: 21 us -> 23.5 us
    ppermute x23 -> x24, waiting for transfers between devices: 72.2 us -> 64.6 us  [swap(): return lax.ppermute(value, 'rep', [(i, i ^ bits) for i in range(groups)])]
    pallas_call x7 -> x8, Pallas kernels: 16.6 us -> 20.4 us  [pick(): pl.pallas_call(functools.partial(pick_kernel, count), grid_spec=pltpu.Pre...]
    ppermute x23 -> x24, starting transfers between devices: 15.2 us -> 17.7 us  [swap(): return lax.ppermute(value, 'rep', [(i, i ^ bits) for i in range(groups)])]
    pallas_call x5 -> x6, Pallas kernels: 28.3 us -> 29.8 us  [outer_update(): pl.pallas_call(functools.partial(outer_kernel, groups, strip), grid_spec=...]
    unnamed x60 -> x64, local copies, waits for them, and re-layouts: 4.37 us -> 4.39 us
  transfers between devices with their start and end apart: 27 -> 28, of which waited for: 14 -> 12; matrix products, arithmetic and copies ran while one was open for 3% -> 3% of each run, Pallas kernels for 37% -> 41%
where the time goes in v7:
time: 213 us; the launch traced here: 212 us
  Pallas kernels  93 us (44%)
  waiting for transfers between devices  68.4 us (32%)
  starting transfers between devices  23.5 us (11%)
  between operations  16.1 us (8%)
  local copies, waits for them, and re-layouts  6.67 us (3%)
  other arithmetic  3.19 us (1%)
    ppermute x24, waiting for transfers between devices, swap(): return lax.ppermute(value, 'rep', [(i, i ^ bits) for i in range(groups)])  64.6 us
    pallas_call x6, Pallas kernels, outer_update(): pl.pallas_call(functools.partial(outer_kernel, groups, strip), grid_spec=...  29.8 us
    pallas_call x8, Pallas kernels, pick(): pl.pallas_call(functools.partial(pick_kernel, count), grid_spec=pltpu.Pre...  20.4 us
    ppermute x24, starting transfers between devices, swap(): return lax.ppermute(value, 'rep', [(i, i ^ bits) for i in range(groups)])  17.7 us
    pallas_call x1, Pallas kernels, policy_products(): pl.pallas_call(policy_kernel, grid=(unit_rows // tile,), in_specs=[pl.Blo...  15.8 us
    pallas_call x1, Pallas kernels, weight_grads(): pl.pallas_call(grads_kernel, grid=(unit_rows // tile,), in_specs=[units,...  12.7 us
    pallas_call x1, Pallas kernels, partial_products(): pl.pallas_call(partial_kernel, grid=(unit_rows // tile,), in_specs=[pl.Bl...  9.91 us
    ppermute x3, starting transfers between devices, per_device(): lax.ppermute(relative, 'fsdp', [(i, i ^ hop) for i in range(ranks)])  5.74 us
  transfers between devices with their start and end apart: 28, of which 12 were waited for; matrix products, arithmetic and copies ran while one was open for 3% of the time, Pallas kernels for 41%

profile of v7, /device:TPU:0, one launch (start us, length us, event | category | flops | bytes accessed | tf_op | source)
XLA Modules:
  0.0 212.1 jit_solution(8205155402837265367)
XLA Ops:
  7.2 1.8 pick.8
  9.0 2.9 %collective-permute-start.3 = (bf16[256,1024]{1,0:T(8,128)(2,1)}, bf16[256,1024]{1,0:T(8,128)(2,1)S(1)}, u32[]{:S(2)}, u32[]{:S(2)}) collective-permute-start(bf16[256,1024]{1,0:T(8,128)(2,1)} %get-tuple-element.73), channel_id=1, source_target_pairs={{0,16},{8,24},{16,0},{24,8},{1,17},{9,25},{17,1},{25,9},{2,18},{10... | collective-permute-start | bytes 1572872 | tf_op jit(solution)/shard_map/ppermute | solution.py:378
  13.4 1.9 collective-permute-start.2
  15.2 9.9 %collective-permute-done.1.refs_1_ = bf16[16,1024]{1,0:T(8,128)(2,1)S(1)} collective-permute-done((bf16[16,1024]{1,0:T(8,128)(2,1)}, bf16[16,1024]{1,0:T(8,128)(2,1)S(1)}, u32[]{:S(2)}, u32[]{:S(2)}) %collective-permute-start.1) | collective-permute-done | bytes 32800 | tf_op jit(solution)/shard_map/ppermute | solution.py:378
  26.0 1.7 assemble.1
  27.7 3.8 %pick.10 = (bf16[1024,1024]{1,0:T(8,128)(2,1)}, f32[8,128]{1,0:T(8,128)}) custom-call(s32[1]{0:T(128)} %bitcast.1.me_ref, bf16[1,1792,4096]{2,1,0:T(8,128)(2,1)} %refs_0_.25, f32[8,128]{1,0:T(8,128)} %get-tuple-element.75.refs_1_), custom_call_target="tpu_custom_call" | custom-call | flops 1 | bytes 1 | tf_op jit(solution)/shard_map/pick/pallas_call | solution.py:63
  31.5 1.7 collective-permute-start.5
  33.2 2.6 %pick.11 = (bf16[512,1024]{1,0:T(8,128)(2,1)}, bf16[512,1024]{1,0:T(8,128)(2,1)}, f32[8,128]{1,0:T(8,128)}) custom-call(s32[1]{0:T(128)} %bitcast.1.me_ref, bf16[1,1792,4096]{2,1,0:T(8,128)(2,1)} %refs_0_.25, bf16[1,1792,4096]{2,1,0:T(8,128)(2,1)} %refs_0_.25, f32[8,128]{1,0:T(8,128)} %get-tuple-element.76.refs_2_), custom_call_target="tpu_custom_call" | custom-call | flops 1 | bytes 1 | tf_op jit(solution)/shard_map/pick/pallas_call | solution.py:63
  36.2 2.5 %collective-permute-done.4.refs_1_.refs_2_ = bf16[512,1024]{1,0:T(8,128)(2,1)S(1)} collective-permute-done((bf16[512,1024]{1,0:T(8,128)(2,1)}, bf16[512,1024]{1,0:T(8,128)(2,1)S(1)}, u32[]{:S(2)}, u32[]{:S(2)}) %collective-permute-start.4) | collective-permute-done | bytes 1048608 | tf_op jit(solution)/shard_map/ppermute | solution.py:378
  38.7 41.5 %collective-permute-done.5.refs_2_.refs_1_ = bf16[1024,1024]{1,0:T(8,128)(2,1)S(1)} collective-permute-done((bf16[1024,1024]{1,0:T(8,128)(2,1)}, bf16[1024,1024]{1,0:T(8,128)(2,1)S(1)}, u32[]{:S(2)}, u32[]{:S(2)}) %collective-permute-start.5) | collective-permute-done | bytes 2097184 | tf_op jit(solution)/shard_map/ppermute | solution.py:378
  81.5 9.9 %partial_products.1 = (f32[128,1792]{1,0:T(8,128)}, bf16[128,1792]{1,0:T(8,128)(2,1)}, f32[128,1792]{1,0:T(8,128)}, bf16[128,1792]{1,0:T(8,128)(2,1)}, f32[128,1...) custom-call(bf16[8,8,16,1024]{3,2,1,0:T(8,128)(2,1)} %bitcast.29, ...), custom_call_target="tpu_custom_call" | custom-call | flops 1 | bytes 1 | tf_op jit(solution)/shard_map/partial_products/pallas_call | solution.py:142
  96.2 2.7 %join.1 = (bf16[128,1792]{1,0:T(8,128)(2,1)}, bf16[128,1792]{1,0:T(8,128)(2,1)}, f32[8,128]{1,0:T(8,128)}) custom-call(f32[128,1792]{1,0:T(8,128)} %get-tuple-element.80.far_gate_ref, bf16[128,1792]{1,0:T(8,128)(2,1)} %copy-done.14, f32[128,1792]{1,0:T(8,128)} %get-tuple-element.82.far_up_ref, bf16[128,1792]{1,0:T(8,128)(2,1)} %copy-done.15, ...), custom_call_target="tpu_custom_call" | custom-call | flops 1 | bytes 1 | tf_op jit(solution)/shard_map/join/pallas_call | solution.py:187
  98.9 1.8 collective-permute-start.10
  100.9 4.3 %pick.12 = (bf16[768,1024]{1,0:T(8,128)(2,1)}, bf16[768,1024]{1,0:T(8,128)(2,1)}, f32[8,128]{1,0:T(8,128)}) custom-call(s32[1]{0:T(128)} %bitcast.1.me_ref, bf16[1,1792,4096]{2,1,0:T(8,128)(2,1)} %refs_0_.25, bf16[1,1792,4096]{2,1,0:T(8,128)(2,1)} %refs_0_.25, f32[8,128]{1,0:T(8,128)} %get-tuple-element.86.refs_2_), custom_call_target="tpu_custom_call" | custom-call | flops 1 | bytes 1 | tf_op jit(solution)/shard_map/pick/pallas_call | solution.py:63
  106.5 1.9 collective-permute-start.17
  108.4 15.8 %policy_products.1 = (f32[128,1792]{1,0:T(8,128)}, f32[128,1792]{1,0:T(8,128)}, bf16[128,4096]{1,0:T(8,128)(2,1)}, f32[8,128]{1,0:T(8,128)}) custom-call(bf16[8,8,16,1024]{3,2,1,0:T(8,128)(2,1)} %bitcast.30, bf16[1,1792,4096]{2,1,0:T(8,128)(2,1)} %refs_0_.25, bf16[1,1792,4096]{2,1,0:T(8,128)(2,1)} %w_up_ref.1, f32[8,128]{1,0:T(8,128)} %get-tuple-element.87.refs_0_), custom_call_target="tpu_custom_call" | custom-call | flops 1 | bytes 1 | tf_op jit(solution)/shard_map/policy_products/pallas_call | solution.py:226
  124.2 4.3 %outer_update.6 = (bf16[1792,1024]{1,0:T(8,128)(2,1)}, f32[1792,1024]{1,0:T(8,128)}, f32[8,128]{1,0:T(8,128)}) custom-call(s32[1]{0:T(128)} %bitcast.1.me_ref, bf16[1792,1024]{1,0:T(8,128)(2,1)} %outer_ref.11, f32[1792,1024]{1,0:T(8,128)} %moment_ref.11, bf16[1,1792,4096]{2,1,0:T(8,128)(2,1)} %refs_0_.25, bf16[256,1024]{1,0:T(8,128)(2,1)} %copy-done.4, ...), custom_call_target="tpu_custom_call" | custom-call | flops 1 | bytes 1 | tf_op jit(solution)/shard_map/outer_update/pallas_call | solution.py:350
  128.6 4.5 %outer_update.7 = (bf16[1792,1024]{1,0:T(8,128)(2,1)}, f32[1792,1024]{1,0:T(8,128)}, f32[8,128]{1,0:T(8,128)}) custom-call(s32[1]{0:T(128)} %bitcast.1.me_ref, bf16[1792,1024]{1,0:T(8,128)(2,1)} %outer_ref.11, f32[1792,1024]{1,0:T(8,128)} %moment_ref.11, bf16[1,1792,4096]{2,1,0:T(8,128)(2,1)} %refs_0_.25, ...), custom_call_target="tpu_custom_call", output_to_operand_aliasing={{0}: (7, {}), {1}: (8, {})} | custom-call | flops 1 | bytes 1 | tf_op jit(solution)/shard_map/outer_update/pallas_call | solution.py:350
  133.2 2.3 %fusion.3 = (f32[128]{0:T(128)S(1)}, f32[128]{0:T(128)S(1)}) fusion(bf16[128,1792]{1,0:T(8,128)(2,1)S(1)} %copy-done.9, bf16[128,1792]{1,0:T(8,128)(2,1)} %collective-permute-done.11, f32[128,1792]{1,0:T(8,128)} %get-tuple-element.92, bf16[128,1792]{1,0:T(8,128)(2,1)S(1)} %copy-done.8, bf16[128,1792]{1,0:T(8,128)(2,1)} %collective-permute-done.10, ...), kind=kLoop, calls=%fused_computation.8 | loop fusion | flops 6192896 | bytes 5964800 | tf_op jit(solution)/shard_map/reduce_sum | solution.py:29
  137.5 2.4 %pick.13 = (bf16[256,1024]{1,0:T(8,128)(2,1)}, bf16[256,1024]{1,0:T(8,128)(2,1)}, bf16[256,1024]{1,0:T(8,128)(2,1)}, f32[8,128]{1,0:T(8,128)}) custom-call(s32[1]{0:T(128)} %bitcast.1.me_ref, bf16[1,1792,4096]{2,1,0:T(8,128)(2,1)} %refs_0_.25, bf16[1,1792,4096]{2,1,0:T(8,128)(2,1)} %refs_0_.25, bf16[1,1792,4096]{2,1,0:T(8,128)(2,1)} %refs_0_.25, ...), custom_call_target="tpu_custom_call" | custom-call | flops 1 | bytes 1 | tf_op jit(solution)/shard_map/pick/pallas_call | solution.py:63
  142.6 2.0 collective-permute-done.13
  144.6 2.6 %collective-permute-start.14 = (f32[8]{0:T(128)S(1)}, f32[8]{0:T(128)S(1)}, u32[]{:S(2)}, u32[]{:S(2)}) collective-permute-start(f32[8]{0:T(128)S(1)} %add.42), channel_id=1, source_target_pairs={{0,4},{1,5},{2,6},{3,7},{4,0},{5,1},{6,2},{7,3},{8,12},{9,13},{10,... | collective-permute-start | bytes 104 | tf_op jit(solution)/shard_map/ppermute | solution.py:441
  147.2 1.9 collective-permute-done.14
  151.2 12.7 %weight_grads.1 = (bf16[1,1792,4096]{2,1,0:T(8,128)(2,1)}, bf16[1,1792,4096]{2,1,0:T(8,128)(2,1)}, f32[8,128]{1,0:T(8,128)}) custom-call(f32[128,1792]{1,0:T(8,128)} %get-tuple-element.88.gate_ref, f32[128,1792]{1,0:T(8,128)} %get-tuple-element.89.up_ref, bf16[128,1792]{1,0:T(8,128)(2,1)} %readout_ref.1, f32[128,1]{1,0:T(8,128)} %copy.25.token_grad_ref, ...), custom_call_target="tpu_custom_call" | custom-call | flops 1 | bytes 1 | tf_op jit(solution)/shard_map/weight_grads/pallas_call | solution.py:278
  163.8 2.0 pick.14
  168.0 10.0 %outer_update.8 = (bf16[1792,1024]{1,0:T(8,128)(2,1)}, f32[1792,1024]{1,0:T(8,128)}, f32[8,128]{1,0:T(8,128)}) custom-call(s32[1]{0:T(128)} %bitcast.1.me_ref, bf16[1792,1024]{1,0:T(8,128)(2,1)} %outer_ref.11, f32[1792,1024]{1,0:T(8,128)} %moment_ref.11, bf16[1,1792,4096]{2,1,0:T(8,128)(2,1)} %refs_0_.25, ...), custom_call_target="tpu_custom_call", output_to_operand_aliasing={{0}: (7, {}), {1}: (8, {})} | custom-call | flops 1 | bytes 1 | tf_op jit(solution)/shard_map/outer_update/pallas_call | solution.py:350
  178.0 2.1 %pick.15 = (bf16[128,1024]{1,0:T(8,128)(2,1)}, bf16[128,1024]{1,0:T(8,128)(2,1)}, bf16[128,1024]{1,0:T(8,128)(2,1)}, f32[8,128]{1,0:T(8,128)}) custom-call(s32[1]{0:T(128)} %bitcast.1.me_ref, bf16[1,1792,4096]{2,1,0:T(8,128)(2,1)} %refs_0_.25, bf16[1,1792,4096]{2,1,0:T(8,128)(2,1)} %refs_0_.25, bf16[1,1792,4096]{2,1,0:T(8,128)(2,1)} %refs_0_.25, ...), custom_call_target="tpu_custom_call" | custom-call | flops 1 | bytes 1 | tf_op jit(solution)/shard_map/pick/pallas_call | solution.py:63
  184.0 4.4 %outer_update.9 = (bf16[1792,1024]{1,0:T(8,128)(2,1)}, f32[1792,1024]{1,0:T(8,128)}, f32[8,128]{1,0:T(8,128)}) custom-call(s32[1]{0:T(128)} %bitcast.1.me_ref, bf16[1792,1024]{1,0:T(8,128)(2,1)} %outer_ref.11, f32[1792,1024]{1,0:T(8,128)} %moment_ref.11, bf16[1,1792,4096]{2,1,0:T(8,128)(2,1)} %refs_0_.25, ...), custom_call_target="tpu_custom_call", output_to_operand_aliasing={{0}: (7, {}), {1}: (8, {})} | custom-call | flops 1 | bytes 1 | tf_op jit(solution)/shard_map/outer_update/pallas_call | solution.py:350
  189.6 3.3 %outer_update.10 = (bf16[1792,1024]{1,0:T(8,128)(2,1)}, f32[1792,1024]{1,0:T(8,128)}, f32[8,128]{1,0:T(8,128)}) custom-call(s32[1]{0:T(128)} %bitcast.1.me_ref, bf16[1792,1024]{1,0:T(8,128)(2,1)} %outer_ref.11, f32[1792,1024]{1,0:T(8,128)} %moment_ref.11, bf16[1,1792,4096]{2,1,0:T(8,128)(2,1)} %refs_0_.25, ...), custom_call_target="tpu_custom_call", output_to_operand_aliasing={{0}: (7, {}), {1}: (8, {})} | custom-call | flops 1 | bytes 1 | tf_op jit(solution)/shard_map/outer_update/pallas_call | solution.py:350
  192.9 1.7 collective-permute-done.19.refs_2_
  194.6 5.6 %collective-permute-done.20.refs_3_ = bf16[128,1024]{1,0:T(8,128)(2,1)S(1)} collective-permute-done((bf16[128,1024]{1,0:T(8,128)(2,1)}, bf16[128,1024]{1,0:T(8,128)(2,1)S(1)}, u32[]{:S(2)}, u32[]{:S(2)}) %collective-permute-start.20) | collective-permute-done | bytes 262176 | tf_op jit(solution)/shard_map/ppermute | solution.py:378
  200.8 3.3 %outer_update.11 = (bf16[1792,1024]{1,0:T(8,128)(2,1)}, f32[1792,1024]{1,0:T(8,128)}, f32[8,128]{1,0:T(8,128)}) custom-call(s32[1]{0:T(128)} %bitcast.1.me_ref, bf16[1792,1024]{1,0:T(8,128)(2,1)} %outer_ref.11, f32[1792,1024]{1,0:T(8,128)} %moment_ref.11, bf16[1,1792,4096]{2,1,0:T(8,128)(2,1)} %refs_0_.25, ...), custom_call_target="tpu_custom_call", output_to_operand_aliasing={{0}: (7, {}), {1}: (8, {})} | custom-call | flops 1 | bytes 1 | tf_op jit(solution)/shard_map/outer_update/pallas_call | solution.py:350
  (126 shorter events, 24.5 us)
Async XLA Ops:
  7.2 73.0 %all-gather.3.cloned.1.call-start = ((), (), s32[]{:S(2)}) async-start(), calls=%async_computation | async-start | bytes 2359296 | tf_op jit(solution)/shard_map/all_gather | solution.py:408
  9.0 16.2 %collective-permute-start.3 = (bf16[256,1024]{1,0:T(8,128)(2,1)}, bf16[256,1024]{1,0:T(8,128)(2,1)S(1)}, u32[]{:S(2)}, u32[]{:S(2)}) collective-permute-start(bf16[256,1024]{1,0:T(8,128)(2,1)} %get-tuple-element.73), channel_id=1, source_target_pairs={{0,16},{8,24},{16,0},{24,8},{1,17},{9,25},{17,1},{25,9},{2,18},{10... | collective-permute-start | bytes 1572872 | tf_op jit(solution)/shard_map/ppermute | solution.py:378
  13.4 1.9 collective-permute-start
  13.4 11.8 %collective-permute-start.1 = (bf16[16,1024]{1,0:T(8,128)(2,1)}, bf16[16,1024]{1,0:T(8,128)(2,1)S(1)}, u32[]{:S(2)}, u32[]{:S(2)}) collective-permute-start(bf16[16,1024]{1,0:T(8,128)(2,1)} %get-tuple-element.70), channel_id=1, source_target_pairs={{0,16},{8,24},{16,0},{24,8},{1,17},{9,25},{17,1},{25,9},{2,18},{10... | collective-permute-start | bytes 98312 | tf_op jit(solution)/shard_map/ppermute | solution.py:378
  13.4 11.8 %collective-permute-start.2 = (bf16[16,1024]{1,0:T(8,128)(2,1)}, bf16[16,1024]{1,0:T(8,128)(2,1)S(1)}, u32[]{:S(2)}, u32[]{:S(2)}) collective-permute-start(bf16[16,1024]{1,0:T(8,128)(2,1)} %get-tuple-element.71), channel_id=1, source_target_pairs={{0,24},{8,16},{16,8},{24,0},{1,25},{9,17},{17,9},{25,1},{2,26},{10... | collective-permute-start | bytes 98312 | tf_op jit(solution)/shard_map/ppermute | solution.py:378
  31.5 48.7 %collective-permute-start.5 = (bf16[1024,1024]{1,0:T(8,128)(2,1)}, bf16[1024,1024]{1,0:T(8,128)(2,1)S(1)}, u32[]{:S(2)}, u32[]{:S(2)}) collective-permute-start(bf16[1024,1024]{1,0:T(8,128)(2,1)} %get-tuple-element.79), channel_id=1, source_target_pairs={{0,16},{8,24},{16,0},{24,8},{1,17},{9,25},{17,1},{25,9},{2,18},{10... | collective-permute-start | bytes 6291464 | tf_op jit(solution)/shard_map/ppermute | solution.py:378
  35.8 2.9 %collective-permute-start.4 = (bf16[512,1024]{1,0:T(8,128)(2,1)}, bf16[512,1024]{1,0:T(8,128)(2,1)S(1)}, u32[]{:S(2)}, u32[]{:S(2)}) collective-permute-start(bf16[512,1024]{1,0:T(8,128)(2,1)} %get-tuple-element.78), channel_id=1, source_target_pairs={{0,8},{8,0},{16,24},{24,16},{1,9},{9,1},{17,25},{25,17},{2,10},{10... | collective-permute-start | bytes 3145736 | tf_op jit(solution)/shard_map/ppermute | solution.py:378
  35.8 88.4 %collective-permute-start.15 = (bf16[512,1024]{1,0:T(8,128)(2,1)}, bf16[512,1024]{1,0:T(8,128)(2,1)}, u32[]{:S(2)}, u32[]{:S(2)}) collective-permute-start(bf16[512,1024]{1,0:T(8,128)(2,1)} %get-tuple-element.95), channel_id=1, source_target_pairs={{0,24},{8,16},{16,8},{24,0},{1,25},{9,17},{17,9},{25,1},{2,26},{10... | collective-permute-start | bytes 3145736 | tf_op jit(solution)/shard_map/ppermute | solution.py:378
  38.7 41.5 %copy-start.1 = (bf16[512,1024]{1,0:T(8,128)(2,1)}, bf16[512,1024]{1,0:T(8,128)(2,1)S(1)}, u32[]{:S(2)}) copy-start(bf16[512,1024]{1,0:T(8,128)(2,1)S(1)} %collective-permute-done.4.refs_1_.refs_2_) | copy-start | bytes 3145732
  91.4 2.1 collective-permute-start.6
  91.5 2.7 %collective-permute-start.7 = (bf16[128,1792]{1,0:T(8,128)(2,1)}, bf16[128,1792]{1,0:T(8,128)(2,1)S(1)}, u32[]{:S(2)}, u32[]{:S(2)}) collective-permute-start(bf16[128,1792]{1,0:T(8,128)(2,1)} %get-tuple-element.83), channel_id=1, source_target_pairs={{0,8},{8,0},{16,24},{24,16},{1,9},{9,1},{17,25},{25,17},{2,10},{10... | collective-permute-start | bytes 1376264 | tf_op jit(solution)/shard_map/ppermute | solution.py:378
  92.0 2.8 %collective-permute-start.8 = (bf16[128,1792]{1,0:T(8,128)(2,1)}, bf16[128,1792]{1,0:T(8,128)(2,1)S(1)}, u32[]{:S(2)}, u32[]{:S(2)}) collective-permute-start(bf16[128,1792]{1,0:T(8,128)(2,1)} %get-tuple-element.84), channel_id=1, source_target_pairs={{0,8},{8,0},{16,24},{24,16},{1,9},{9,1},{17,25},{25,17},{2,10},{10... | collective-permute-start | bytes 1376264 | tf_op jit(solution)/shard_map/ppermute | solution.py:378
  92.0 3.4 %collective-permute-start.9 = (bf16[128,1792]{1,0:T(8,128)(2,1)}, bf16[128,1792]{1,0:T(8,128)(2,1)S(1)}, u32[]{:S(2)}, u32[]{:S(2)}) collective-permute-start(bf16[128,1792]{1,0:T(8,128)(2,1)} %get-tuple-element.85), channel_id=1, source_target_pairs={{0,8},{8,0},{16,24},{24,16},{1,9},{9,1},{17,25},{25,17},{2,10},{10... | collective-permute-start | bytes 1376264 | tf_op jit(solution)/shard_map/ppermute | solution.py:378
  98.9 34.2 %collective-permute-start.10 = (bf16[128,1792]{1,0:T(8,128)(2,1)}, bf16[128,1792]{1,0:T(8,128)(2,1)}, u32[]{:S(2)}, u32[]{:S(2)}) collective-permute-start(bf16[128,1792]{1,0:T(8,128)(2,1)} %get-tuple-element.91), channel_id=1, source_target_pairs={{0,16},{8,24},{16,0},{24,8},{1,17},{9,25},{17,1},{25,9},{2,18},{10... | collective-permute-start | bytes 1376264 | tf_op jit(solution)/shard_map/ppermute | solution.py:378
  100.6 32.5 %collective-permute-start.11 = (bf16[128,1792]{1,0:T(8,128)(2,1)}, bf16[128,1792]{1,0:T(8,128)(2,1)}, u32[]{:S(2)}, u32[]{:S(2)}) collective-permute-start(bf16[128,1792]{1,0:T(8,128)(2,1)} %get-tuple-element.93), channel_id=1, source_target_pairs={{0,16},{8,24},{16,0},{24,8},{1,17},{9,25},{17,1},{25,9},{2,18},{10... | collective-permute-start | bytes 1376264 | tf_op jit(solution)/shard_map/ppermute | solution.py:378
  105.3 60.6 %collective-permute-start.16 = (bf16[768,1024]{1,0:T(8,128)(2,1)}, bf16[768,1024]{1,0:T(8,128)(2,1)}, u32[]{:S(2)}, u32[]{:S(2)}) collective-permute-start(bf16[768,1024]{1,0:T(8,128)(2,1)} %get-tuple-element.104), channel_id=1, source_target_pairs={{0,8},{8,0},{16,24},{24,16},{1,9},{9,1},{17,25},{25,17},{2,10},{10... | collective-permute-start | bytes 4718600 | tf_op jit(solution)/shard_map/ppermute | solution.py:378
  106.5 61.0 %collective-permute-start.17 = (bf16[768,1024]{1,0:T(8,128)(2,1)}, bf16[768,1024]{1,0:T(8,128)(2,1)}, u32[]{:S(2)}, u32[]{:S(2)}) collective-permute-start(bf16[768,1024]{1,0:T(8,128)(2,1)} %get-tuple-element.105), channel_id=1, source_target_pairs={{0,24},{8,16},{16,8},{24,0},{1,25},{9,17},{17,9},{25,1},{2,26},{10... | collective-permute-start | bytes 4718600 | tf_op jit(solution)/shard_map/ppermute | solution.py:378
  135.9 4.5 %collective-permute-start.12 = (f32[8]{0:T(128)S(1)}, f32[8]{0:T(128)S(1)}, u32[]{:S(2)}, u32[]{:S(2)}) collective-permute-start(f32[8]{0:T(128)S(1)} %sub.19), channel_id=1, source_target_pairs={{0,1},{1,0},{2,3},{3,2},{4,5},{5,4},{6,7},{7,6},{8,9},{9,8},{10,11... | collective-permute-start | bytes 104 | tf_op jit(solution)/shard_map/ppermute | solution.py:441
  137.5 11.6 %copy-start.30 = (s32[1,4]{1,0:T(1,128)S(1)}, s32[1,4]{1,0:T(1,128)}, u32[]{:S(2)}) copy-start(s32[1,4]{1,0:T(1,128)} %slice.7) | copy-start | bytes 52
  137.5 11.8 %copy-start.31 = (s32[1,4]{1,0:T(1,128)S(1)}, s32[1,4]{1,0:T(1,128)}, u32[]{:S(2)}) copy-start(s32[1,4]{1,0:T(1,128)} %slice.6) | copy-start | bytes 52
  137.5 12.9 %copy-start.27 = (s32[128]{0:T(128)S(1)}, s32[128]{0:T(128)}, u32[]{:S(2)}) copy-start(s32[128]{0:T(128)} %param.11) | copy-start | bytes 1540
  139.9 41.3 %collective-permute-start.24 = (bf16[256,1024]{1,0:T(8,128)(2,1)}, bf16[256,1024]{1,0:T(8,128)(2,1)S(1)}, u32[]{:S(2)}, u32[]{:S(2)}) collective-permute-start(bf16[256,1024]{1,0:T(8,128)(2,1)} %get-tuple-element.117), channel_id=1, source_target_pairs={{0,8},{8,0},{16,24},{24,16},{1,9},{9,1},{17,25},{25,17},{2,10},{10... | collective-permute-start | bytes 1572872 | tf_op jit(solution)/shard_map/ppermute | solution.py:378
  139.9 42.0 %collective-permute-start.25 = (bf16[256,1024]{1,0:T(8,128)(2,1)}, bf16[256,1024]{1,0:T(8,128)(2,1)S(1)}, u32[]{:S(2)}, u32[]{:S(2)}) collective-permute-start(bf16[256,1024]{1,0:T(8,128)(2,1)} %get-tuple-element.118), channel_id=1, source_target_pairs={{0,16},{8,24},{16,0},{24,8},{1,17},{9,25},{17,1},{25,9},{2,18},{10... | collective-permute-start | bytes 1572872 | tf_op jit(solution)/shard_map/ppermute | solution.py:378
  141.1 3.5 %collective-permute-start.13 = (f32[8]{0:T(128)S(1)}, f32[8]{0:T(128)S(1)}, u32[]{:S(2)}, u32[]{:S(2)}) collective-permute-start(f32[8]{0:T(128)S(1)} %add.41), channel_id=1, source_target_pairs={{0,2},{1,3},{2,0},{3,1},{4,6},{5,7},{6,4},{7,5},{8,10},{9,11},{10,... | collective-permute-start | bytes 104 | tf_op jit(solution)/shard_map/ppermute | solution.py:441
  144.6 4.4 %collective-permute-start.14 = (f32[8]{0:T(128)S(1)}, f32[8]{0:T(128)S(1)}, u32[]{:S(2)}, u32[]{:S(2)}) collective-permute-start(f32[8]{0:T(128)S(1)} %add.42), channel_id=1, source_target_pairs={{0,4},{1,5},{2,6},{3,7},{4,0},{5,1},{6,2},{7,3},{8,12},{9,13},{10,... | collective-permute-start | bytes 104 | tf_op jit(solution)/shard_map/ppermute | solution.py:441
  149.0 33.4 %collective-permute-start.26 = (bf16[256,1024]{1,0:T(8,128)(2,1)}, bf16[256,1024]{1,0:T(8,128)(2,1)S(1)}, u32[]{:S(2)}, u32[]{:S(2)}) collective-permute-start(bf16[256,1024]{1,0:T(8,128)(2,1)} %get-tuple-element.119), channel_id=1, source_target_pairs={{0,24},{8,16},{16,8},{24,0},{1,25},{9,17},{17,9},{25,1},{2,26},{10... | collective-permute-start | bytes 1572872 | tf_op jit(solution)/shard_map/ppermute | solution.py:378
  165.9 14.3 %collective-permute-start.21 = (bf16[128,1024]{1,0:T(8,128)(2,1)}, bf16[128,1024]{1,0:T(8,128)(2,1)S(1)}, u32[]{:S(2)}, u32[]{:S(2)}) collective-permute-start(bf16[128,1024]{1,0:T(8,128)(2,1)} %get-tuple-element.114), channel_id=1, source_target_pairs={{0,8},{8,0},{16,24},{24,16},{1,9},{9,1},{17,25},{25,17},{2,10},{10... | collective-permute-start | bytes 786440 | tf_op jit(solution)/shard_map/ppermute | solution.py:378
  167.5 20.9 %collective-permute-start.22 = (bf16[128,1024]{1,0:T(8,128)(2,1)}, bf16[128,1024]{1,0:T(8,128)(2,1)S(1)}, u32[]{:S(2)}, u32[]{:S(2)}) collective-permute-start(bf16[128,1024]{1,0:T(8,128)(2,1)} %get-tuple-element.115), channel_id=1, source_target_pairs={{0,16},{8,24},{16,0},{24,8},{1,17},{9,25},{17,1},{25,9},{2,18},{10... | collective-permute-start | bytes 786440 | tf_op jit(solution)/shard_map/ppermute | solution.py:378
  180.2 8.7 %collective-permute-start.23 = (bf16[128,1024]{1,0:T(8,128)(2,1)S(1)}, bf16[128,1024]{1,0:T(8,128)(2,1)S(1)}, u32[]{:S(2)}, u32[]{:S(2)}) collective-permute-start(bf16[128,1024]{1,0:T(8,128)(2,1)S(1)} %copy-done.28), channel_id=1, source_target_pairs={{0,24},{8,16},{16,8},{24,0},{1,25},{9,17},{17,9},{25,1},{2,26},{10... | collective-permute-start | bytes 786440 | tf_op jit(solution)/shard_map/ppermute | solution.py:378
  181.2 11.7 %collective-permute-start.18 = (bf16[128,1024]{1,0:T(8,128)(2,1)}, bf16[128,1024]{1,0:T(8,128)(2,1)S(1)}, u32[]{:S(2)}, u32[]{:S(2)}) collective-permute-start(bf16[128,1024]{1,0:T(8,128)(2,1)} %get-tuple-element.111), channel_id=1, source_target_pairs={{0,8},{8,0},{16,24},{24,16},{1,9},{9,1},{17,25},{25,17},{2,10},{10... | collective-permute-start | bytes 786440 | tf_op jit(solution)/shard_map/ppermute | solution.py:378
  181.9 12.6 %collective-permute-start.19 = (bf16[128,1024]{1,0:T(8,128)(2,1)}, bf16[128,1024]{1,0:T(8,128)(2,1)S(1)}, u32[]{:S(2)}, u32[]{:S(2)}) collective-permute-start(bf16[128,1024]{1,0:T(8,128)(2,1)} %get-tuple-element.112), channel_id=1, source_target_pairs={{0,16},{8,24},{16,0},{24,8},{1,17},{9,25},{17,1},{25,9},{2,18},{10... | collective-permute-start | bytes 786440 | tf_op jit(solution)/shard_map/ppermute | solution.py:378
  182.4 17.7 %collective-permute-start.20 = (bf16[128,1024]{1,0:T(8,128)(2,1)}, bf16[128,1024]{1,0:T(8,128)(2,1)S(1)}, u32[]{:S(2)}, u32[]{:S(2)}) collective-permute-start(bf16[128,1024]{1,0:T(8,128)(2,1)} %get-tuple-element.113), channel_id=1, source_target_pairs={{0,24},{8,16},{16,8},{24,0},{1,25},{9,17},{17,9},{25,1},{2,26},{10... | collective-permute-start | bytes 786440 | tf_op jit(solution)/shard_map/ppermute | solution.py:378
  (28 other events, 85.9 us)
Sparse Core Ops, SparseCore 0:
  27.8 50.7 all-gather.2

commit v8 on v6

--- a/solution.py
+++ b/solution.py
@@ -80,6 +80,22 @@
         name="pick",
     )(me, *[weight] * count, *after)
     return parts, token
+
+
+def settle_kernel(*refs):
+    mark(refs[-1])
+
+
+def settle(*after):
+    return pl.pallas_call(
+        settle_kernel,
+        in_specs=[STAY] * len(after),
+        out_specs=pl.BlockSpec(memory_space=pltpu.VMEM),
+        out_shape=TOKEN,
+        compiler_params=pltpu.CompilerParams(vmem_limit_bytes=VMEM_LIMIT),
+        cost_estimate=pl.CostEstimate(flops=1, bytes_accessed=44_000_000, transcendentals=0),
+        name="settle",
+    )(*after)
 
 
 def assemble_kernel(groups, me_ref, tokens_ref, *refs):
@@ -407,7 +423,7 @@
     gathered = lax.all_gather(assembled, "fsdp", axis=0, tiled=False)
     (near, _), token = send(0, 6, (1, 3), token)
 
-    *parts, token = partial_products(gathered, outer_gate, outer_up, token, near, *early)
+    *parts, token = partial_products(gathered, outer_gate, outer_up, settle(token, near, *early))
     for at in (1, 3, 5, 7):
         parts[at] = swap(parts[at], 1)
     stay_gate, near_gate, far_gate, both_gate, stay_up, near_up, far_up, both_up = parts

time: 213 us -> 213 us (level)
    unnamed x60 -> x62, local copies, waits for them, and re-layouts: 4.37 us -> 4.35 us
where the time goes in v8:
time: 213 us; the launch traced here: 212 us
  Pallas kernels  88.2 us (41%)
  waiting for transfers between devices  75.5 us (35%)
  starting transfers between devices  21 us (10%)
  between operations  16.1 us (8%)
  local copies, waits for them, and re-layouts  6.6 us (3%)
  other arithmetic  3.19 us (1%)
    ppermute x23, waiting for transfers between devices, swap(): return lax.ppermute(value, 'rep', [(i, i ^ bits) for i in range(groups)])  71.6 us
    pallas_call x5, Pallas kernels, outer_update(): pl.pallas_call(functools.partial(outer_kernel, groups, strip), grid_spec=...  28.3 us
    pallas_call x7, Pallas kernels, pick(): pl.pallas_call(functools.partial(pick_kernel, count), grid_spec=pltpu.Pre...  16.6 us
    pallas_call x1, Pallas kernels, policy_products(): pl.pallas_call(policy_kernel, grid=(unit_rows // tile,), in_specs=[pl.Blo...  15.8 us
    ppermute x23, starting transfers between devices, swap(): return lax.ppermute(value, 'rep', [(i, i ^ bits) for i in range(groups)])  15.2 us
    pallas_call x1, Pallas kernels, weight_grads(): pl.pallas_call(grads_kernel, grid=(unit_rows // tile,), in_specs=[units,...  12.7 us
    pallas_call x1, Pallas kernels, partial_products(): pl.pallas_call(partial_kernel, grid=(unit_rows // tile,), in_specs=[pl.Bl...  9.93 us
    ppermute x3, starting transfers between devices, per_device(): lax.ppermute(relative, 'fsdp', [(i, i ^ hop) for i in range(ranks)])  5.75 us
  transfers between devices with their start and end apart: 27, of which 14 were waited for; matrix products, arithmetic and copies ran while one was open for 3% of the time, Pallas kernels for 37%

profile of v8, /device:TPU:0, one launch (start us, length us, event | category | flops | bytes accessed | tf_op | source)
XLA Modules:
  0.0 211.7 jit_solution(8879019549106699409)
XLA Ops:
  7.2 2.9 %pick.7 = (bf16[1280,1024]{1,0:T(8,128)(2,1)}, f32[8,128]{1,0:T(8,128)}) custom-call(s32[1]{0:T(128)} %bitcast.1.me_ref, bf16[1,1792,4096]{2,1,0:T(8,128)(2,1)} %refs_0_.21), custom_call_target="tpu_custom_call" | custom-call | flops 1 | bytes 1 | tf_op jit(solution)/shard_map/pick/pallas_call | solution.py:63
  10.1 1.4 pick.8
  12.0 2.5 %collective-permute-start.1 = (bf16[16,1024]{1,0:T(8,128)(2,1)}, bf16[16,1024]{1,0:T(8,128)(2,1)S(1)}, u32[]{:S(2)}, u32[]{:S(2)}) collective-permute-start(bf16[16,1024]{1,0:T(8,128)(2,1)} %get-tuple-element.65), channel_id=1, source_target_pairs={{0,16},{8,24},{16,0},{24,8},{1,17},{9,25},{17,1},{25,9},{2,18},{10... | collective-permute-start | bytes 98312 | tf_op jit(solution)/shard_map/ppermute | solution.py:394
  14.7 2.1 %collective-permute-done.1.refs_1_ = bf16[16,1024]{1,0:T(8,128)(2,1)S(1)} collective-permute-done((bf16[16,1024]{1,0:T(8,128)(2,1)}, bf16[16,1024]{1,0:T(8,128)(2,1)S(1)}, u32[]{:S(2)}, u32[]{:S(2)}) %collective-permute-start.1) | collective-permute-done | bytes 32800 | tf_op jit(solution)/shard_map/ppermute | solution.py:394
  18.7 1.6 assemble.1
  21.2 3.1 %pick.9 = (bf16[768,1024]{1,0:T(8,128)(2,1)}, bf16[768,1024]{1,0:T(8,128)(2,1)}, f32[8,128]{1,0:T(8,128)}) custom-call(s32[1]{0:T(128)} %bitcast.1.me_ref, bf16[1,1792,4096]{2,1,0:T(8,128)(2,1)} %refs_0_.21, bf16[1,1792,4096]{2,1,0:T(8,128)(2,1)} %refs_0_.21, f32[8,128]{1,0:T(8,128)} %get-tuple-element.69.refs_2_), custom_call_target="tpu_custom_call" | custom-call | flops 1 | bytes 1 | tf_op jit(solution)/shard_map/pick/pallas_call | solution.py:63
  24.4 1.3 collective-permute-start.14
  25.7 2.3 %collective-permute-done.3.refs_1_.refs_2_ = bf16[768,1024]{1,0:T(8,128)(2,1)S(1)} collective-permute-done((bf16[768,1024]{1,0:T(8,128)(2,1)}, bf16[768,1024]{1,0:T(8,128)(2,1)S(1)}, u32[]{:S(2)}, u32[]{:S(2)}) %collective-permute-start.3) | collective-permute-done | bytes 1572896 | tf_op jit(solution)/shard_map/ppermute | solution.py:394
  28.0 52.3 %collective-permute-done.4.refs_2_.refs_1_ = bf16[1280,1024]{1,0:T(8,128)(2,1)S(1)} collective-permute-done((bf16[1280,1024]{1,0:T(8,128)(2,1)}, bf16[1280,1024]{1,0:T(8,128)(2,1)S(1)}, u32[]{:S(2)}, u32[]{:S(2)}) %collective-permute-start.4) | collective-permute-done | bytes 2621472 | tf_op jit(solution)/shard_map/ppermute | solution.py:394
  80.3 1.5 copy-done
  82.4 9.9 %partial_products.1 = (f32[128,1792]{1,0:T(8,128)}, bf16[128,1792]{1,0:T(8,128)(2,1)}, f32[128,1792]{1,0:T(8,128)}, bf16[128,1792]{1,0:T(8,128)(2,1)}, f32[128,1...) custom-call(bf16[8,8,16,1024]{3,2,1,0:T(8,128)(2,1)} %bitcast.29, ...), custom_call_target="tpu_custom_call" | custom-call | flops 1 | bytes 1 | tf_op jit(solution)/shard_map/partial_products/pallas_call | solution.py:158
  97.2 2.6 %join.1 = (bf16[128,1792]{1,0:T(8,128)(2,1)}, bf16[128,1792]{1,0:T(8,128)(2,1)}, f32[8,128]{1,0:T(8,128)}) custom-call(f32[128,1792]{1,0:T(8,128)} %get-tuple-element.73.far_gate_ref, bf16[128,1792]{1,0:T(8,128)(2,1)} %copy-done.13, f32[128,1792]{1,0:T(8,128)} %get-tuple-element.75.far_up_ref, bf16[128,1792]{1,0:T(8,128)(2,1)} %copy-done.14, ...), custom_call_target="tpu_custom_call" | custom-call | flops 1 | bytes 1 | tf_op jit(solution)/shard_map/join/pallas_call | solution.py:203
  103.0 2.6 %pick.10 = (bf16[512,1024]{1,0:T(8,128)(2,1)}, bf16[512,1024]{1,0:T(8,128)(2,1)}, f32[8,128]{1,0:T(8,128)}) custom-call(s32[1]{0:T(128)} %bitcast.1.me_ref, bf16[1,1792,4096]{2,1,0:T(8,128)(2,1)} %refs_0_.21, bf16[1,1792,4096]{2,1,0:T(8,128)(2,1)} %refs_0_.21, f32[8,128]{1,0:T(8,128)} %get-tuple-element.79.refs_2_), custom_call_target="tpu_custom_call" | custom-call | flops 1 | bytes 1 | tf_op jit(solution)/shard_map/pick/pallas_call | solution.py:63
  106.6 15.8 %policy_products.1 = (f32[128,1792]{1,0:T(8,128)}, f32[128,1792]{1,0:T(8,128)}, bf16[128,4096]{1,0:T(8,128)(2,1)}, f32[8,128]{1,0:T(8,128)}) custom-call(bf16[8,8,16,1024]{3,2,1,0:T(8,128)(2,1)} %bitcast.30, bf16[1,1792,4096]{2,1,0:T(8,128)(2,1)} %refs_0_.21, bf16[1,1792,4096]{2,1,0:T(8,128)(2,1)} %w_up_ref.1, f32[8,128]{1,0:T(8,128)} %get-tuple-element.80.refs_0_), custom_call_target="tpu_custom_call" | custom-call | flops 1 | bytes 1 | tf_op jit(solution)/shard_map/policy_products/pallas_call | solution.py:242
  122.4 10.2 %outer_update.5 = (bf16[1792,1024]{1,0:T(8,128)(2,1)}, f32[1792,1024]{1,0:T(8,128)}, f32[8,128]{1,0:T(8,128)}) custom-call(s32[1]{0:T(128)} %bitcast.1.me_ref, bf16[1792,1024]{1,0:T(8,128)(2,1)} %outer_ref.9, f32[1792,1024]{1,0:T(8,128)} %moment_ref.9, bf16[1,1792,4096]{2,1,0:T(8,128)(2,1)} %refs_0_.21, bf16[1280,1024]{1,0:T(8,128)(2,1)} %copy-done, ...), custom_call_target="tpu_custom_call" | custom-call | flops 1 | bytes 1 | tf_op jit(solution)/shard_map/outer_update/pallas_call | solution.py:366
  133.8 2.3 %fusion.3 = (f32[128]{0:T(128)S(1)}, f32[128]{0:T(128)S(1)}) fusion(bf16[128,1792]{1,0:T(8,128)(2,1)S(1)} %copy-done.8, bf16[128,1792]{1,0:T(8,128)(2,1)} %collective-permute-done.10, f32[128,1792]{1,0:T(8,128)} %get-tuple-element.85, bf16[128,1792]{1,0:T(8,128)(2,1)S(1)} %copy-done.7, bf16[128,1792]{1,0:T(8,128)(2,1)} %collective-permute-done.9, ...), kind=kLoop, calls=%fused_computation.8 | loop fusion | flops 6192896 | bytes 5964800 | tf_op jit(solution)/shard_map/reduce_sum | solution.py:29
  136.5 1.6 collective-permute-start.11
  138.1 2.4 %pick.11 = (bf16[256,1024]{1,0:T(8,128)(2,1)}, bf16[256,1024]{1,0:T(8,128)(2,1)}, bf16[256,1024]{1,0:T(8,128)(2,1)}, f32[8,128]{1,0:T(8,128)}) custom-call(s32[1]{0:T(128)} %bitcast.1.me_ref, bf16[1,1792,4096]{2,1,0:T(8,128)(2,1)} %refs_0_.21, bf16[1,1792,4096]{2,1,0:T(8,128)(2,1)} %refs_0_.21, bf16[1,1792,4096]{2,1,0:T(8,128)(2,1)} %refs_0_.21, ...), custom_call_target="tpu_custom_call" | custom-call | flops 1 | bytes 1 | tf_op jit(solution)/shard_map/pick/pallas_call | solution.py:63
  142.1 1.6 collective-permute-start.12
  143.7 2.0 collective-permute-done.12
  145.7 2.6 %collective-permute-start.13 = (f32[8]{0:T(128)S(1)}, f32[8]{0:T(128)S(1)}, u32[]{:S(2)}, u32[]{:S(2)}) collective-permute-start(f32[8]{0:T(128)S(1)} %add.42), channel_id=1, source_target_pairs={{0,4},{1,5},{2,6},{3,7},{4,0},{5,1},{6,2},{7,3},{8,12},{9,13},{10,... | collective-permute-start | bytes 104 | tf_op jit(solution)/shard_map/ppermute | solution.py:455
  148.3 1.9 collective-permute-done.13
  152.2 12.7 %weight_grads.1 = (bf16[1,1792,4096]{2,1,0:T(8,128)(2,1)}, bf16[1,1792,4096]{2,1,0:T(8,128)(2,1)}, f32[8,128]{1,0:T(8,128)}) custom-call(f32[128,1792]{1,0:T(8,128)} %get-tuple-element.81.gate_ref, f32[128,1792]{1,0:T(8,128)} %get-tuple-element.82.up_ref, bf16[128,1792]{1,0:T(8,128)(2,1)} %readout_ref.1, f32[128,1]{1,0:T(8,128)} %copy.23.token_grad_ref, ...), custom_call_target="tpu_custom_call" | custom-call | flops 1 | bytes 1 | tf_op jit(solution)/shard_map/weight_grads/pallas_call | solution.py:294
  164.9 2.0 pick.12
  169.1 7.2 %outer_update.6 = (bf16[1792,1024]{1,0:T(8,128)(2,1)}, f32[1792,1024]{1,0:T(8,128)}, f32[8,128]{1,0:T(8,128)}) custom-call(s32[1]{0:T(128)} %bitcast.1.me_ref, bf16[1792,1024]{1,0:T(8,128)(2,1)} %outer_ref.9, f32[1792,1024]{1,0:T(8,128)} %moment_ref.9, bf16[1,1792,4096]{2,1,0:T(8,128)(2,1)} %refs_0_.21, ...), custom_call_target="tpu_custom_call", output_to_operand_aliasing={{0}: (7, {}), {1}: (8, {})} | custom-call | flops 1 | bytes 1 | tf_op jit(solution)/shard_map/outer_update/pallas_call | solution.py:366
  176.3 2.1 pick.13
  181.8 4.4 %outer_update.7 = (bf16[1792,1024]{1,0:T(8,128)(2,1)}, f32[1792,1024]{1,0:T(8,128)}, f32[8,128]{1,0:T(8,128)}) custom-call(s32[1]{0:T(128)} %bitcast.1.me_ref, bf16[1792,1024]{1,0:T(8,128)(2,1)} %outer_ref.9, f32[1792,1024]{1,0:T(8,128)} %moment_ref.9, bf16[1,1792,4096]{2,1,0:T(8,128)(2,1)} %refs_0_.21, ...), custom_call_target="tpu_custom_call", output_to_operand_aliasing={{0}: (7, {}), {1}: (8, {})} | custom-call | flops 1 | bytes 1 | tf_op jit(solution)/shard_map/outer_update/pallas_call | solution.py:366
  186.2 2.3 %collective-permute-done.22.refs_3_ = bf16[128,1024]{1,0:T(8,128)(2,1)S(1)} collective-permute-done((bf16[128,1024]{1,0:T(8,128)(2,1)S(1)}, bf16[128,1024]{1,0:T(8,128)(2,1)S(1)}, u32[]{:S(2)}, u32[]{:S(2)}) %collective-permute-start.22) | collective-permute-done | bytes 262176 | tf_op jit(solution)/shard_map/ppermute | solution.py:394
  189.2 3.3 %outer_update.8 = (bf16[1792,1024]{1,0:T(8,128)(2,1)}, f32[1792,1024]{1,0:T(8,128)}, f32[8,128]{1,0:T(8,128)}) custom-call(s32[1]{0:T(128)} %bitcast.1.me_ref, bf16[1792,1024]{1,0:T(8,128)(2,1)} %outer_ref.9, f32[1792,1024]{1,0:T(8,128)} %moment_ref.9, bf16[1,1792,4096]{2,1,0:T(8,128)(2,1)} %refs_0_.21, ...), custom_call_target="tpu_custom_call", output_to_operand_aliasing={{0}: (7, {}), {1}: (8, {})} | custom-call | flops 1 | bytes 1 | tf_op jit(solution)/shard_map/outer_update/pallas_call | solution.py:366
  192.5 3.0 %collective-permute-done.18.refs_2_ = bf16[128,1024]{1,0:T(8,128)(2,1)S(1)} collective-permute-done((bf16[128,1024]{1,0:T(8,128)(2,1)}, bf16[128,1024]{1,0:T(8,128)(2,1)S(1)}, u32[]{:S(2)}, u32[]{:S(2)}) %collective-permute-start.18) | collective-permute-done | bytes 262176 | tf_op jit(solution)/shard_map/ppermute | solution.py:394
  195.5 4.2 %collective-permute-done.19.refs_3_ = bf16[128,1024]{1,0:T(8,128)(2,1)S(1)} collective-permute-done((bf16[128,1024]{1,0:T(8,128)(2,1)}, bf16[128,1024]{1,0:T(8,128)(2,1)S(1)}, u32[]{:S(2)}, u32[]{:S(2)}) %collective-permute-start.19) | collective-permute-done | bytes 262176 | tf_op jit(solution)/shard_map/ppermute | solution.py:394
  200.4 3.3 %outer_update.9 = (bf16[1792,1024]{1,0:T(8,128)(2,1)}, f32[1792,1024]{1,0:T(8,128)}, f32[8,128]{1,0:T(8,128)}) custom-call(s32[1]{0:T(128)} %bitcast.1.me_ref, bf16[1792,1024]{1,0:T(8,128)(2,1)} %outer_ref.9, f32[1792,1024]{1,0:T(8,128)} %moment_ref.9, bf16[1,1792,4096]{2,1,0:T(8,128)(2,1)} %refs_0_.21, ...), custom_call_target="tpu_custom_call", output_to_operand_aliasing={{0}: (7, {}), {1}: (8, {})} | custom-call | flops 1 | bytes 1 | tf_op jit(solution)/shard_map/outer_update/pallas_call | solution.py:366
  (121 shorter events, 24.7 us)
Async XLA Ops:
  7.2 75.2 %all-gather.3.cloned.1.call-start = ((), (), s32[]{:S(2)}) async-start(), calls=%async_computation | async-start | bytes 2359296 | tf_op jit(solution)/shard_map/all_gather | solution.py:423
  11.6 3.1 %collective-permute-start = (bf16[16,1024]{1,0:T(8,128)(2,1)}, bf16[16,1024]{1,0:T(8,128)(2,1)S(1)}, u32[]{:S(2)}, u32[]{:S(2)}) collective-permute-start(bf16[16,1024]{1,0:T(8,128)(2,1)} %get-tuple-element.64), channel_id=1, source_target_pairs={{0,8},{8,0},{16,24},{24,16},{1,9},{9,1},{17,25},{25,17},{2,10},{10... | collective-permute-start | bytes 98312 | tf_op jit(solution)/shard_map/ppermute | solution.py:394
  12.0 4.8 %collective-permute-start.1 = (bf16[16,1024]{1,0:T(8,128)(2,1)}, bf16[16,1024]{1,0:T(8,128)(2,1)S(1)}, u32[]{:S(2)}, u32[]{:S(2)}) collective-permute-start(bf16[16,1024]{1,0:T(8,128)(2,1)} %get-tuple-element.65), channel_id=1, source_target_pairs={{0,16},{8,24},{16,0},{24,8},{1,17},{9,25},{17,1},{25,9},{2,18},{10... | collective-permute-start | bytes 98312 | tf_op jit(solution)/shard_map/ppermute | solution.py:394
  14.5 3.6 %collective-permute-start.2 = (bf16[16,1024]{1,0:T(8,128)(2,1)}, bf16[16,1024]{1,0:T(8,128)(2,1)S(1)}, u32[]{:S(2)}, u32[]{:S(2)}) collective-permute-start(bf16[16,1024]{1,0:T(8,128)(2,1)} %get-tuple-element.66), channel_id=1, source_target_pairs={{0,24},{8,16},{16,8},{24,0},{1,25},{9,17},{17,9},{25,1},{2,26},{10... | collective-permute-start | bytes 98312 | tf_op jit(solution)/shard_map/ppermute | solution.py:394
  20.3 60.0 %collective-permute-start.4 = (bf16[1280,1024]{1,0:T(8,128)(2,1)}, bf16[1280,1024]{1,0:T(8,128)(2,1)S(1)}, u32[]{:S(2)}, u32[]{:S(2)}) collective-permute-start(bf16[1280,1024]{1,0:T(8,128)(2,1)} %get-tuple-element.72), channel_id=1, source_target_pairs={{0,16},{8,24},{16,0},{24,8},{1,17},{9,25},{17,1},{25,9},{2,18},{10... | collective-permute-start | bytes 7864328 | tf_op jit(solution)/shard_map/ppermute | solution.py:394
  24.4 3.6 %collective-permute-start.3 = (bf16[768,1024]{1,0:T(8,128)(2,1)}, bf16[768,1024]{1,0:T(8,128)(2,1)S(1)}, u32[]{:S(2)}, u32[]{:S(2)}) collective-permute-start(bf16[768,1024]{1,0:T(8,128)(2,1)} %get-tuple-element.71), channel_id=1, source_target_pairs={{0,8},{8,0},{16,24},{24,16},{1,9},{9,1},{17,25},{25,17},{2,10},{10... | collective-permute-start | bytes 4718600 | tf_op jit(solution)/shard_map/ppermute | solution.py:394
  24.4 98.0 %collective-permute-start.14 = (bf16[768,1024]{1,0:T(8,128)(2,1)}, bf16[768,1024]{1,0:T(8,128)(2,1)}, u32[]{:S(2)}, u32[]{:S(2)}) collective-permute-start(bf16[768,1024]{1,0:T(8,128)(2,1)} %get-tuple-element.88), channel_id=1, source_target_pairs={{0,24},{8,16},{16,8},{24,0},{1,25},{9,17},{17,9},{25,1},{2,26},{10... | collective-permute-start | bytes 4718600 | tf_op jit(solution)/shard_map/ppermute | solution.py:394
  28.0 52.3 %copy-start.1 = (bf16[768,1024]{1,0:T(8,128)(2,1)}, bf16[768,1024]{1,0:T(8,128)(2,1)S(1)}, u32[]{:S(2)}) copy-start(bf16[768,1024]{1,0:T(8,128)(2,1)S(1)} %collective-permute-done.3.refs_1_.refs_2_) | copy-start | bytes 4718596
  92.3 2.1 collective-permute-start.5
  92.4 2.7 %collective-permute-start.6 = (bf16[128,1792]{1,0:T(8,128)(2,1)}, bf16[128,1792]{1,0:T(8,128)(2,1)S(1)}, u32[]{:S(2)}, u32[]{:S(2)}) collective-permute-start(bf16[128,1792]{1,0:T(8,128)(2,1)} %get-tuple-element.76), channel_id=1, source_target_pairs={{0,8},{8,0},{16,24},{24,16},{1,9},{9,1},{17,25},{25,17},{2,10},{10... | collective-permute-start | bytes 1376264 | tf_op jit(solution)/shard_map/ppermute | solution.py:394
  92.9 2.8 %collective-permute-start.7 = (bf16[128,1792]{1,0:T(8,128)(2,1)}, bf16[128,1792]{1,0:T(8,128)(2,1)S(1)}, u32[]{:S(2)}, u32[]{:S(2)}) collective-permute-start(bf16[128,1792]{1,0:T(8,128)(2,1)} %get-tuple-element.77), channel_id=1, source_target_pairs={{0,8},{8,0},{16,24},{24,16},{1,9},{9,1},{17,25},{25,17},{2,10},{10... | collective-permute-start | bytes 1376264 | tf_op jit(solution)/shard_map/ppermute | solution.py:394
  93.0 3.4 %collective-permute-start.8 = (bf16[128,1792]{1,0:T(8,128)(2,1)}, bf16[128,1792]{1,0:T(8,128)(2,1)S(1)}, u32[]{:S(2)}, u32[]{:S(2)}) collective-permute-start(bf16[128,1792]{1,0:T(8,128)(2,1)} %get-tuple-element.78), channel_id=1, source_target_pairs={{0,8},{8,0},{16,24},{24,16},{1,9},{9,1},{17,25},{25,17},{2,10},{10... | collective-permute-start | bytes 1376264 | tf_op jit(solution)/shard_map/ppermute | solution.py:394
  99.8 32.8 %collective-permute-start.9 = (bf16[128,1792]{1,0:T(8,128)(2,1)}, bf16[128,1792]{1,0:T(8,128)(2,1)}, u32[]{:S(2)}, u32[]{:S(2)}) collective-permute-start(bf16[128,1792]{1,0:T(8,128)(2,1)} %get-tuple-element.84), channel_id=1, source_target_pairs={{0,16},{8,24},{16,0},{24,8},{1,17},{9,25},{17,1},{25,9},{2,18},{10... | collective-permute-start | bytes 1376264 | tf_op jit(solution)/shard_map/ppermute | solution.py:394
  100.6 33.1 %collective-permute-start.10 = (bf16[128,1792]{1,0:T(8,128)(2,1)}, bf16[128,1792]{1,0:T(8,128)(2,1)}, u32[]{:S(2)}, u32[]{:S(2)}) collective-permute-start(bf16[128,1792]{1,0:T(8,128)(2,1)} %get-tuple-element.86), channel_id=1, source_target_pairs={{0,16},{8,24},{16,0},{24,8},{1,17},{9,25},{17,1},{25,9},{2,18},{10... | collective-permute-start | bytes 1376264 | tf_op jit(solution)/shard_map/ppermute | solution.py:394
  105.6 61.4 %collective-permute-start.15 = (bf16[512,1024]{1,0:T(8,128)(2,1)}, bf16[512,1024]{1,0:T(8,128)(2,1)}, u32[]{:S(2)}, u32[]{:S(2)}) collective-permute-start(bf16[512,1024]{1,0:T(8,128)(2,1)} %get-tuple-element.94), channel_id=1, source_target_pairs={{0,8},{8,0},{16,24},{24,16},{1,9},{9,1},{17,25},{25,17},{2,10},{10... | collective-permute-start | bytes 3145736 | tf_op jit(solution)/shard_map/ppermute | solution.py:394
  105.6 62.6 %collective-permute-start.16 = (bf16[512,1024]{1,0:T(8,128)(2,1)}, bf16[512,1024]{1,0:T(8,128)(2,1)}, u32[]{:S(2)}, u32[]{:S(2)}) collective-permute-start(bf16[512,1024]{1,0:T(8,128)(2,1)} %get-tuple-element.95), channel_id=1, source_target_pairs={{0,24},{8,16},{16,8},{24,0},{1,25},{9,17},{17,9},{25,1},{2,26},{10... | collective-permute-start | bytes 3145736 | tf_op jit(solution)/shard_map/ppermute | solution.py:394
  122.4 11.4 %copy-start.2 = (f32[128,1792]{1,0:T(8,128)S(1)}, f32[128,1792]{1,0:T(8,128)}, u32[]{:S(2)}) copy-start(f32[128,1792]{1,0:T(8,128)} %get-tuple-element.81.gate_ref) | copy-start | bytes 2752516
  136.5 5.0 %collective-permute-start.11 = (f32[8]{0:T(128)S(1)}, f32[8]{0:T(128)S(1)}, u32[]{:S(2)}, u32[]{:S(2)}) collective-permute-start(f32[8]{0:T(128)S(1)} %sub.19), channel_id=1, source_target_pairs={{0,1},{1,0},{2,3},{3,2},{4,5},{5,4},{6,7},{7,6},{8,9},{9,8},{10,11... | collective-permute-start | bytes 104 | tf_op jit(solution)/shard_map/ppermute | solution.py:455
  138.1 12.0 %copy-start.29 = (s32[1,4]{1,0:T(1,128)S(1)}, s32[1,4]{1,0:T(1,128)}, u32[]{:S(2)}) copy-start(s32[1,4]{1,0:T(1,128)} %slice.7) | copy-start | bytes 52
  138.1 12.2 %copy-start.30 = (s32[1,4]{1,0:T(1,128)S(1)}, s32[1,4]{1,0:T(1,128)}, u32[]{:S(2)}) copy-start(s32[1,4]{1,0:T(1,128)} %slice.6) | copy-start | bytes 52
  138.1 13.4 %copy-start.26 = (s32[128]{0:T(128)S(1)}, s32[128]{0:T(128)}, u32[]{:S(2)}) copy-start(s32[128]{0:T(128)} %param.11) | copy-start | bytes 1540
  140.5 38.5 %collective-permute-start.23 = (bf16[256,1024]{1,0:T(8,128)(2,1)}, bf16[256,1024]{1,0:T(8,128)(2,1)S(1)}, u32[]{:S(2)}, u32[]{:S(2)}) collective-permute-start(bf16[256,1024]{1,0:T(8,128)(2,1)} %get-tuple-element.107), channel_id=1, source_target_pairs={{0,8},{8,0},{16,24},{24,16},{1,9},{9,1},{17,25},{25,17},{2,10},{10... | collective-permute-start | bytes 1572872 | tf_op jit(solution)/shard_map/ppermute | solution.py:394
  140.5 39.2 %collective-permute-start.24 = (bf16[256,1024]{1,0:T(8,128)(2,1)}, bf16[256,1024]{1,0:T(8,128)(2,1)S(1)}, u32[]{:S(2)}, u32[]{:S(2)}) collective-permute-start(bf16[256,1024]{1,0:T(8,128)(2,1)} %get-tuple-element.108), channel_id=1, source_target_pairs={{0,16},{8,24},{16,0},{24,8},{1,17},{9,25},{17,1},{25,9},{2,18},{10... | collective-permute-start | bytes 1572872 | tf_op jit(solution)/shard_map/ppermute | solution.py:394
  142.1 3.5 %collective-permute-start.12 = (f32[8]{0:T(128)S(1)}, f32[8]{0:T(128)S(1)}, u32[]{:S(2)}, u32[]{:S(2)}) collective-permute-start(f32[8]{0:T(128)S(1)} %add.41), channel_id=1, source_target_pairs={{0,2},{1,3},{2,0},{3,1},{4,6},{5,7},{6,4},{7,5},{8,10},{9,11},{10,... | collective-permute-start | bytes 104 | tf_op jit(solution)/shard_map/ppermute | solution.py:455
  145.7 4.4 %collective-permute-start.13 = (f32[8]{0:T(128)S(1)}, f32[8]{0:T(128)S(1)}, u32[]{:S(2)}, u32[]{:S(2)}) collective-permute-start(f32[8]{0:T(128)S(1)} %add.42), channel_id=1, source_target_pairs={{0,4},{1,5},{2,6},{3,7},{4,0},{5,1},{6,2},{7,3},{8,12},{9,13},{10,... | collective-permute-start | bytes 104 | tf_op jit(solution)/shard_map/ppermute | solution.py:455
  150.1 30.5 %collective-permute-start.25 = (bf16[256,1024]{1,0:T(8,128)(2,1)}, bf16[256,1024]{1,0:T(8,128)(2,1)S(1)}, u32[]{:S(2)}, u32[]{:S(2)}) collective-permute-start(bf16[256,1024]{1,0:T(8,128)(2,1)} %get-tuple-element.109), channel_id=1, source_target_pairs={{0,24},{8,16},{16,8},{24,0},{1,25},{9,17},{17,9},{25,1},{2,26},{10... | collective-permute-start | bytes 1572872 | tf_op jit(solution)/shard_map/ppermute | solution.py:394
  167.0 11.4 %collective-permute-start.20 = (bf16[128,1024]{1,0:T(8,128)(2,1)}, bf16[128,1024]{1,0:T(8,128)(2,1)S(1)}, u32[]{:S(2)}, u32[]{:S(2)}) collective-permute-start(bf16[128,1024]{1,0:T(8,128)(2,1)} %get-tuple-element.104), channel_id=1, source_target_pairs={{0,8},{8,0},{16,24},{24,16},{1,9},{9,1},{17,25},{25,17},{2,10},{10... | collective-permute-start | bytes 786440 | tf_op jit(solution)/shard_map/ppermute | solution.py:394
  168.2 18.0 %collective-permute-start.21 = (bf16[128,1024]{1,0:T(8,128)(2,1)}, bf16[128,1024]{1,0:T(8,128)(2,1)S(1)}, u32[]{:S(2)}, u32[]{:S(2)}) collective-permute-start(bf16[128,1024]{1,0:T(8,128)(2,1)} %get-tuple-element.105), channel_id=1, source_target_pairs={{0,16},{8,24},{16,0},{24,8},{1,17},{9,25},{17,1},{25,9},{2,18},{10... | collective-permute-start | bytes 786440 | tf_op jit(solution)/shard_map/ppermute | solution.py:394
  178.4 10.1 %collective-permute-start.22 = (bf16[128,1024]{1,0:T(8,128)(2,1)S(1)}, bf16[128,1024]{1,0:T(8,128)(2,1)S(1)}, u32[]{:S(2)}, u32[]{:S(2)}) collective-permute-start(bf16[128,1024]{1,0:T(8,128)(2,1)S(1)} %copy-done.27), channel_id=1, source_target_pairs={{0,24},{8,16},{16,8},{24,0},{1,25},{9,17},{17,9},{25,1},{2,26},{10... | collective-permute-start | bytes 786440 | tf_op jit(solution)/shard_map/ppermute | solution.py:394
  179.0 13.5 %collective-permute-start.17 = (bf16[128,1024]{1,0:T(8,128)(2,1)}, bf16[128,1024]{1,0:T(8,128)(2,1)S(1)}, u32[]{:S(2)}, u32[]{:S(2)}) collective-permute-start(bf16[128,1024]{1,0:T(8,128)(2,1)} %get-tuple-element.101), channel_id=1, source_target_pairs={{0,8},{8,0},{16,24},{24,16},{1,9},{9,1},{17,25},{25,17},{2,10},{10... | collective-permute-start | bytes 786440 | tf_op jit(solution)/shard_map/ppermute | solution.py:394
  179.7 15.8 %collective-permute-start.18 = (bf16[128,1024]{1,0:T(8,128)(2,1)}, bf16[128,1024]{1,0:T(8,128)(2,1)S(1)}, u32[]{:S(2)}, u32[]{:S(2)}) collective-permute-start(bf16[128,1024]{1,0:T(8,128)(2,1)} %get-tuple-element.102), channel_id=1, source_target_pairs={{0,16},{8,24},{16,0},{24,8},{1,17},{9,25},{17,1},{25,9},{2,18},{10... | collective-permute-start | bytes 786440 | tf_op jit(solution)/shard_map/ppermute | solution.py:394
  180.6 19.1 %collective-permute-start.19 = (bf16[128,1024]{1,0:T(8,128)(2,1)}, bf16[128,1024]{1,0:T(8,128)(2,1)S(1)}, u32[]{:S(2)}, u32[]{:S(2)}) collective-permute-start(bf16[128,1024]{1,0:T(8,128)(2,1)} %get-tuple-element.103), channel_id=1, source_target_pairs={{0,24},{8,16},{16,8},{24,0},{1,25},{9,17},{17,9},{25,1},{2,26},{10... | collective-permute-start | bytes 786440 | tf_op jit(solution)/shard_map/ppermute | solution.py:394
  (26 other events, 114.4 us)
Sparse Core Ops, SparseCore 0:
  20.5 49.9 all-gather.2
